TPU v7x, 512 devices: a whole 4x8x8 slice. The times are simulated.
512 devices in a mesh: section: 16 (over y, x_lo), dp: 32 (over x_hi, z, core).
Axes of the slice: x: 4 (x_hi: 2, x_lo: 2; x = x_hi * 2 + x_lo), y: 8, z: 8, core: 2. Of those that a mesh axis runs over, the one named last changes fastest.
Arguments:
- inputs: bfloat16 [64, 512, 1024], P('dp', None, 'section'), may hold values from -6 to 6
- cotangent: bfloat16 [64, 512, 1024], P('dp', None, 'section'), may hold values from -6 to 6
- weights: bfloat16 [16, 1024, 1024], P('section'), may hold values from -0.09375 to 0.09375
- proj_in: bfloat16 [16, 1024, 64], P('section'), may hold values from -0.1875 to 0.1875
- proj_out: bfloat16 [16, 1024, 64], P('section'), may hold values from -0.1875 to 0.1875
- query_factors: bfloat16 [16, 512, 4096], P('section', 'dp'), may hold values from -0.0009765625 to 0.0009765625
Outputs:
- scores: float32 [64, 512], P('section', 'dp')
All inputs are finite; a program needn't handle non-finite values.
Results may differ from a plain program's by a relative error of at most 0.02.
Values may be sent and summed in bfloat16 or wider, within the bound.
No kernel may reach another device: no remote copies, remote signals or barrier semaphores. Data moves between devices by JAX's collectives and lax.ppermute only.
A program may use at most 64 MiB of HBM per device.

v0:
```python
import jax
import jax.numpy as jnp
from jax import lax
from jax.sharding import PartitionSpec as P

BLOCK = 128


def from_behind(value, axis, steps):
    count = lax.axis_size(axis)
    initial, last = (max(0, -steps), min(count, count - steps))
    return lax.ppermute(value, axis, [(source, source + steps) for source in range(initial, last)])


def forward_layer(hidden, weight):
    preact = jnp.dot(hidden, weight, preferred_element_type=jnp.float32)
    return (hidden.astype(jnp.float32) + jax.nn.silu(preact)).astype(jnp.bfloat16)


def backward_layer(hidden, upstream, weight, left_map, right_map):
    preact = jnp.dot(hidden, weight, preferred_element_type=jnp.float32)
    sigmoid_vals = jax.nn.sigmoid(preact)
    pre_grad = (
        upstream.astype(jnp.float32) * sigmoid_vals * (1.0 + preact * (1.0 - sigmoid_vals))
    ).astype(jnp.bfloat16)
    carried = lax.dot_general(
        pre_grad, weight, (((1,), (1,)), ((), ())), preferred_element_type=jnp.float32
    )
    downstream = (upstream.astype(jnp.float32) + carried).astype(jnp.bfloat16)
    left_proj = jnp.dot(hidden, left_map, preferred_element_type=jnp.float32)
    right_proj = jnp.dot(pre_grad, right_map, preferred_element_type=jnp.float32)
    factor = lax.dot_general(
        left_proj,
        right_proj,
        (((0,), (0,)), ((), ())),
        precision=lax.Precision.HIGHEST,
        preferred_element_type=jnp.float32,
    )
    return (downstream, factor.reshape(-1))


def on_device(inputs, cotangent, weights, proj_in, proj_out, query_factors):
    sections = lax.axis_size("section")
    position = lax.axis_index("section")
    width = weights.shape[1]
    weight = weights[0]
    left_map = proj_in[0]
    right_map = proj_out[0]
    features = lax.all_gather(inputs, "section", axis=2, tiled=True)
    seed_rows = lax.all_gather(cotangent, "section", axis=2, tiled=True)
    sequences = features.shape[0]
    per_sequence = features.shape[1] // BLOCK
    micro = sequences * per_sequence
    features = features.reshape(micro, BLOCK, width)
    seed_rows = seed_rows.reshape(micro, BLOCK, width)
    rank_square = left_map.shape[1] * right_map.shape[1]
    empty_block = jnp.zeros((BLOCK, width), jnp.bfloat16)
    stash_init = jnp.zeros((micro, BLOCK, width), jnp.bfloat16)
    factor_init = jnp.zeros((sequences, rank_square), jnp.float32)

    def run_forward(current):
        return forward_layer(current, weight)

    def skip_forward(current):
        return jnp.zeros_like(current)

    def store_block(stash, current, safe):
        return lax.dynamic_update_index_in_dim(stash, current, safe, 0)

    def keep_stash(stash, current, safe):
        return stash

    def forward_step(index, incoming, stash):
        active = jnp.logical_and(index >= 0, index < micro)
        safe = jnp.clip(index, 0, micro - 1)
        first_rows = lax.dynamic_index_in_dim(features, safe, 0, keepdims=False)
        current = jnp.where(position == 0, first_rows, incoming)
        output = lax.cond(active, run_forward, skip_forward, current)
        stash = lax.cond(active, store_block, keep_stash, stash, current, safe)
        return (output, stash)

    def run_backward(hidden, current, factors, safe):
        downstream, factor = backward_layer(hidden, current, weight, left_map, right_map)
        row_index = safe // per_sequence
        previous = lax.dynamic_index_in_dim(factors, row_index, 0, keepdims=False)
        return (
            downstream,
            lax.dynamic_update_index_in_dim(factors, previous + factor, row_index, 0),
        )

    def skip_backward(hidden, current, factors, safe):
        return (jnp.zeros_like(current), factors)

    def backward_step(index, incoming, stash, factors):
        active = jnp.logical_and(index >= 0, index < micro)
        safe = jnp.clip(index, 0, micro - 1)
        last_rows = lax.dynamic_index_in_dim(seed_rows, safe, 0, keepdims=False)
        current = jnp.where(position == sections - 1, last_rows, incoming)
        hidden = lax.dynamic_index_in_dim(stash, safe, 0, keepdims=False)
        return lax.cond(active, run_backward, skip_backward, hidden, current, factors, safe)

    def forward_loop(moment, carry):
        incoming, stash = carry
        output, stash = forward_step(moment - position, incoming, stash)
        return (from_behind(output, "section", 1), stash)

    arrived, stash_done = lax.fori_loop(
        0, micro + sections - 1, forward_loop, (empty_block, stash_init)
    )

    def backward_loop(moment, carry):
        incoming, factors = carry
        downstream, factors = backward_step(
            moment - (sections - 1 - position), incoming, stash_done, factors
        )
        return (from_behind(downstream, "section", -1), factors)

    returned, factors = lax.fori_loop(
        0, micro + sections - 1, backward_loop, (empty_block, factor_init)
    )
    local_queries = query_factors[0].astype(jnp.float32)
    table = lax.dot_general(
        lax.all_gather(factors, "dp", axis=0, tiled=True),
        local_queries,
        (((1,), (1,)), ((), ())),
        precision=lax.Precision.HIGHEST,
        preferred_element_type=jnp.float32,
    )
    return lax.psum_scatter(table, "section", scatter_dimension=0, tiled=True)


def solution(mesh):
    placed = (
        P("dp", None, "section"),
        P("dp", None, "section"),
        P("section", None, None),
        P("section", None, None),
        P("section", None, None),
        P("section", "dp", None),
    )
    return jax.shard_map(
        on_device, mesh=mesh, in_specs=placed, out_specs=P("section", "dp"), check_vma=False
    )
```

profile of v0, /device:TPU:1, one launch (start us, length us, event | category | flops | bytes accessed | tf_op | source)
XLA Modules:
  0.0 945.7 jit_solution(14958328270559257058)
XLA Ops:
  10.9 70.5 %all-gather.7.cloned.1.call-done = bf16[2,512,1024]{1,2,0:T(8,128)(2,1)} async-done(((bf16[2,512,64]{1,2,0:T(8,128)(2,1)}), bf16[2,512,1024]{1,2,0:T(8,128)(2,1)}) %all-gather.7.cloned.1.call-update) | async-done | bytes 2097168 | tf_op jit(solution)/shard_map/all_gather | solution.py:49
  85.4 72.8 %all-gather.5.cloned.1.call-done = bf16[2,512,1024]{1,2,0:T(8,128)(2,1)} async-done(((bf16[2,512,64]{1,2,0:T(8,128)(2,1)}), bf16[2,512,1024]{1,2,0:T(8,128)(2,1)}) %all-gather.5.cloned.1.call-update) | async-done | bytes 2097168 | tf_op jit(solution)/shard_map/all_gather | solution.py:50
  164.4 230.3 %while.39 = (s32[]{:T(128)}, bf16[128,1024]{1,0:T(8,128)(2,1)S(1)}, bf16[8,128,1024]{2,1,0:T(8,128)(2,1)}, s32[]{:T(128)}, pred[]{:T(512)}, /*index=5*/bf16[8,12...) while((s32[]{:T(128)}, bf16[128,1024]{1,0:T(8,128)(2,1)S(1)}, ...), condition=%wide.region_5.6_spmd, body=%wide.region_0.5_spmd.sunk | while | flops 269484032 | bytes 4981046 | solution.py:107
  329.7 9.2 collective-permute-start
  384.0 7.4 collective-permute-start
  395.4 360.3 %while.40 = (s32[]{:T(128)}, bf16[128,1024]{1,0:T(8,128)(2,1)}, f32[2,4096]{1,0:T(2,128)S(1)}, s32[]{:T(128)}, pred[]{:T(512)}, /*index=5*/bf16[8,128,1024]{2,1,...) while((s32[]{:T(128)}, bf16[128,1024]{1,0:T(8,128)(2,1)}, ...), condition=%wide.region_9.10_spmd, body=%wide.region_6.9_spmd.sunk | while | flops 580128768 | bytes 12323859 | solution.py:118
  396.8 8.7 collective-permute-done.1
  407.5 8.7 collective-permute-done.1
  418.3 9.3 collective-permute-done.1
  429.6 11.9 %collective-permute-done.1 = bf16[128,1024]{1,0:T(8,128)(2,1)S(1)} collective-permute-done((bf16[128,1024]{1,0:T(8,128)(2,1)S(1)}, bf16[128,1024]{1,0:T(8,128)(2,1)S(1)}, u32[]{:S(2)}, u32[]{:S(2)}) %collective-permute-start.1) | collective-permute-done | bytes 262176 | tf_op jit(solution)/shard_map/while/body/eval_jaxpr/ppermute | solution.py:12
  443.6 13.1 %collective-permute-done.1 = bf16[128,1024]{1,0:T(8,128)(2,1)S(1)} collective-permute-done((bf16[128,1024]{1,0:T(8,128)(2,1)S(1)}, bf16[128,1024]{1,0:T(8,128)(2,1)S(1)}, u32[]{:S(2)}, u32[]{:S(2)}) %collective-permute-start.1) | collective-permute-done | bytes 262176 | tf_op jit(solution)/shard_map/while/body/eval_jaxpr/ppermute | solution.py:12
  458.7 8.6 collective-permute-done.1
  477.2 7.6 collective-permute-done.1
  486.9 7.6 collective-permute-done.1
  496.5 9.0 collective-permute-done.1
  507.6 10.0 %collective-permute-done.1 = bf16[128,1024]{1,0:T(8,128)(2,1)S(1)} collective-permute-done((bf16[128,1024]{1,0:T(8,128)(2,1)S(1)}, bf16[128,1024]{1,0:T(8,128)(2,1)S(1)}, u32[]{:S(2)}, u32[]{:S(2)}) %collective-permute-start.1) | collective-permute-done | bytes 262176 | tf_op jit(solution)/shard_map/while/body/eval_jaxpr/ppermute | solution.py:12
  519.6 10.0 %collective-permute-done.1 = bf16[128,1024]{1,0:T(8,128)(2,1)S(1)} collective-permute-done((bf16[128,1024]{1,0:T(8,128)(2,1)S(1)}, bf16[128,1024]{1,0:T(8,128)(2,1)S(1)}, u32[]{:S(2)}, u32[]{:S(2)}) %collective-permute-start.1) | collective-permute-done | bytes 262176 | tf_op jit(solution)/shard_map/while/body/eval_jaxpr/ppermute | solution.py:12
  531.6 11.0 %collective-permute-done.1 = bf16[128,1024]{1,0:T(8,128)(2,1)S(1)} collective-permute-done((bf16[128,1024]{1,0:T(8,128)(2,1)S(1)}, bf16[128,1024]{1,0:T(8,128)(2,1)S(1)}, u32[]{:S(2)}, u32[]{:S(2)}) %collective-permute-start.1) | collective-permute-done | bytes 262176 | tf_op jit(solution)/shard_map/while/body/eval_jaxpr/ppermute | solution.py:12
  544.6 9.3 collective-permute-done.1
  556.0 65.0 %collective-permute-done.1 = bf16[128,1024]{1,0:T(8,128)(2,1)S(1)} collective-permute-done((bf16[128,1024]{1,0:T(8,128)(2,1)S(1)}, bf16[128,1024]{1,0:T(8,128)(2,1)S(1)}, u32[]{:S(2)}, u32[]{:S(2)}) %collective-permute-start.1) | collective-permute-done | bytes 262176 | tf_op jit(solution)/shard_map/while/body/eval_jaxpr/ppermute | solution.py:12
  629.6 8.2 collective-permute-done.1
  638.5 6.6 conditional.8
  646.5 8.5 collective-permute-done.1
  663.6 7.9 collective-permute-done.1
  680.2 8.0 collective-permute-done.1
  688.9 6.6 conditional.8
  696.9 7.8 collective-permute-done.1
  713.3 7.9 collective-permute-done.1
  729.8 7.9 collective-permute-done.1
  746.4 8.6 collective-permute-done.1
  758.2 129.2 %all-gather.9.cloned.1.call-done = f32[32,2,4096]{2,1,0:T(2,128)} async-done(((f32[1,2,4096]{2,1,0:T(2,128)}), f32[32,2,4096]{2,1,0:T(2,128)}) %all-gather.9.cloned.1.call-update) | async-done | bytes 1048592 | tf_op jit(solution)/shard_map/all_gather | solution.py:123
  890.0 48.6 %all-reduce = f32[64,16]{1,0:T(8,128)S(1)} all-reduce(f32[64,16]{1,0:T(8,128)S(1)} %fusion.20), channel_id=2, replica_groups=mesh['section'=16,'dp'=32] {'section'}, use_global_device_ids=true, to_apply=%region_10.11.clone | all-reduce | flops 1024 | bytes 8192
  (370 shorter events, 388.1 us)
Async XLA Ops:
  6.5 74.9 %all-gather.7.cloned.1.call-start = ((), (), s32[]{:S(2)}) async-start(), calls=%async_computation.1 | async-start | bytes 2228224 | tf_op jit(solution)/shard_map/all_gather | solution.py:49
  7.3 150.9 %all-gather.5.cloned.1.call-start = ((), (), s32[]{:S(2)}) async-start(), calls=%async_computation | async-start | bytes 2228224 | tf_op jit(solution)/shard_map/all_gather | solution.py:50
  8.0 879.4 %all-gather.9.cloned.1.call-start = ((), (), s32[]{:S(2)}) async-start(), calls=%async_computation.2 | async-start | bytes 1081344 | tf_op jit(solution)/shard_map/all_gather | solution.py:123
  172.0 9.4 collective-permute-start
  251.0 9.0 collective-permute-start
  261.0 10.4 %collective-permute-start = (bf16[128,1024]{1,0:T(8,128)(2,1)S(1)}, bf16[128,1024]{1,0:T(8,128)(2,1)S(1)}, u32[]{:S(2)}, u32[]{:S(2)}) collective-permute-start(bf16[128,1024]{1,0:T(8,128)(2,1)S(1)} %get-tuple-element.721), channel_id=1, source_target_pairs={{0,32},{32,64},{64,96},{96,128},{128,160},{160,192},{192,224},{224... | collective-permute-start | bytes 786440 | tf_op jit(solution)/shard_map/while/body/eval_jaxpr/ppermute | solution.py:12
  272.4 10.7 %collective-permute-start = (bf16[128,1024]{1,0:T(8,128)(2,1)S(1)}, bf16[128,1024]{1,0:T(8,128)(2,1)S(1)}, u32[]{:S(2)}, u32[]{:S(2)}) collective-permute-start(bf16[128,1024]{1,0:T(8,128)(2,1)S(1)} %get-tuple-element.721), channel_id=1, source_target_pairs={{0,32},{32,64},{64,96},{96,128},{128,160},{160,192},{192,224},{224... | collective-permute-start | bytes 786440 | tf_op jit(solution)/shard_map/while/body/eval_jaxpr/ppermute | solution.py:12
  329.7 12.5 %collective-permute-start = (bf16[128,1024]{1,0:T(8,128)(2,1)S(1)}, bf16[128,1024]{1,0:T(8,128)(2,1)S(1)}, u32[]{:S(2)}, u32[]{:S(2)}) collective-permute-start(bf16[128,1024]{1,0:T(8,128)(2,1)S(1)} %get-tuple-element.721), channel_id=1, source_target_pairs={{0,32},{32,64},{64,96},{96,128},{128,160},{160,192},{192,224},{224... | collective-permute-start | bytes 786440 | tf_op jit(solution)/shard_map/while/body/eval_jaxpr/ppermute | solution.py:12
  363.0 9.5 collective-permute-start
  373.5 9.5 %collective-permute-start = (bf16[128,1024]{1,0:T(8,128)(2,1)S(1)}, bf16[128,1024]{1,0:T(8,128)(2,1)S(1)}, u32[]{:S(2)}, u32[]{:S(2)}) collective-permute-start(bf16[128,1024]{1,0:T(8,128)(2,1)S(1)} %get-tuple-element.721), channel_id=1, source_target_pairs={{0,32},{32,64},{64,96},{96,128},{128,160},{160,192},{192,224},{224... | collective-permute-start | bytes 786440 | tf_op jit(solution)/shard_map/while/body/eval_jaxpr/ppermute | solution.py:12
  384.0 10.7 %collective-permute-start = (bf16[128,1024]{1,0:T(8,128)(2,1)S(1)}, bf16[128,1024]{1,0:T(8,128)(2,1)S(1)}, u32[]{:S(2)}, u32[]{:S(2)}) collective-permute-start(bf16[128,1024]{1,0:T(8,128)(2,1)S(1)} %get-tuple-element.721), channel_id=1, source_target_pairs={{0,32},{32,64},{64,96},{96,128},{128,160},{160,192},{192,224},{224... | collective-permute-start | bytes 786440 | tf_op jit(solution)/shard_map/while/body/eval_jaxpr/ppermute | solution.py:12
  395.5 10.0 %collective-permute-start.1 = (bf16[128,1024]{1,0:T(8,128)(2,1)S(1)}, bf16[128,1024]{1,0:T(8,128)(2,1)S(1)}, u32[]{:S(2)}, u32[]{:S(2)}) collective-permute-start(bf16[128,1024]{1,0:T(8,128)(2,1)S(1)} %get-tuple-element.643), channel_id=1, source_target_pairs={{32,0},{64,32},{96,64},{128,96},{160,128},{192,160},{224,192},{256... | collective-permute-start | bytes 786440 | tf_op jit(solution)/shard_map/while/body/eval_jaxpr/ppermute | solution.py:12
  406.2 10.0 %collective-permute-start.1 = (bf16[128,1024]{1,0:T(8,128)(2,1)S(1)}, bf16[128,1024]{1,0:T(8,128)(2,1)S(1)}, u32[]{:S(2)}, u32[]{:S(2)}) collective-permute-start(bf16[128,1024]{1,0:T(8,128)(2,1)S(1)} %get-tuple-element.643), channel_id=1, source_target_pairs={{32,0},{64,32},{96,64},{128,96},{160,128},{192,160},{224,192},{256... | collective-permute-start | bytes 786440 | tf_op jit(solution)/shard_map/while/body/eval_jaxpr/ppermute | solution.py:12
  417.0 10.6 %collective-permute-start.1 = (bf16[128,1024]{1,0:T(8,128)(2,1)S(1)}, bf16[128,1024]{1,0:T(8,128)(2,1)S(1)}, u32[]{:S(2)}, u32[]{:S(2)}) collective-permute-start(bf16[128,1024]{1,0:T(8,128)(2,1)S(1)} %get-tuple-element.643), channel_id=1, source_target_pairs={{32,0},{64,32},{96,64},{128,96},{160,128},{192,160},{224,192},{256... | collective-permute-start | bytes 786440 | tf_op jit(solution)/shard_map/while/body/eval_jaxpr/ppermute | solution.py:12
  428.3 13.2 %collective-permute-start.1 = (bf16[128,1024]{1,0:T(8,128)(2,1)S(1)}, bf16[128,1024]{1,0:T(8,128)(2,1)S(1)}, u32[]{:S(2)}, u32[]{:S(2)}) collective-permute-start(bf16[128,1024]{1,0:T(8,128)(2,1)S(1)} %get-tuple-element.643), channel_id=1, source_target_pairs={{32,0},{64,32},{96,64},{128,96},{160,128},{192,160},{224,192},{256... | collective-permute-start | bytes 786440 | tf_op jit(solution)/shard_map/while/body/eval_jaxpr/ppermute | solution.py:12
  442.3 14.4 %collective-permute-start.1 = (bf16[128,1024]{1,0:T(8,128)(2,1)S(1)}, bf16[128,1024]{1,0:T(8,128)(2,1)S(1)}, u32[]{:S(2)}, u32[]{:S(2)}) collective-permute-start(bf16[128,1024]{1,0:T(8,128)(2,1)S(1)} %get-tuple-element.643), channel_id=1, source_target_pairs={{32,0},{64,32},{96,64},{128,96},{160,128},{192,160},{224,192},{256... | collective-permute-start | bytes 786440 | tf_op jit(solution)/shard_map/while/body/eval_jaxpr/ppermute | solution.py:12
  457.4 9.9 %collective-permute-start.1 = (bf16[128,1024]{1,0:T(8,128)(2,1)S(1)}, bf16[128,1024]{1,0:T(8,128)(2,1)S(1)}, u32[]{:S(2)}, u32[]{:S(2)}) collective-permute-start(bf16[128,1024]{1,0:T(8,128)(2,1)S(1)} %get-tuple-element.643), channel_id=1, source_target_pairs={{32,0},{64,32},{96,64},{128,96},{160,128},{192,160},{224,192},{256... | collective-permute-start | bytes 786440 | tf_op jit(solution)/shard_map/while/body/eval_jaxpr/ppermute | solution.py:12
  475.9 8.9 collective-permute-start.1
  495.2 10.3 %collective-permute-start.1 = (bf16[128,1024]{1,0:T(8,128)(2,1)S(1)}, bf16[128,1024]{1,0:T(8,128)(2,1)S(1)}, u32[]{:S(2)}, u32[]{:S(2)}) collective-permute-start(bf16[128,1024]{1,0:T(8,128)(2,1)S(1)} %get-tuple-element.643), channel_id=1, source_target_pairs={{32,0},{64,32},{96,64},{128,96},{160,128},{192,160},{224,192},{256... | collective-permute-start | bytes 786440 | tf_op jit(solution)/shard_map/while/body/eval_jaxpr/ppermute | solution.py:12
  506.3 11.3 %collective-permute-start.1 = (bf16[128,1024]{1,0:T(8,128)(2,1)S(1)}, bf16[128,1024]{1,0:T(8,128)(2,1)S(1)}, u32[]{:S(2)}, u32[]{:S(2)}) collective-permute-start(bf16[128,1024]{1,0:T(8,128)(2,1)S(1)} %get-tuple-element.643), channel_id=1, source_target_pairs={{32,0},{64,32},{96,64},{128,96},{160,128},{192,160},{224,192},{256... | collective-permute-start | bytes 786440 | tf_op jit(solution)/shard_map/while/body/eval_jaxpr/ppermute | solution.py:12
  518.3 11.3 %collective-permute-start.1 = (bf16[128,1024]{1,0:T(8,128)(2,1)S(1)}, bf16[128,1024]{1,0:T(8,128)(2,1)S(1)}, u32[]{:S(2)}, u32[]{:S(2)}) collective-permute-start(bf16[128,1024]{1,0:T(8,128)(2,1)S(1)} %get-tuple-element.643), channel_id=1, source_target_pairs={{32,0},{64,32},{96,64},{128,96},{160,128},{192,160},{224,192},{256... | collective-permute-start | bytes 786440 | tf_op jit(solution)/shard_map/while/body/eval_jaxpr/ppermute | solution.py:12
  530.3 12.3 %collective-permute-start.1 = (bf16[128,1024]{1,0:T(8,128)(2,1)S(1)}, bf16[128,1024]{1,0:T(8,128)(2,1)S(1)}, u32[]{:S(2)}, u32[]{:S(2)}) collective-permute-start(bf16[128,1024]{1,0:T(8,128)(2,1)S(1)} %get-tuple-element.643), channel_id=1, source_target_pairs={{32,0},{64,32},{96,64},{128,96},{160,128},{192,160},{224,192},{256... | collective-permute-start | bytes 786440 | tf_op jit(solution)/shard_map/while/body/eval_jaxpr/ppermute | solution.py:12
  543.3 10.6 %collective-permute-start.1 = (bf16[128,1024]{1,0:T(8,128)(2,1)S(1)}, bf16[128,1024]{1,0:T(8,128)(2,1)S(1)}, u32[]{:S(2)}, u32[]{:S(2)}) collective-permute-start(bf16[128,1024]{1,0:T(8,128)(2,1)S(1)} %get-tuple-element.643), channel_id=1, source_target_pairs={{32,0},{64,32},{96,64},{128,96},{160,128},{192,160},{224,192},{256... | collective-permute-start | bytes 786440 | tf_op jit(solution)/shard_map/while/body/eval_jaxpr/ppermute | solution.py:12
  554.7 66.3 %collective-permute-start.1 = (bf16[128,1024]{1,0:T(8,128)(2,1)S(1)}, bf16[128,1024]{1,0:T(8,128)(2,1)S(1)}, u32[]{:S(2)}, u32[]{:S(2)}) collective-permute-start(bf16[128,1024]{1,0:T(8,128)(2,1)S(1)} %get-tuple-element.643), channel_id=1, source_target_pairs={{32,0},{64,32},{96,64},{128,96},{160,128},{192,160},{224,192},{256... | collective-permute-start | bytes 786440 | tf_op jit(solution)/shard_map/while/body/eval_jaxpr/ppermute | solution.py:12
  628.3 9.5 %collective-permute-start.1 = (bf16[128,1024]{1,0:T(8,128)(2,1)S(1)}, bf16[128,1024]{1,0:T(8,128)(2,1)S(1)}, u32[]{:S(2)}, u32[]{:S(2)}) collective-permute-start(bf16[128,1024]{1,0:T(8,128)(2,1)S(1)} %get-tuple-element.643), channel_id=1, source_target_pairs={{32,0},{64,32},{96,64},{128,96},{160,128},{192,160},{224,192},{256... | collective-permute-start | bytes 786440 | tf_op jit(solution)/shard_map/while/body/eval_jaxpr/ppermute | solution.py:12
  645.2 9.8 %collective-permute-start.1 = (bf16[128,1024]{1,0:T(8,128)(2,1)S(1)}, bf16[128,1024]{1,0:T(8,128)(2,1)S(1)}, u32[]{:S(2)}, u32[]{:S(2)}) collective-permute-start(bf16[128,1024]{1,0:T(8,128)(2,1)S(1)} %get-tuple-element.643), channel_id=1, source_target_pairs={{32,0},{64,32},{96,64},{128,96},{160,128},{192,160},{224,192},{256... | collective-permute-start | bytes 786440 | tf_op jit(solution)/shard_map/while/body/eval_jaxpr/ppermute | solution.py:12
  662.3 9.2 collective-permute-start.1
  678.9 9.3 collective-permute-start.1
  695.6 9.1 collective-permute-start.1
  712.0 9.2 collective-permute-start.1
  728.5 9.2 collective-permute-start.1
  745.1 9.9 %collective-permute-start.1 = (bf16[128,1024]{1,0:T(8,128)(2,1)S(1)}, bf16[128,1024]{1,0:T(8,128)(2,1)S(1)}, u32[]{:S(2)}, u32[]{:S(2)}) collective-permute-start(bf16[128,1024]{1,0:T(8,128)(2,1)S(1)} %get-tuple-element.643), channel_id=1, source_target_pairs={{32,0},{64,32},{96,64},{128,96},{160,128},{192,160},{224,192},{256... | collective-permute-start | bytes 786440 | tf_op jit(solution)/shard_map/while/body/eval_jaxpr/ppermute | solution.py:12
  (59 other events, 1062.7 us)
Sparse Core Ops, SparseCore 0:
  9.4 71.9 all-gather.6
  83.5 74.5 all-gather.4
  756.4 130.9 all-gather.8
where the time goes:
time: 961 us; the launch traced here: 946 us
  waiting for transfers between devices  614 us (64%)
  starting transfers between devices  146 us (15%)
  matrix products  54.6 us (6%)
  blocking collectives  48.6 us (5%)
  local copies, waits for them, and re-layouts  43.1 us (4%)
  other arithmetic  22.7 us (2%)
  between operations  13.8 us (1%)
    ppermute x46, waiting for transfers between devices, from_behind(): lax.ppermute(value, axis, [(source, source + steps) for source in range(i...  340 us
    ppermute x46, starting transfers between devices, from_behind(): lax.ppermute(value, axis, [(source, source + steps) for source in range(i...  146 us
    all_gather x1, waiting for transfers between devices, on_device(): lax.all_gather(factors, 'dp', axis=0, tiled=True)  129 us
    all_gather x1, waiting for transfers between devices, on_device(): seed_rows = lax.all_gather(cotangent, 'section', axis=2, tiled=True)  72.8 us
    all_gather x1, waiting for transfers between devices, on_device(): features = lax.all_gather(inputs, 'section', axis=2, tiled=True)  70.5 us
    unnamed x1, blocking collectives  48.6 us
    select_n x23, other arithmetic, forward_step(): current = jnp.where(position == 0, first_rows, incoming)  22.5 us
  transfers between devices with their start and end apart: 49, of which 49 were waited for; matrix products, arithmetic and copies ran while one was open for 1% of the time, Pallas kernels for 0%

commit v1 on v0

v1 whole, which is shorter than its diff:
```python
import functools

import jax
import jax.numpy as jnp
from jax import lax
from jax.experimental import pallas as pl
from jax.experimental.pallas import tpu as pltpu
from jax.sharding import PartitionSpec as P

AXES = ("section", "dp")
TOK = 128
STAGE = 8
D = 1024
RANK = 64
PACK = D + 2 * RANK
PIECE = 128


def flat(x, y, z, c):
    return (y % 8 * 2 + x % 2) * 32 + ((x % 4 // 2) * 8 + z % 8) * 2 + c


def pairs(target):
    out = []
    for x in range(4):
        for y in range(8):
            for z in range(8):
                for c in range(2):
                    to = target(x, y, z, c)
                    if to is not None:
                        out.append((flat(x, y, z, c), flat(*to)))
    return out


def move(value, target):
    return lax.ppermute(value, AXES, pairs(target))


def swap_core(value):
    return move(value, lambda x, y, z, c: (x, y, z, 1 - c))


BUFFERS = []
for core_flag in (0, 1):
    for column_flag, quarter in ((0, 0), (0, 1), (0, 3), (1, 0), (1, 2), (1, 1), (1, 3), (0, 2)):
        BUFFERS.append((column_flag, core_flag, quarter))


def gather_stage(pack, core, quarter):
    half = lax.dynamic_slice_in_dim(pack, core * (D // 2), D // 2, 0)
    piece = lax.dynamic_slice_in_dim(pack, (core * 4 + quarter) * PIECE, PIECE, 0)
    rows = [
        move(piece, lambda x, y, z, c, r=r: (x, y // 4 * 4 + (y + r) % 4, z, c)) for r in (1, 2, 3)
    ]
    beside = move(half, lambda x, y, z, c: (x + 1 if c == 0 else x - 1, y, z, c))
    beside_other = swap_core(beside)
    own = jnp.stack(rows)
    above = move(own, lambda x, y, z, c: (x, y, z - 1, c))
    below = move(own, lambda x, y, z, c: (x, y, z + 1, c))
    near = move(own, lambda x, y, z, c: (x ^ 1, y, z, c))
    far = move(own, lambda x, y, z, c: (3 - x, y, z, c))
    near_above = move(near, lambda x, y, z, c: (x, y, z - 1, c))
    near_below = move(near, lambda x, y, z, c: (x, y, z + 1, c))
    own_far = move(far, lambda x, y, z, c: (x ^ 1, y, z, c))
    mine = [own, above, below, near, far, near_above, near_below, own_far]
    return [beside, beside_other] + mine + [swap_core(value) for value in mine]


def load_layers(place, pack, beside, buffers, layers, sems, reverse):
    row, col, core, quarter = (place[k] for k in range(4))
    for step in range(4):
        source_row = 3 - step if reverse else step
        distance = (row - source_row) & 3
        mine, other = source_row * 2 + col, source_row * 2 + 1 - col

        @pl.when(distance == 0)
        def _():
            pltpu.make_async_copy(pack, layers.at[mine], sems.at[mine]).start()
            for flag in (0, 1):
                side = jnp.where(flag == 0, core, 1 - core)
                rows = pl.ds(pl.multiple_of(side * (D // 2), D // 2), D // 2)
                pltpu.make_async_copy(
                    beside[flag], layers.at[other, rows], sems.at[other]
                ).start()

        @pl.when(distance > 0)
        def _():
            for (column_flag, core_flag, shift), ref in zip(BUFFERS, buffers):
                slot = other if column_flag else mine
                side = 1 - core if core_flag else core
                piece = side * 4 + ((quarter + shift) & 3)
                rows = pl.ds(pl.multiple_of(piece * PIECE, PIECE), PIECE)
                pltpu.make_async_copy(
                    ref.at[distance - 1], layers.at[slot, rows], sems.at[slot]
                ).start()


def await_layer(layers, sems, slot):
    pltpu.make_async_copy(layers.at[slot], layers.at[slot], sems.at[slot]).wait()


def forward_one(slot, hidden, layers, slope, left):
    both = jnp.dot(hidden, layers[slot], preferred_element_type=jnp.float32)
    preact = both[:, :D]
    sig = jax.nn.sigmoid(preact)
    slope[slot] = sig * (1.0 + preact * (1.0 - sig))
    left[slot] = both[:, D:]
    return (hidden.astype(jnp.float32) + preact * sig).astype(jnp.bfloat16)


def backward_one(slot, upstream, layers, slope, left, factor):
    wide = upstream.astype(jnp.float32)
    grad = (wide * slope[slot]).astype(jnp.bfloat16)
    right = jnp.dot(grad, layers[slot, :, D:], preferred_element_type=jnp.float32)
    carried = lax.dot_general(
        grad, layers[slot, :, :D], (((1,), (1,)), ((), ())), preferred_element_type=jnp.float32
    )
    product = lax.dot_general(
        left[slot],
        right,
        (((0,), (0,)), ((), ())),
        precision=lax.Precision.HIGHEST,
        preferred_element_type=jnp.float32,
    )
    factor[slot] = product[:RANK, RANK:].astype(jnp.bfloat16)
    return (wide + carried).astype(jnp.bfloat16)


def rows_of(arrived):
    return jnp.concatenate([arrived[k] for k in range(arrived.shape[0])], axis=1)


def first_kernel(place, arrived, pack, *refs):
    beside, buffers = refs[:2], refs[2:18]
    hidden_out, slope, left, layers, sems = refs[18:]

    @pl.when(place[4] == 0)
    def _():
        load_layers(place, pack, beside, buffers, layers, sems, False)
        hidden_out[...] = rows_of(arrived)

        def body(slot, carry):
            await_layer(layers, sems, slot)
            hidden_out[...] = forward_one(slot, hidden_out[...], layers, slope, left)
            return carry

        lax.fori_loop(0, STAGE, body, 0)


def middle_kernel(place, hidden, arrived, pack, *refs):
    beside, buffers = refs[:2], refs[2:18]
    upstream, factor, current, slope, left, layers, sems = refs[18:]

    @pl.when(place[4] == 1)
    def _():
        load_layers(place, pack, beside, buffers, layers, sems, False)
        current[...] = hidden[...]
        upstream[...] = rows_of(arrived)

        def ahead(slot, carry):
            await_layer(layers, sems, slot)
            current[...] = forward_one(slot, current[...], layers, slope, left)
            return carry

        lax.fori_loop(0, STAGE, ahead, 0)

        def back(step, carry):
            slot = STAGE - 1 - step
            upstream[...] = backward_one(slot, upstream[...], layers, slope, left, factor)
            return carry

        lax.fori_loop(0, STAGE, back, 0)


def last_kernel(place, upstream, slope, left, pack, *refs):
    beside, buffers = refs[:2], refs[2:18]
    factor, current, layers, sems = refs[18:]

    @pl.when(place[4] == 0)
    def _():
        load_layers(place, pack, beside, buffers, layers, sems, True)
        current[...] = upstream[...]

        def back(step, carry):
            slot = STAGE - 1 - step
            await_layer(layers, sems, slot)
            current[...] = backward_one(slot, current[...], layers, slope, left, factor)
            return carry

        lax.fori_loop(0, STAGE, back, 0)


VMEM = pl.BlockSpec(memory_space=pltpu.VMEM)
SMEM = pl.BlockSpec(memory_space=pltpu.SMEM)
HBM = pl.BlockSpec(memory_space=pl.ANY)
PARAMS = pltpu.CompilerParams(vmem_limit_bytes=48 * 1024 * 1024)
TOKENS = jax.ShapeDtypeStruct((TOK, D), jnp.bfloat16)
SLOPE = jax.ShapeDtypeStruct((STAGE, TOK, D), jnp.float32)
LEFT = jax.ShapeDtypeStruct((STAGE, TOK, 2 * RANK), jnp.float32)
FACTOR = jax.ShapeDtypeStruct((STAGE, RANK, RANK), jnp.bfloat16)
LAYERS = pltpu.VMEM((STAGE, D, PACK), jnp.bfloat16)
SEMS = pltpu.SemaphoreType.DMA((STAGE,))


def scratch(shape):
    return pltpu.VMEM(shape.shape, shape.dtype)


def cost(passes):
    return pl.CostEstimate(
        flops=2 * passes * STAGE * TOK * D * PACK,
        bytes_accessed=STAGE * D * PACK * 2,
        transcendentals=STAGE * TOK * D,
    )


def on_device(inputs, cotangent, weights, proj_in, proj_out, query_factors):
    section, dp = lax.axis_index("section"), lax.axis_index("dp")
    y, col = section // 2, section % 2
    x_hi, z, core = dp // 16, dp // 2 % 8, dp % 2
    stage = y // 4
    quarter = (z + 2 * x_hi) % 4
    place = jnp.stack([y % 4, col, core, quarter, stage]).astype(jnp.int32)

    ahead = inputs.reshape(STAGE, TOK, -1)
    seeds = cotangent.reshape(4, 2, TOK, -1)[::-1].reshape(STAGE, TOK, -1)
    arrived = lax.all_to_all(
        jnp.concatenate([ahead, seeds]), "section", 0, 0, tiled=True
    )

    pack = jnp.concatenate([weights[0], proj_in[0], proj_out[0]], axis=1)
    gathered = gather_stage(pack, core, quarter)

    across = [[(h * 8 + k) * 2 + c for h in range(2) for c in range(2)] for k in range(8)]
    along = [[(h * 8 + k) * 2 + c for k in range(8)] for h in range(2) for c in range(2)]
    local = query_factors[0]
    queries = lax.all_to_all(
        jnp.broadcast_to(local[None], (4,) + local.shape),
        "dp",
        0,
        0,
        tiled=True,
        axis_index_groups=across,
    ).reshape(4 * local.shape[0], -1)

    hidden, slope, left = pl.pallas_call(
        first_kernel,
        out_shape=(TOKENS, SLOPE, LEFT),
        in_specs=[SMEM, VMEM] + [HBM] * 19,
        out_specs=(VMEM, VMEM, VMEM),
        scratch_shapes=[LAYERS, SEMS],
        compiler_params=PARAMS,
        cost_estimate=cost(1),
        name="forward_first_stage",
    )(place, arrived, pack, *gathered)
    hidden = move(hidden, lambda x, y, z, c: (x, 7 - y, z, c) if y < 4 else None)
    upstream, factor_late = pl.pallas_call(
        middle_kernel,
        out_shape=(TOKENS, FACTOR),
        in_specs=[SMEM, VMEM, VMEM] + [HBM] * 19,
        out_specs=(VMEM, VMEM),
        scratch_shapes=[scratch(TOKENS), scratch(SLOPE), scratch(LEFT), LAYERS, SEMS],
        compiler_params=PARAMS,
        cost_estimate=cost(2),
        name="second_stage",
    )(place, hidden, arrived, pack, *gathered)
    upstream = move(upstream, lambda x, y, z, c: (x, 7 - y, z, c) if y > 3 else None)
    factor_early = pl.pallas_call(
        last_kernel,
        out_shape=FACTOR,
        in_specs=[SMEM, VMEM, VMEM, VMEM] + [HBM] * 19,
        out_specs=VMEM,
        scratch_shapes=[scratch(TOKENS), LAYERS, SEMS],
        compiler_params=PARAMS,
        cost_estimate=cost(1),
        name="backward_first_stage",
    )(place, upstream, slope, left, pack, *gathered)

    factor = jnp.where(stage == 0, factor_early, factor_late).reshape(STAGE, -1)
    groups = [list(range(8)), list(range(8, 16))]
    parts = lax.all_to_all(factor, "section", 0, 0, tiled=True, axis_index_groups=groups)
    sums = parts.reshape(2, 4, -1).astype(jnp.float32).sum(1)
    sums = jnp.where(stage == 0, sums, sums[::-1]).astype(jnp.bfloat16)
    sums = lax.all_to_all(
        jnp.broadcast_to(sums[None], (8,) + sums.shape),
        "dp",
        0,
        0,
        tiled=True,
        axis_index_groups=along,
    ).reshape(16, -1)
    table = lax.dot_general(
        sums, queries, (((1,), (1,)), ((), ())), preferred_element_type=jnp.float32
    ).reshape(8, 2, -1)

    outgoing = lax.dynamic_update_slice_in_dim(
        jnp.zeros((16,) + table.shape[1:], jnp.float32), table, x_hi * 8, 0
    )
    scores = lax.all_to_all(outgoing, "section", 0, 0, tiled=True).sum(0)
    scores = scores.reshape(2, 4, -1).transpose(1, 0, 2)
    scores = lax.all_to_all(scores, "dp", 0, 0, tiled=True, axis_index_groups=across)
    return scores.reshape(2, 4, -1).sum(0)


def solution(mesh):
    placed = (
        P("dp", None, "section"),
        P("dp", None, "section"),
        P("section", None, None),
        P("section", None, None),
        P("section", None, None),
        P("section", "dp", None),
    )
    return jax.shard_map(
        on_device, mesh=mesh, in_specs=placed, out_specs=P("section", "dp"), check_vma=False
    )
```

time: 961 us -> 276 us (0.29); the launches traced: 946 us -> 274 us
  waiting for transfers between devices: 614 us -> 80.6 us
  matrix products: 54.6 us -> 0.25 us
  starting transfers between devices: 146 us -> 107 us
  Pallas kernels: 0 us -> 22.8 us
  blocking collectives: 48.6 us -> 29.2 us
  other arithmetic: 22.7 us -> 3.9 us
  between operations: 13.8 us -> 0.64 us
  local copies, waits for them, and re-layouts: 43.1 us -> 30.2 us
    ppermute x46 -> x22, waiting for transfers between devices: 340 us -> 54.3 us  [move(): return lax.ppermute(value, AXES, pairs(target))]
    all_gather x3 -> x0, waiting for transfers between devices: 272 us -> none  [the longest x1 129 us: on_device(): lax.all_gather(factors, 'dp', axis=0, tiled=True)]
    ppermute x46 -> x22, starting transfers between devices: 146 us -> 83.3 us  [move(): return lax.ppermute(value, AXES, pairs(target))]
    dot_general x49 -> x1, matrix products: 54.6 us -> 0.25 us  [on_device(): lax.dot_general(sums, queries, (((1,), (1,)), ((), ())), preferred_elemen...]
    unnamed x1 -> x0, blocking collectives: 48.6 us -> none
    all_to_all x0 -> x3, blocking collectives: none -> 29.2 us  [the longest x1 10.3 us: on_device(): lax.all_to_all(scores, 'dp', 0, 0, tiled=True, axis_index_groups=across)]
    all_to_all x0 -> x3, waiting for transfers between devices: none -> 26.4 us  [the longest x1 10.7 us: on_device(): lax.all_to_all(jnp.concatenate([ahead, seeds]), 'section', 0, 0, tiled=True)]
    all_to_all x0 -> x3, starting transfers between devices: none -> 23.3 us  [the longest x1 14 us: on_device(): lax.all_to_all(jnp.concatenate([ahead, seeds]), 'section', 0, 0, tiled=True)]
  transfers between devices with their start and end apart: 49 -> 25, of which waited for: 49 -> 10; matrix products, arithmetic and copies ran while one was open for 1% -> 5% of each run, Pallas kernels for 0% -> 0%
where the time goes in v1:
time: 276 us; the launch traced here: 274 us
  starting transfers between devices  107 us (39%)
  waiting for transfers between devices  80.6 us (29%)
  local copies, waits for them, and re-layouts  30.2 us (11%)
  blocking collectives  29.2 us (11%)
  Pallas kernels  22.8 us (8%)
  other arithmetic  3.9 us (1%)
    ppermute x22, starting transfers between devices, move(): return lax.ppermute(value, AXES, pairs(target))  83.3 us
    ppermute x22, waiting for transfers between devices, move(): return lax.ppermute(value, AXES, pairs(target))  54.3 us
    all_to_all x1, starting transfers between devices, on_device(): lax.all_to_all(jnp.concatenate([ahead, seeds]), 'section', 0, 0, tiled=True)  14 us
    unnamed x34, local copies, waits for them, and re-layouts  12.7 us
    pallas_call x1, Pallas kernels, on_device(): pl.pallas_call(last_kernel, out_shape=FACTOR, in_specs=[SMEM, VMEM, VMEM,...  12.4 us
    all_to_all x1, waiting for transfers between devices, on_device(): lax.all_to_all(jnp.concatenate([ahead, seeds]), 'section', 0, 0, tiled=True)  10.7 us
    all_to_all x1, blocking collectives, on_device(): lax.all_to_all(scores, 'dp', 0, 0, tiled=True, axis_index_groups=across)  10.3 us
    all_to_all x1, blocking collectives, on_device(): scores = lax.all_to_all(outgoing, 'section', 0, 0, tiled=True).sum(0)  9.88 us
  transfers between devices with their start and end apart: 25, of which 10 were waited for; matrix products, arithmetic and copies ran while one was open for 5% of the time, Pallas kernels for 0%

profile of v1, /device:TPU:1, one launch (start us, length us, event | category | flops | bytes accessed | tf_op | source)
XLA Modules:
  0.0 274.2 jit_solution(9237078226097061503)
XLA Ops:
  2.2 3.8 %concatenate.7.pack = bf16[1024,1152]{1,0:T(8,128)(2,1)S(1)} concatenate(bf16[1024,1024]{1,0:T(8,128)(2,1)} %bitcast.23, bf16[1024,64]{1,0:T(8,128)(2,1)S(1)} %bitcast.25, bf16[1024,64]{1,0:T(8,128)(2,1)S(1)} %bitcast.26), dimensions={1} | concatenate | bytes 4718592 | tf_op jit(solution)/shard_map/concatenate | solution.py:231
  6.0 5.0 %collective-permute-start.3 = (bf16[128,1152]{1,0:T(8,128)(2,1)S(1)}, bf16[128,1152]{1,0:T(8,128)(2,1)S(1)}, u32[]{:S(2)}, u32[]{:S(2)}) collective-permute-start(bf16[128,1152]{1,0:T(8,128)(2,1)S(1)} %constant_dynamic-slice_fusion), channel_id=1, source_target_pairs={{0,128},{1,129},{2,130},{3,131},{4,132},{5,133},{6,134},{7,135},{8... | collective-permute-start | bytes 884744 | tf_op jit(solution)/shard_map/ppermute | solution.py:36
  11.1 3.0 %collective-permute-start.4 = (bf16[128,1152]{1,0:T(8,128)(2,1)S(1)}, bf16[128,1152]{1,0:T(8,128)(2,1)S(1)}, u32[]{:S(2)}, u32[]{:S(2)}) collective-permute-start(bf16[128,1152]{1,0:T(8,128)(2,1)S(1)} %constant_dynamic-slice_fusion), channel_id=1, source_target_pairs={{0,192},{1,193},{2,194},{3,195},{4,196},{5,197},{6,198},{7,199},{8... | collective-permute-start | bytes 884744 | tf_op jit(solution)/shard_map/ppermute | solution.py:36
  14.0 2.3 collective-permute-start.2
  16.4 7.6 %collective-permute-done.3 = bf16[128,1152]{1,0:T(8,128)(2,1)S(1)} collective-permute-done((bf16[128,1152]{1,0:T(8,128)(2,1)S(1)}, bf16[128,1152]{1,0:T(8,128)(2,1)S(1)}, u32[]{:S(2)}, u32[]{:S(2)}) %collective-permute-start.3) | collective-permute-done | bytes 294944 | tf_op jit(solution)/shard_map/ppermute | solution.py:36
  23.9 5.9 %collective-permute-done.2 = bf16[128,1152]{1,0:T(8,128)(2,1)S(1)} collective-permute-done((bf16[128,1152]{1,0:T(8,128)(2,1)S(1)}, bf16[128,1152]{1,0:T(8,128)(2,1)S(1)}, u32[]{:S(2)}, u32[]{:S(2)}) %collective-permute-start.2) | collective-permute-done | bytes 294944 | tf_op jit(solution)/shard_map/ppermute | solution.py:36
  29.9 4.6 %collective-permute-start.7 = (bf16[3,128,1152]{2,1,0:T(8,128)(2,1)S(1)}, bf16[3,128,1152]{2,1,0:T(8,128)(2,1)S(1)}, u32[]{:S(2)}, u32[]{:S(2)}) collective-permute-start(bf16[3,128,1152]{2,1,0:T(8,128)(2,1)S(1)} %pad_maximum_fusion.refs_2_), channel_id=1, source_target_pairs={{0,32},{1,33},{2,34},{3,35},{4,36},{5,37},{6,38},{7,39},{8,40},{9,... | collective-permute-start | bytes 2654216 | tf_op jit(solution)/shard_map/ppermute | solution.py:36
  34.5 3.7 %collective-permute-start.8 = (bf16[3,128,1152]{2,1,0:T(8,128)(2,1)S(1)}, bf16[3,128,1152]{2,1,0:T(8,128)(2,1)S(1)}, u32[]{:S(2)}, u32[]{:S(2)}) collective-permute-start(bf16[3,128,1152]{2,1,0:T(8,128)(2,1)S(1)} %pad_maximum_fusion.refs_2_), channel_id=1, source_target_pairs={{0,48},{1,49},{2,50},{3,51},{4,52},{5,53},{6,54},{7,55},{8,56},{9,... | collective-permute-start | bytes 2654216 | tf_op jit(solution)/shard_map/ppermute | solution.py:36
  39.7 10.7 %collective-permute-start.5 = (bf16[3,128,1152]{2,1,0:T(8,128)(2,1)S(1)}, bf16[3,128,1152]{2,1,0:T(8,128)(2,1)S(1)}, u32[]{:S(2)}, u32[]{:S(2)}) collective-permute-start(bf16[3,128,1152]{2,1,0:T(8,128)(2,1)S(1)} %pad_maximum_fusion.refs_2_), channel_id=1, source_target_pairs={{0,14},{1,15},{2,0},{3,1},{4,2},{5,3},{6,4},{7,5},{8,6},{9,7},{10,... | collective-permute-start | bytes 2654216 | tf_op jit(solution)/shard_map/ppermute | solution.py:36
  50.3 2.8 %collective-permute-start = (bf16[512,1152]{1,0:T(8,128)(2,1)S(1)}, bf16[512,1152]{1,0:T(8,128)(2,1)}, u32[]{:S(2)}, u32[]{:S(2)}) collective-permute-start(bf16[512,1152]{1,0:T(8,128)(2,1)S(1)} %constant_dynamic-slice_fusion.1), channel_id=1, source_target_pairs={{0,32},{1,49},{2,34},{3,51},{4,36},{5,53},{6,38},{7,55},{8,40},{9,... | collective-permute-start | bytes 3538952 | tf_op jit(solution)/shard_map/ppermute | solution.py:36
  55.0 5.1 %collective-permute-start.12 = (bf16[3,128,1152]{2,1,0:T(8,128)(2,1)S(1)}, bf16[3,128,1152]{2,1,0:T(8,128)(2,1)S(1)}, u32[]{:S(2)}, u32[]{:S(2)}) collective-permute-start(bf16[3,128,1152]{2,1,0:T(8,128)(2,1)S(1)} %pad_maximum_fusion.refs_2_), channel_id=1, source_target_pairs={{0,1},{1,0},{2,3},{3,2},{4,5},{5,4},{6,7},{7,6},{8,9},{9,8},{10,11... | collective-permute-start | bytes 2654216 | tf_op jit(solution)/shard_map/ppermute | solution.py:36
  60.2 10.9 %collective-permute-start.9 = (bf16[3,128,1152]{2,1,0:T(8,128)(2,1)S(1)}, bf16[3,128,1152]{2,1,0:T(8,128)(2,1)}, u32[]{:S(2)}, u32[]{:S(2)}) collective-permute-start(bf16[3,128,1152]{2,1,0:T(8,128)(2,1)S(1)} %collective-permute-done.7.refs_5_), channel_id=1, source_target_pairs={{0,14},{1,15},{2,0},{3,1},{4,2},{5,3},{6,4},{7,5},{8,6},{9,7},{10,... | collective-permute-start | bytes 2654216 | tf_op jit(solution)/shard_map/ppermute | solution.py:36
  74.2 3.4 %collective-permute-start.11 = (bf16[3,128,1152]{2,1,0:T(8,128)(2,1)S(1)}, bf16[3,128,1152]{2,1,0:T(8,128)(2,1)}, u32[]{:S(2)}, u32[]{:S(2)}) collective-permute-start(bf16[3,128,1152]{2,1,0:T(8,128)(2,1)S(1)} %collective-permute-done.8.refs_6_), channel_id=1, source_target_pairs={{0,32},{1,33},{2,34},{3,35},{4,36},{5,37},{6,38},{7,39},{8,40},{9,... | collective-permute-start | bytes 2654216 | tf_op jit(solution)/shard_map/ppermute | solution.py:36
  77.6 7.6 %collective-permute-start.13 = (bf16[3,128,1152]{2,1,0:T(8,128)(2,1)S(1)}, bf16[3,128,1152]{2,1,0:T(8,128)(2,1)S(1)}, u32[]{:S(2)}, u32[]{:S(2)}) collective-permute-start(bf16[3,128,1152]{2,1,0:T(8,128)(2,1)S(1)} %collective-permute-done.5.refs_3_), channel_id=1, source_target_pairs={{0,1},{1,0},{2,3},{3,2},{4,5},{5,4},{6,7},{7,6},{8,9},{9,8},{10,11... | collective-permute-start | bytes 2654216 | tf_op jit(solution)/shard_map/ppermute | solution.py:36
  88.9 3.9 %collective-permute-start.15 = (bf16[3,128,1152]{2,1,0:T(8,128)(2,1)S(1)}, bf16[3,128,1152]{2,1,0:T(8,128)(2,1)S(1)}, u32[]{:S(2)}, u32[]{:S(2)}) collective-permute-start(bf16[3,128,1152]{2,1,0:T(8,128)(2,1)S(1)} %collective-permute-done.7.refs_5_), channel_id=1, source_target_pairs={{0,1},{1,0},{2,3},{3,2},{4,5},{5,4},{6,7},{7,6},{8,9},{9,8},{10,11... | collective-permute-start | bytes 2654216 | tf_op jit(solution)/shard_map/ppermute | solution.py:36
  92.8 3.1 %collective-permute-done.10.refs_8_ = bf16[3,128,1152]{2,1,0:T(8,128)(2,1)} collective-permute-done((bf16[3,128,1152]{2,1,0:T(8,128)(2,1)S(1)}, bf16[3,128,1152]{2,1,0:T(8,128)(2,1)}, u32[]{:S(2)}, u32[]{:S(2)}) %collective-permute-start.10) | collective-permute-done | bytes 884768 | tf_op jit(solution)/shard_map/ppermute | solution.py:36
  96.0 3.2 %collective-permute-start.1 = (bf16[512,1152]{1,0:T(8,128)(2,1)}, bf16[512,1152]{1,0:T(8,128)(2,1)}, u32[]{:S(2)}, u32[]{:S(2)}) collective-permute-start(bf16[512,1152]{1,0:T(8,128)(2,1)} %collective-permute-done.refs_0_), channel_id=1, source_target_pairs={{0,1},{1,0},{2,3},{3,2},{4,5},{5,4},{6,7},{7,6},{8,9},{9,8},{10,11... | collective-permute-start | bytes 3538952 | tf_op jit(solution)/shard_map/ppermute | solution.py:36
  101.2 2.4 collective-permute-start.17
  106.5 2.4 collective-permute-start.19
  119.0 14.0 %all-to-all-start = ((bf16[16,128,64]{1,2,0:T(8,128)(2,1)}), bf16[16,128,64]{1,2,0:T(8,128)(2,1)}, u32[]{:S(2)}, u32[]{:S(2)}) async-start(bf16[16,128,64]{1,2,0:T(8,128)(2,1)} %copy.29), calls=%async_computation | async-start | bytes 524288 | tf_op jit(solution)/shard_map/all_to_all | solution.py:227
  133.1 10.7 %all-to-all-done = bf16[16,128,64]{1,2,0:T(8,128)(2,1)} async-done(((bf16[16,128,64]{1,2,0:T(8,128)(2,1)}), bf16[16,128,64]{1,2,0:T(8,128)(2,1)}, u32[]{:S(2)}, u32[]{:S(2)}) %all-to-all-start) | async-done | bytes 262176 | tf_op jit(solution)/shard_map/all_to_all | solution.py:227
  148.0 9.1 %forward_first_stage.1 = (bf16[128,1024]{1,0:T(8,128)(2,1)S(1)}, f32[8,128,1024]{2,1,0:T(8,128)}, f32[8,128,128]{2,1,0:T(8,128)S(1)}) custom-call(s32[5]{0:T(128)S(1)} %stack.35.place, bf16[16,128,64]{2,1,0:T(8,128)(2,1)S(1)} %copy-done.3, bf16[1024,1152]{1,0:T(8,128)(2,1)} %copy-done.8, bf16[512,1152]{1,0:T(8,128)(2,1)} %collective-permute-done.refs_0_, ...), custom_call_target="tpu_custom_call" | custom-call | flops 2415919104 | bytes 18874368 | tf_op jit(solution)/shard_map/forward_first_stage/pallas_call | solution.py:246
  158.4 11.0 %collective-permute-done.20.hidden = bf16[128,1024]{1,0:T(8,128)(2,1)S(1)} collective-permute-done((bf16[128,1024]{1,0:T(8,128)(2,1)S(1)}, bf16[128,1024]{1,0:T(8,128)(2,1)S(1)}, u32[]{:S(2)}, u32[]{:S(2)}) %collective-permute-start.20) | collective-permute-done | bytes 262176 | tf_op jit(solution)/shard_map/ppermute | solution.py:36
  172.7 24.7 %collective-permute-done.21.upstream = bf16[128,1024]{1,0:T(8,128)(2,1)} collective-permute-done((bf16[128,1024]{1,0:T(8,128)(2,1)}, bf16[128,1024]{1,0:T(8,128)(2,1)}, u32[]{:S(2)}, u32[]{:S(2)}) %collective-permute-start.21) | collective-permute-done | bytes 262176 | tf_op jit(solution)/shard_map/ppermute | solution.py:36
  199.6 12.4 %backward_first_stage.1 = bf16[8,64,64]{2,1,0:T(8,128)(2,1)S(1)} custom-call(s32[5]{0:T(128)S(1)} %stack.35.place, bf16[128,1024]{1,0:T(8,128)(2,1)} %collective-permute-done.21.upstream, f32[8,128,1024]{2,1,0:T(8,128)} %get-tuple-element.12.slope, f32[8,128,128]{2,1,0:T(8,128)S(1)} %copy-done.5, bf16[1024,1152]{1,0:T(8,128)(2,1)} %copy-done.8, ...), custom_call_target="tpu_custom_call" | custom-call | flops 2415919104 | bytes 18874368 | tf_op jit(solution)/shard_map/backward_first_stage/pallas_call | solution.py:268
  213.7 8.9 %all_to_all.35 = bf16[8,2,2048]{2,1,0:T(2,128)(2,1)S(1)} all-to-all(bf16[8,2,2048]{2,1,0:T(2,128)(2,1)S(1)} %reshape.40), channel_id=1, replica_groups={{0,32,64,96,128,160,192,224},{256,288,320,352,384,416,448,480},{1,33,65..., dimensions={0} | all-to-all | bytes 131072 | tf_op jit(solution)/shard_map/all_to_all | solution.py:281
  224.4 6.0 %all-to-all-start.3 = ((bf16[4,16,4096]{2,1,0:T(8,128)(2,1)}), bf16[4,16,4096]{2,1,0:T(8,128)(2,1)S(1)}, u32[]{:S(2)}, u32[]{:S(2)}) async-start(bf16[4,16,4096]{2,1,0:T(8,128)(2,1)} %broadcast_in_dim.19), calls=%async_computation.3 | async-start | bytes 1048576 | tf_op jit(solution)/shard_map/all_to_all | solution.py:237
  231.8 8.0 %all-to-all-done.3 = bf16[4,16,4096]{2,1,0:T(8,128)(2,1)S(1)} async-done(((bf16[4,16,4096]{2,1,0:T(8,128)(2,1)}), bf16[4,16,4096]{2,1,0:T(8,128)(2,1)S(1)}, u32[]{:S(2)}, u32[]{:S(2)}) %all-to-all-start.3) | async-done | bytes 524320 | tf_op jit(solution)/shard_map/all_to_all | solution.py:237
  240.6 3.4 %all-to-all-start.2 = ((bf16[8,2,4096]{2,1,0:T(2,128)(2,1)}), bf16[8,2,4096]{2,1,0:T(2,128)(2,1)S(1)}, u32[]{:S(2)}, u32[]{:S(2)}) async-start(bf16[8,2,4096]{2,1,0:T(2,128)(2,1)} %broadcast_in_dim.17), calls=%async_computation.2 | async-start | bytes 262144 | tf_op jit(solution)/shard_map/all_to_all | solution.py:284
  244.0 7.7 %all-to-all-done.2 = bf16[8,2,4096]{2,1,0:T(2,128)(2,1)S(1)} async-done(((bf16[8,2,4096]{2,1,0:T(2,128)(2,1)}), bf16[8,2,4096]{2,1,0:T(2,128)(2,1)S(1)}, u32[]{:S(2)}, u32[]{:S(2)}) %all-to-all-start.2) | async-done | bytes 131104 | tf_op jit(solution)/shard_map/all_to_all | solution.py:284
  252.0 9.9 %all_to_all.36 = f32[16,1,128]{2,1,0:T(1,128)S(1)} all-to-all(f32[16,1,128]{2,1,0:T(1,128)S(1)} %reshape.42), channel_id=1, replica_groups=mesh['section'=16,'dp'=32] {'section'}, dimensions={0} | all-to-all | bytes 16384 | tf_op jit(solution)/shard_map/all_to_all | solution.py:299
  263.3 10.3 %all_to_all.37 = f32[4,2,16]{2,1,0:T(2,128)S(1)} all-to-all(f32[4,2,16]{2,1,0:T(2,128)S(1)} %copy.37), channel_id=1, replica_groups={{0,1,16,17},{2,3,18,19},{4,5,20,21},{6,7,22,23},{8,9,24,25},{10,11,26,2..., dimensions={0} | all-to-all | bytes 1024 | tf_op jit(solution)/shard_map/all_to_all | solution.py:301
  (89 shorter events, 46.0 us)
Async XLA Ops:
  6.0 23.9 %copy-start.8 = (bf16[1024,1152]{1,0:T(8,128)(2,1)}, bf16[1024,1152]{1,0:T(8,128)(2,1)S(1)}, u32[]{:S(2)}) copy-start(bf16[1024,1152]{1,0:T(8,128)(2,1)S(1)} %concatenate.7.pack) | copy-start | bytes 7077892
  6.0 17.9 %collective-permute-start.3 = (bf16[128,1152]{1,0:T(8,128)(2,1)S(1)}, bf16[128,1152]{1,0:T(8,128)(2,1)S(1)}, u32[]{:S(2)}, u32[]{:S(2)}) collective-permute-start(bf16[128,1152]{1,0:T(8,128)(2,1)S(1)} %constant_dynamic-slice_fusion), channel_id=1, source_target_pairs={{0,128},{1,129},{2,130},{3,131},{4,132},{5,133},{6,134},{7,135},{8... | collective-permute-start | bytes 884744 | tf_op jit(solution)/shard_map/ppermute | solution.py:36
  11.1 12.9 %collective-permute-start.4 = (bf16[128,1152]{1,0:T(8,128)(2,1)S(1)}, bf16[128,1152]{1,0:T(8,128)(2,1)S(1)}, u32[]{:S(2)}, u32[]{:S(2)}) collective-permute-start(bf16[128,1152]{1,0:T(8,128)(2,1)S(1)} %constant_dynamic-slice_fusion), channel_id=1, source_target_pairs={{0,192},{1,193},{2,194},{3,195},{4,196},{5,197},{6,198},{7,199},{8... | collective-permute-start | bytes 884744 | tf_op jit(solution)/shard_map/ppermute | solution.py:36
  14.0 15.8 %collective-permute-start.2 = (bf16[128,1152]{1,0:T(8,128)(2,1)S(1)}, bf16[128,1152]{1,0:T(8,128)(2,1)S(1)}, u32[]{:S(2)}, u32[]{:S(2)}) collective-permute-start(bf16[128,1152]{1,0:T(8,128)(2,1)S(1)} %constant_dynamic-slice_fusion), channel_id=1, source_target_pairs={{0,64},{1,65},{2,66},{3,67},{4,68},{5,69},{6,70},{7,71},{8,72},{9,... | collective-permute-start | bytes 884744 | tf_op jit(solution)/shard_map/ppermute | solution.py:36
  29.9 25.1 %collective-permute-start.7 = (bf16[3,128,1152]{2,1,0:T(8,128)(2,1)S(1)}, bf16[3,128,1152]{2,1,0:T(8,128)(2,1)S(1)}, u32[]{:S(2)}, u32[]{:S(2)}) collective-permute-start(bf16[3,128,1152]{2,1,0:T(8,128)(2,1)S(1)} %pad_maximum_fusion.refs_2_), channel_id=1, source_target_pairs={{0,32},{1,33},{2,34},{3,35},{4,36},{5,37},{6,38},{7,39},{8,40},{9,... | collective-permute-start | bytes 2654216 | tf_op jit(solution)/shard_map/ppermute | solution.py:36
  34.5 25.6 %collective-permute-start.8 = (bf16[3,128,1152]{2,1,0:T(8,128)(2,1)S(1)}, bf16[3,128,1152]{2,1,0:T(8,128)(2,1)S(1)}, u32[]{:S(2)}, u32[]{:S(2)}) collective-permute-start(bf16[3,128,1152]{2,1,0:T(8,128)(2,1)S(1)} %pad_maximum_fusion.refs_2_), channel_id=1, source_target_pairs={{0,48},{1,49},{2,50},{3,51},{4,52},{5,53},{6,54},{7,55},{8,56},{9,... | collective-permute-start | bytes 2654216 | tf_op jit(solution)/shard_map/ppermute | solution.py:36
  39.7 31.5 %collective-permute-start.5 = (bf16[3,128,1152]{2,1,0:T(8,128)(2,1)S(1)}, bf16[3,128,1152]{2,1,0:T(8,128)(2,1)S(1)}, u32[]{:S(2)}, u32[]{:S(2)}) collective-permute-start(bf16[3,128,1152]{2,1,0:T(8,128)(2,1)S(1)} %pad_maximum_fusion.refs_2_), channel_id=1, source_target_pairs={{0,14},{1,15},{2,0},{3,1},{4,2},{5,3},{6,4},{7,5},{8,6},{9,7},{10,... | collective-permute-start | bytes 2654216 | tf_op jit(solution)/shard_map/ppermute | solution.py:36
  50.3 34.9 %collective-permute-start = (bf16[512,1152]{1,0:T(8,128)(2,1)S(1)}, bf16[512,1152]{1,0:T(8,128)(2,1)}, u32[]{:S(2)}, u32[]{:S(2)}) collective-permute-start(bf16[512,1152]{1,0:T(8,128)(2,1)S(1)} %constant_dynamic-slice_fusion.1), channel_id=1, source_target_pairs={{0,32},{1,49},{2,34},{3,51},{4,36},{5,53},{6,38},{7,55},{8,40},{9,... | collective-permute-start | bytes 3538952 | tf_op jit(solution)/shard_map/ppermute | solution.py:36
  53.1 21.1 %collective-permute-start.6 = (bf16[3,128,1152]{2,1,0:T(8,128)(2,1)S(1)}, bf16[3,128,1152]{2,1,0:T(8,128)(2,1)S(1)}, u32[]{:S(2)}, u32[]{:S(2)}) collective-permute-start(bf16[3,128,1152]{2,1,0:T(8,128)(2,1)S(1)} %pad_maximum_fusion.refs_2_), channel_id=1, source_target_pairs={{0,2},{1,3},{2,4},{3,5},{4,6},{5,7},{6,8},{7,9},{8,10},{9,11},{10,... | collective-permute-start | bytes 2654216 | tf_op jit(solution)/shard_map/ppermute | solution.py:36
  55.0 22.5 %collective-permute-start.12 = (bf16[3,128,1152]{2,1,0:T(8,128)(2,1)S(1)}, bf16[3,128,1152]{2,1,0:T(8,128)(2,1)S(1)}, u32[]{:S(2)}, u32[]{:S(2)}) collective-permute-start(bf16[3,128,1152]{2,1,0:T(8,128)(2,1)S(1)} %pad_maximum_fusion.refs_2_), channel_id=1, source_target_pairs={{0,1},{1,0},{2,3},{3,2},{4,5},{5,4},{6,7},{7,6},{8,9},{9,8},{10,11... | collective-permute-start | bytes 2654216 | tf_op jit(solution)/shard_map/ppermute | solution.py:36
  60.2 28.8 %collective-permute-start.9 = (bf16[3,128,1152]{2,1,0:T(8,128)(2,1)S(1)}, bf16[3,128,1152]{2,1,0:T(8,128)(2,1)}, u32[]{:S(2)}, u32[]{:S(2)}) collective-permute-start(bf16[3,128,1152]{2,1,0:T(8,128)(2,1)S(1)} %collective-permute-done.7.refs_5_), channel_id=1, source_target_pairs={{0,14},{1,15},{2,0},{3,1},{4,2},{5,3},{6,4},{7,5},{8,6},{9,7},{10,... | collective-permute-start | bytes 2654216 | tf_op jit(solution)/shard_map/ppermute | solution.py:36
  71.1 24.9 %collective-permute-start.10 = (bf16[3,128,1152]{2,1,0:T(8,128)(2,1)S(1)}, bf16[3,128,1152]{2,1,0:T(8,128)(2,1)}, u32[]{:S(2)}, u32[]{:S(2)}) collective-permute-start(bf16[3,128,1152]{2,1,0:T(8,128)(2,1)S(1)} %collective-permute-done.7.refs_5_), channel_id=1, source_target_pairs={{0,2},{1,3},{2,4},{3,5},{4,6},{5,7},{6,8},{7,9},{8,10},{9,11},{10,... | collective-permute-start | bytes 2654216 | tf_op jit(solution)/shard_map/ppermute | solution.py:36
  74.2 25.1 %collective-permute-start.11 = (bf16[3,128,1152]{2,1,0:T(8,128)(2,1)S(1)}, bf16[3,128,1152]{2,1,0:T(8,128)(2,1)}, u32[]{:S(2)}, u32[]{:S(2)}) collective-permute-start(bf16[3,128,1152]{2,1,0:T(8,128)(2,1)S(1)} %collective-permute-done.8.refs_6_), channel_id=1, source_target_pairs={{0,32},{1,33},{2,34},{3,35},{4,36},{5,37},{6,38},{7,39},{8,40},{9,... | collective-permute-start | bytes 2654216 | tf_op jit(solution)/shard_map/ppermute | solution.py:36
  77.6 28.0 %copy-start.9 = (bf16[3,128,1152]{2,1,0:T(8,128)(2,1)}, bf16[3,128,1152]{2,1,0:T(8,128)(2,1)S(1)}, u32[]{:S(2)}) copy-start(bf16[3,128,1152]{2,1,0:T(8,128)(2,1)S(1)} %collective-permute-done.12.refs_10_) | copy-start | bytes 2654212
  77.6 23.6 %collective-permute-start.13 = (bf16[3,128,1152]{2,1,0:T(8,128)(2,1)S(1)}, bf16[3,128,1152]{2,1,0:T(8,128)(2,1)S(1)}, u32[]{:S(2)}, u32[]{:S(2)}) collective-permute-start(bf16[3,128,1152]{2,1,0:T(8,128)(2,1)S(1)} %collective-permute-done.5.refs_3_), channel_id=1, source_target_pairs={{0,1},{1,0},{2,3},{3,2},{4,5},{5,4},{6,7},{7,6},{8,9},{9,8},{10,11... | collective-permute-start | bytes 2654216 | tf_op jit(solution)/shard_map/ppermute | solution.py:36
  85.2 18.4 %collective-permute-start.14 = (bf16[3,128,1152]{2,1,0:T(8,128)(2,1)S(1)}, bf16[3,128,1152]{2,1,0:T(8,128)(2,1)S(1)}, u32[]{:S(2)}, u32[]{:S(2)}) collective-permute-start(bf16[3,128,1152]{2,1,0:T(8,128)(2,1)S(1)} %collective-permute-done.6.refs_4_), channel_id=1, source_target_pairs={{0,1},{1,0},{2,3},{3,2},{4,5},{5,4},{6,7},{7,6},{8,9},{9,8},{10,11... | collective-permute-start | bytes 2654216 | tf_op jit(solution)/shard_map/ppermute | solution.py:36
  88.9 16.6 %collective-permute-start.15 = (bf16[3,128,1152]{2,1,0:T(8,128)(2,1)S(1)}, bf16[3,128,1152]{2,1,0:T(8,128)(2,1)S(1)}, u32[]{:S(2)}, u32[]{:S(2)}) collective-permute-start(bf16[3,128,1152]{2,1,0:T(8,128)(2,1)S(1)} %collective-permute-done.7.refs_5_), channel_id=1, source_target_pairs={{0,1},{1,0},{2,3},{3,2},{4,5},{5,4},{6,7},{7,6},{8,9},{9,8},{10,11... | collective-permute-start | bytes 2654216 | tf_op jit(solution)/shard_map/ppermute | solution.py:36
  96.0 49.8 %collective-permute-start.1 = (bf16[512,1152]{1,0:T(8,128)(2,1)}, bf16[512,1152]{1,0:T(8,128)(2,1)}, u32[]{:S(2)}, u32[]{:S(2)}) collective-permute-start(bf16[512,1152]{1,0:T(8,128)(2,1)} %collective-permute-done.refs_0_), channel_id=1, source_target_pairs={{0,1},{1,0},{2,3},{3,2},{4,5},{5,4},{6,7},{7,6},{8,9},{9,8},{10,11... | collective-permute-start | bytes 3538952 | tf_op jit(solution)/shard_map/ppermute | solution.py:36
  99.3 46.5 %collective-permute-start.16 = (bf16[3,128,1152]{2,1,0:T(8,128)(2,1)S(1)}, bf16[3,128,1152]{2,1,0:T(8,128)(2,1)}, u32[]{:S(2)}, u32[]{:S(2)}) collective-permute-start(bf16[3,128,1152]{2,1,0:T(8,128)(2,1)S(1)} %collective-permute-done.8.refs_6_), channel_id=1, source_target_pairs={{0,1},{1,0},{2,3},{3,2},{4,5},{5,4},{6,7},{7,6},{8,9},{9,8},{10,11... | collective-permute-start | bytes 2654216 | tf_op jit(solution)/shard_map/ppermute | solution.py:36
  101.2 4.4 %copy-start.10 = (bf16[3,128,1152]{2,1,0:T(8,128)(2,1)}, bf16[3,128,1152]{2,1,0:T(8,128)(2,1)S(1)}, u32[]{:S(2)}) copy-start(bf16[3,128,1152]{2,1,0:T(8,128)(2,1)S(1)} %collective-permute-done.13.refs_11_) | copy-start | bytes 2654212
  101.2 44.6 %collective-permute-start.17 = (bf16[3,128,1152]{2,1,0:T(8,128)(2,1)}, bf16[3,128,1152]{2,1,0:T(8,128)(2,1)}, u32[]{:S(2)}, u32[]{:S(2)}) collective-permute-start(bf16[3,128,1152]{2,1,0:T(8,128)(2,1)} %collective-permute-done.9.refs_7_), channel_id=1, source_target_pairs={{0,1},{1,0},{2,3},{3,2},{4,5},{5,4},{6,7},{7,6},{8,9},{9,8},{10,11... | collective-permute-start | bytes 2654216 | tf_op jit(solution)/shard_map/ppermute | solution.py:36
  103.6 2.0 copy-start.11
  103.6 42.2 %collective-permute-start.18 = (bf16[3,128,1152]{2,1,0:T(8,128)(2,1)}, bf16[3,128,1152]{2,1,0:T(8,128)(2,1)}, u32[]{:S(2)}, u32[]{:S(2)}) collective-permute-start(bf16[3,128,1152]{2,1,0:T(8,128)(2,1)} %collective-permute-done.10.refs_8_), channel_id=1, source_target_pairs={{0,1},{1,0},{2,3},{3,2},{4,5},{5,4},{6,7},{7,6},{8,9},{9,8},{10,11... | collective-permute-start | bytes 2654216 | tf_op jit(solution)/shard_map/ppermute | solution.py:36
  106.5 39.3 %collective-permute-start.19 = (bf16[3,128,1152]{2,1,0:T(8,128)(2,1)}, bf16[3,128,1152]{2,1,0:T(8,128)(2,1)}, u32[]{:S(2)}, u32[]{:S(2)}) collective-permute-start(bf16[3,128,1152]{2,1,0:T(8,128)(2,1)} %collective-permute-done.11.refs_9_), channel_id=1, source_target_pairs={{0,1},{1,0},{2,3},{3,2},{4,5},{5,4},{6,7},{7,6},{8,9},{9,8},{10,11... | collective-permute-start | bytes 2654216 | tf_op jit(solution)/shard_map/ppermute | solution.py:36
  119.0 24.8 %all-to-all-start = ((bf16[16,128,64]{1,2,0:T(8,128)(2,1)}), bf16[16,128,64]{1,2,0:T(8,128)(2,1)}, u32[]{:S(2)}, u32[]{:S(2)}) async-start(bf16[16,128,64]{1,2,0:T(8,128)(2,1)} %copy.29), calls=%async_computation | async-start | bytes 524288 | tf_op jit(solution)/shard_map/all_to_all | solution.py:227
  145.8 1.2 copy-start.1
  157.1 13.6 %copy-start.4 = (f32[8,128,128]{2,1,0:T(8,128)}, f32[8,128,128]{2,1,0:T(8,128)S(1)}, u32[]{:S(2)}) copy-start(f32[8,128,128]{2,1,0:T(8,128)S(1)} %get-tuple-element.13.left) | copy-start | bytes 1572868
  157.1 12.3 %collective-permute-start.20 = (bf16[128,1024]{1,0:T(8,128)(2,1)S(1)}, bf16[128,1024]{1,0:T(8,128)(2,1)S(1)}, u32[]{:S(2)}, u32[]{:S(2)}) collective-permute-start(bf16[128,1024]{1,0:T(8,128)(2,1)S(1)} %get-tuple-element.10), channel_id=1, source_target_pairs={{0,448},{1,449},{2,450},{3,451},{4,452},{5,453},{6,454},{7,455},{8... | collective-permute-start | bytes 786440 | tf_op jit(solution)/shard_map/ppermute | solution.py:36
  171.4 26.0 %collective-permute-start.21 = (bf16[128,1024]{1,0:T(8,128)(2,1)}, bf16[128,1024]{1,0:T(8,128)(2,1)}, u32[]{:S(2)}, u32[]{:S(2)}) collective-permute-start(bf16[128,1024]{1,0:T(8,128)(2,1)} %get-tuple-element.11), channel_id=1, source_target_pairs={{256,192},{257,193},{258,194},{259,195},{260,196},{261,197},{262,1... | collective-permute-start | bytes 786440 | tf_op jit(solution)/shard_map/ppermute | solution.py:36
  199.6 12.5 %copy-start.7 = (bf16[8,64,64]{2,1,0:T(8,128)(2,1)S(1)}, bf16[8,64,64]{2,1,0:T(8,128)(2,1)}, u32[]{:S(2)}) copy-start(bf16[8,64,64]{2,1,0:T(8,128)(2,1)} %copy-done.6) | copy-start | bytes 196612
  224.4 15.4 %all-to-all-start.3 = ((bf16[4,16,4096]{2,1,0:T(8,128)(2,1)}), bf16[4,16,4096]{2,1,0:T(8,128)(2,1)S(1)}, u32[]{:S(2)}, u32[]{:S(2)}) async-start(bf16[4,16,4096]{2,1,0:T(8,128)(2,1)} %broadcast_in_dim.19), calls=%async_computation.3 | async-start | bytes 1048576 | tf_op jit(solution)/shard_map/all_to_all | solution.py:237
  240.6 11.1 %all-to-all-start.2 = ((bf16[8,2,4096]{2,1,0:T(2,128)(2,1)}), bf16[8,2,4096]{2,1,0:T(2,128)(2,1)S(1)}, u32[]{:S(2)}, u32[]{:S(2)}) async-start(bf16[8,2,4096]{2,1,0:T(2,128)(2,1)} %broadcast_in_dim.17), calls=%async_computation.2 | async-start | bytes 262144 | tf_op jit(solution)/shard_map/all_to_all | solution.py:284
  (6 other events, 5.7 us)

commit v2 on v1

v2 whole, which is shorter than its diff:
```python
import functools

import jax
import jax.numpy as jnp
from jax import lax
from jax.experimental import pallas as pl
from jax.experimental.pallas import tpu as pltpu
from jax.sharding import PartitionSpec as P

AXES = ("section", "dp")
TOK = 128
STAGE = 8
D = 1024
RANK = 64
PACK = D + 2 * RANK
PIECE = PACK // 8


def flat(x, y, z, c):
    return (y % 8 * 2 + x % 2) * 32 + ((x % 4 // 2) * 8 + z % 8) * 2 + c


def pairs(target):
    out = []
    for x in range(4):
        for y in range(8):
            for z in range(8):
                for c in range(2):
                    to = target(x, y, z, c)
                    if to is not None:
                        out.append((flat(x, y, z, c), flat(*to)))
    return out


def move(value, target):
    return lax.ppermute(value, AXES, pairs(target))


def swap_core(value):
    return move(value, lambda x, y, z, c: (x, y, z, 1 - c))


def gather_rows(pack, core, quarter):
    piece = lax.dynamic_slice_in_dim(pack, (core * 4 + quarter) * PIECE, PIECE, 0)
    rows = [
        move(piece, lambda x, y, z, c, r=r: (x, y // 4 * 4 + (y + r) % 4, z, c)) for r in (1, 2, 3)
    ]
    half = lax.dynamic_slice_in_dim(pack, core * (PACK // 2), PACK // 2, 0)
    beside = move(half, lambda x, y, z, c: (x + 1 if c == 0 else x - 1, y, z, c))
    return rows, beside


def along_z(value):
    return move(value, lambda x, y, z, c: (x, y, z + 1 - 2 * (c ^ (x // 2)), c))


def along_x(value):
    return move(value, lambda x, y, z, c: (x ^ 1 if c == 0 else 3 - x, y, z, c))


def assemble(place, pieces, halves, whole, layers, sems):
    row, col, core = (place[k] for k in range(3))
    copies = []

    def put(source, slot, rows):
        target = layers.at[slot] if rows is None else layers.at[slot, rows]
        copies.append(pltpu.make_async_copy(source, target, sems.at[len(copies)]))

    if whole is not None:
        put(whole, row * 2 + col, None)
    for half, ref in halves:
        put(ref, row * 2 + 1 - col, pl.ds(pl.multiple_of(half * (PACK // 2), PACK // 2), PACK // 2))
    for distance in (1, 2, 3):
        source_row = (row - distance) & 3
        for source, other_col, other_core, quarter in pieces:
            slot = source_row * 2 + (1 - col if other_col else col)
            half = 1 - core if other_core else core
            start = pl.multiple_of((half * 4 + (quarter & 3)) * PIECE, PIECE)
            put(source.at[distance - 1], slot, pl.ds(start, PIECE))
    for copy in copies:
        copy.start()
    for copy in copies:
        copy.wait()


def early_kernel(place, pack, beside, own, own_other, up, up_more, side, side_more, layers, sems):
    core, quarter, way = (place[k] for k in (2, 3, 4))
    pieces = [
        (own, 0, 0, quarter),
        (own_other, 0, 1, quarter),
        (up, 0, 0, quarter - way),
        (up_more, 0, 1, quarter - way),
        (side, 1, 0, quarter + 2 * core),
        (side_more, 1, 1, quarter + 2 * core),
    ]
    assemble(place, pieces, ((core, beside),), pack, layers, sems)


def late_kernel(
    place, beside, up, up_more, side, side_more, turn, turn_more, turn_other, turn_more_other,
    two, two_more, before, layers, sems
):
    core, quarter, way = (place[k] for k in (2, 3, 4))
    pieces = [
        (up, 0, 1, quarter + way),
        (up_more, 0, 0, quarter + way),
        (side, 1, 1, quarter + 2 * (1 - core)),
        (side_more, 1, 0, quarter + 2 * (1 - core)),
        (turn, 1, 0, quarter - way),
        (turn_more, 1, 1, quarter - way),
        (turn_other, 1, 1, quarter + way),
        (turn_more_other, 1, 0, quarter + way),
        (two, 0, 0, quarter + 2),
        (two_more, 0, 1, quarter + 2),
    ]
    assemble(place, pieces, ((1 - core, beside),), None, layers, sems)


CHUNK = 256


def forward_one(slot, current, layers, slope, left):
    hidden = current[...]
    left[slot] = lax.dot_general(
        layers[slot, D:], hidden, (((1,), (1,)), ((), ())), preferred_element_type=jnp.float32
    )
    for start in range(0, D, CHUNK):
        cols = slice(start, start + CHUNK)
        preact = jnp.dot(hidden, layers[slot, :D, cols], preferred_element_type=jnp.float32)
        sig = jax.nn.sigmoid(preact)
        slope[slot, :, cols] = sig * (1.0 + preact * (1.0 - sig))
        current[:, cols] = (hidden[:, cols].astype(jnp.float32) + preact * sig).astype(jnp.bfloat16)


def backward_one(slot, current, layers, slope, left, factor):
    upstream = current[...].astype(jnp.float32)
    grad = (upstream * slope[slot]).astype(jnp.bfloat16)
    nt = (((1,), (1,)), ((), ()))
    right = lax.dot_general(grad, layers[slot, D:], nt, preferred_element_type=jnp.float32)
    product = jnp.dot(
        left[slot],
        right,
        precision=lax.Precision.HIGHEST,
        preferred_element_type=jnp.float32,
    )
    factor[slot] = product[:RANK, RANK:].astype(jnp.bfloat16)
    for start in range(0, D, CHUNK):
        cols = slice(start, start + CHUNK)
        carried = lax.dot_general(
            grad, layers[slot, cols], nt, preferred_element_type=jnp.float32
        )
        current[:, cols] = (upstream[:, cols] + carried).astype(jnp.bfloat16)


def rows_of(arrived):
    return arrived[...].reshape(D, TOK).T


def first_kernel(place, arrived, layers, current, slope_out, left, slope, sems):
    def keep(slot):
        return pltpu.make_async_copy(slope.at[slot], slope_out.at[slot], sems.at[slot])

    @pl.when(place[5] == 0)
    def _():
        current[...] = rows_of(arrived)

        def body(slot, carry):
            forward_one(slot, current, layers, slope, left)
            keep(slot).start()
            return carry

        lax.fori_loop(0, STAGE, body, 0)
        for slot in range(STAGE):
            keep(slot).wait()


def middle_kernel(place, hidden, arrived, layers, upstream, factor, current, slope, left):
    @pl.when(place[5] == 1)
    def _():
        current[...] = hidden[...]
        upstream[...] = rows_of(arrived)

        def ahead(slot, carry):
            forward_one(slot, current, layers, slope, left)
            return carry

        lax.fori_loop(0, STAGE, ahead, 0)

        def back(step, carry):
            backward_one(STAGE - 1 - step, upstream, layers, slope, left, factor)
            return carry

        lax.fori_loop(0, STAGE, back, 0)


def last_kernel(place, upstream, slope_in, left, late, layers_in, factor, current, slope, layers, sems):
    def fetch(slot):
        return (
            pltpu.make_async_copy(slope_in.at[slot], slope.at[slot], sems.at[0, slot]),
            pltpu.make_async_copy(layers_in.at[slot], layers.at[slot], sems.at[1, slot]),
        )

    @pl.when(place[5] == 0)
    def _():
        for slot in reversed(range(STAGE)):
            for copy in fetch(slot):
                copy.start()
        current[...] = upstream[...]

        def back(step, carry):
            slot = STAGE - 1 - step
            for copy in fetch(slot):
                copy.wait()
            backward_one(slot, current, layers, slope, left, factor)
            return carry

        lax.fori_loop(0, STAGE, back, 0)

    @pl.when(place[5] == 1)
    def _():
        factor[...] = late[...]


VMEM = pl.BlockSpec(memory_space=pltpu.VMEM)
SMEM = pl.BlockSpec(memory_space=pltpu.SMEM)
ANY = pl.BlockSpec(memory_space=pl.ANY)
HBM = pl.BlockSpec(memory_space=pltpu.HBM)
PARAMS = pltpu.CompilerParams(vmem_limit_bytes=10 * 1024 * 1024)
LARGE = pltpu.CompilerParams(vmem_limit_bytes=30 * 1024 * 1024)
TOKENS = jax.ShapeDtypeStruct((TOK, D), jnp.bfloat16)
SLOPE = jax.ShapeDtypeStruct((STAGE, TOK, D), jnp.float32)
LEFT = jax.ShapeDtypeStruct((STAGE, 2 * RANK, TOK), jnp.float32)
FACTOR = jax.ShapeDtypeStruct((STAGE, RANK, RANK), jnp.bfloat16)
LAYERS = jax.ShapeDtypeStruct((STAGE, PACK, D), jnp.bfloat16)


def scratch(shape):
    return pltpu.VMEM(shape.shape, shape.dtype)


def cost(passes):
    return pl.CostEstimate(
        flops=2 * passes * STAGE * TOK * D * PACK,
        bytes_accessed=STAGE * D * PACK * 2,
        transcendentals=STAGE * TOK * D,
    )


def on_device(inputs, cotangent, weights, proj_in, proj_out, query_factors):
    section, dp = lax.axis_index("section"), lax.axis_index("dp")
    y, col = section // 2, section % 2
    x_hi, z, core = dp // 16, dp // 2 % 8, dp % 2
    stage = y // 4
    quarter = (z + 2 * x_hi) % 4
    way = 1 - 2 * (core ^ x_hi)
    place = jnp.stack([y % 4, col, core, quarter, way, stage]).astype(jnp.int32)

    pack = jnp.concatenate([weights[0], proj_in[0].T, proj_out[0].T])
    rows, beside = gather_rows(pack, core, quarter)

    ahead, seeds = (
        value.reshape(2, 4, TOK, -1).transpose(0, 1, 3, 2).reshape(STAGE, -1, TOK)
        for value in (inputs, cotangent)
    )
    order = [ahead] + [seeds[k : k + 2] for k in (6, 4, 2, 0)]
    rows[0], order = lax.optimization_barrier((rows[0], jnp.concatenate(order)))
    arrived = lax.all_to_all(order, "section", 0, 0, tiled=True)

    own = jnp.stack(rows)
    up, side = along_z(own), along_x(own)
    own_other = swap_core(own)
    own_other, beside = lax.optimization_barrier((own_other, beside))
    up_more, side_more = along_z(own_other), along_x(own_other)
    turn, two = along_x(up), along_z(up)
    turn, two, up_more, side_more, arrived = lax.optimization_barrier(
        (turn, two, up_more, side_more, arrived)
    )
    turn_more, two_more = along_x(up_more), along_z(up_more)
    layers = pl.pallas_call(
        early_kernel,
        out_shape=LAYERS,
        in_specs=[SMEM] + [ANY] * 8,
        out_specs=VMEM,
        scratch_shapes=[pltpu.SemaphoreType.DMA((20,))],
        compiler_params=PARAMS,
        name="place_early_pieces",
    )(place, pack, beside, own, own_other, up, up_more, side, side_more)
    swapped = [swap_core(value) for value in (beside, up, up_more, side, side_more)]
    queries = query_factors
    layers, queries = lax.optimization_barrier((layers, queries))
    queries = jnp.concatenate([queries, swap_core(queries)])
    queries = jnp.concatenate([queries, move(queries, lambda x, y, z, c: (x ^ 2, y, z, c))])
    layers = pl.pallas_call(
        late_kernel,
        out_shape=LAYERS,
        in_specs=[SMEM] + [ANY] * 11 + [VMEM],
        out_specs=VMEM,
        scratch_shapes=[pltpu.SemaphoreType.DMA((31,))],
        input_output_aliases={12: 0},
        compiler_params=PARAMS,
        name="place_late_pieces",
    )(
        place, *swapped, turn, turn_more, swap_core(turn), swap_core(turn_more), two, two_more, layers
    )

    hidden, slope, left = pl.pallas_call(
        first_kernel,
        out_shape=(TOKENS, SLOPE, LEFT),
        in_specs=[SMEM, VMEM, VMEM],
        out_specs=(VMEM, HBM, VMEM),
        scratch_shapes=[scratch(SLOPE), pltpu.SemaphoreType.DMA((STAGE,))],
        compiler_params=PARAMS,
        cost_estimate=cost(1),
        name="forward_first_stage",
    )(place, arrived, layers)
    hidden = move(hidden, lambda x, y, z, c: (x, 7 - y, z, c) if y < 4 else None)
    upstream, factor_late = pl.pallas_call(
        middle_kernel,
        out_shape=(TOKENS, FACTOR),
        in_specs=[SMEM, VMEM, VMEM, VMEM],
        out_specs=(VMEM, VMEM),
        scratch_shapes=[scratch(TOKENS), scratch(SLOPE), scratch(LEFT)],
        compiler_params=PARAMS,
        cost_estimate=cost(2),
        name="second_stage",
    )(place, hidden, arrived, layers)
    upstream = move(upstream, lambda x, y, z, c: (x, 7 - y, z, c) if y > 3 else None)
    upstream, queries = lax.optimization_barrier((upstream, queries))
    factor = pl.pallas_call(
        last_kernel,
        out_shape=FACTOR,
        in_specs=[SMEM, VMEM, HBM, VMEM, VMEM, HBM],
        out_specs=VMEM,
        scratch_shapes=[
            scratch(TOKENS),
            scratch(SLOPE),
            scratch(LAYERS),
            pltpu.SemaphoreType.DMA((2, STAGE)),
        ],
        compiler_params=LARGE,
        cost_estimate=cost(1),
        name="backward_first_stage",
    )(place, upstream, slope, left, factor_late, pltpu.with_memory_space_constraint(layers, pltpu.HBM))

    factor = factor.reshape(STAGE, -1)
    groups = [list(range(8)), list(range(8, 16))]
    parts = lax.all_to_all(factor, "section", 0, 0, tiled=True, axis_index_groups=groups)
    low, high = parts.reshape(2, 4, -1).astype(jnp.float32).sum(1)
    along = [[(h * 8 + k) * 2 + c for k in range(8)] for h in range(2) for c in range(2)]
    sums = jnp.stack([jnp.where(stage == 0, low, high), jnp.where(stage == 0, high, low)])
    sums = sums.astype(jnp.bfloat16)
    sums = lax.all_to_all(
        jnp.broadcast_to(sums[None], (8,) + sums.shape),
        "dp",
        0,
        0,
        tiled=True,
        axis_index_groups=along,
    ).reshape(16, -1)
    table = lax.dot_general(
        sums, queries.reshape(-1, sums.shape[1]), (((1,), (1,)), ((), ())),
        preferred_element_type=jnp.float32,
    ).reshape(16, 2, 2, -1)
    table = jnp.where(x_hi == 0, table, table[:, ::-1])
    table = jnp.where(core == 0, table, table[:, :, ::-1]).reshape(8, 2, -1)

    outgoing = lax.dynamic_update_slice_in_dim(
        jnp.zeros((16,) + table.shape[1:], jnp.float32), table, x_hi * 8, 0
    )
    across = [[(h * 8 + k) * 2 + c for h in range(2) for c in range(2)] for k in range(8)]
    scores = lax.all_to_all(outgoing, "section", 0, 0, tiled=True).sum(0)
    scores = scores.reshape(2, 4, -1).transpose(1, 0, 2)
    scores = lax.all_to_all(scores, "dp", 0, 0, tiled=True, axis_index_groups=across)
    return scores.reshape(2, 4, -1).sum(0)


def solution(mesh):
    placed = (
        P("dp", None, "section"),
        P("dp", None, "section"),
        P("section", None, None),
        P("section", None, None),
        P("section", None, None),
        P("section", "dp", None),
    )
    return jax.shard_map(
        on_device, mesh=mesh, in_specs=placed, out_specs=P("section", "dp"), check_vma=False
    )
```

time: 276 us -> 227 us (0.82)
  local copies, waits for them, and re-layouts: 30.2 us -> 4.86 us
  waiting for transfers between devices: 80.6 us -> 68.3 us
  starting transfers between devices: 107 us -> 95.8 us
  blocking collectives: 29.2 us -> 22.8 us
  Pallas kernels: 22.8 us -> 26.6 us
    unnamed x34 -> x24, local copies, waits for them, and re-layouts: 12.7 us -> 1.65 us
    all_to_all x2, starting transfers between devices: 20 us -> 11 us  [the longest x1 6.67 us: on_device(): arrived = lax.all_to_all(order, 'section', 0, 0, tiled=True)]
    all_to_all x1 -> x0, blocking collectives: 8.93 us -> none  [on_device(): lax.all_to_all(factor, 'section', 0, 0, tiled=True, axis_index_groups=gro...]
    all_to_all x2, waiting for transfers between devices: 18.7 us -> 10.1 us  [the longest x1 5.86 us: on_device(): lax.all_to_all(factor, 'section', 0, 0, tiled=True, axis_index_groups=gro...]
    pallas_call x1 -> x3, Pallas kernels: 12.4 us -> 19.3 us  [the longest x1 11.1 us: on_device(): pl.pallas_call(last_kernel, out_shape=FACTOR, in_specs=[SMEM, VMEM, HBM,...]
    concatenate x2 -> x1, local copies, waits for them, and re-layouts: 4.55 us -> 0.01 us  [on_device(): rows[0], order = lax.optimization_barrier((rows[0], jnp.concatenate(order)))]
    ppermute x22 -> x24, waiting for transfers between devices: 54.3 us -> 50.1 us  [move(): return lax.ppermute(value, AXES, pairs(target))]
    reshape x2 -> x4, local copies, waits for them, and re-layouts: 3.28 us -> 0.2 us  [the longest x1 0.1 us: on_device(): table = jnp.where(core == 0, table, table[:, :, ::-1]).reshape(8, 2, -1)]
  transfers between devices with their start and end apart: 25 -> 27, of which waited for: 10 -> 9; matrix products, arithmetic and copies ran while one was open for 5% -> 1% of each run, Pallas kernels for 0% -> 7%
where the time goes in v2:
time: 227 us; the launch traced here: 226 us
  starting transfers between devices  95.8 us (42%)
  waiting for transfers between devices  68.3 us (30%)
  Pallas kernels  26.6 us (12%)
  blocking collectives  22.8 us (10%)
  other arithmetic  6.11 us (3%)
  local copies, waits for them, and re-layouts  4.86 us (2%)
    ppermute x24, starting transfers between devices, move(): return lax.ppermute(value, AXES, pairs(target))  80.6 us
    ppermute x24, waiting for transfers between devices, move(): return lax.ppermute(value, AXES, pairs(target))  50.1 us
    all_to_all x1, blocking collectives, on_device(): lax.all_to_all(scores, 'dp', 0, 0, tiled=True, axis_index_groups=across)  13 us
    pallas_call x1, Pallas kernels, on_device(): pl.pallas_call(last_kernel, out_shape=FACTOR, in_specs=[SMEM, VMEM, HBM,...  11.1 us
    all_to_all x1, blocking collectives, on_device(): scores = lax.all_to_all(outgoing, 'section', 0, 0, tiled=True).sum(0)  9.88 us
    all_to_all x1, waiting for transfers between devices, on_device(): lax.all_to_all(jnp.broadcast_to(sums[None], (8,) + sums.shape), 'dp', 0,...  8.03 us
    all_to_all x1, starting transfers between devices, on_device(): arrived = lax.all_to_all(order, 'section', 0, 0, tiled=True)  6.67 us
    pallas_call x1, Pallas kernels, on_device(): pl.pallas_call(first_kernel, out_shape=(TOKENS, SLOPE, LEFT), in_specs=[S...  6.35 us
  transfers between devices with their start and end apart: 27, of which 9 were waited for; matrix products, arithmetic and copies ran while one was open for 1% of the time, Pallas kernels for 7%

profile of v2, /device:TPU:1, one launch (start us, length us, event | category | flops | bytes accessed | tf_op | source)
XLA Modules:
  0.0 225.9 jit_solution(2011651670825728786)
XLA Ops:
  2.7 6.0 %collective-permute-start.2 = (bf16[144,1024]{1,0:T(8,128)(2,1)}, bf16[144,1024]{1,0:T(8,128)(2,1)S(1)}, u32[]{:S(2)}, u32[]{:S(2)}) collective-permute-start(bf16[144,1024]{1,0:T(8,128)(2,1)} %constant_dynamic-slice_fusion.1), channel_id=1, source_target_pairs={{0,192},{1,193},{2,194},{3,195},{4,196},{5,197},{6,198},{7,199},{8... | collective-permute-start | bytes 884744 | tf_op jit(solution)/shard_map/ppermute | solution.py:36
  10.7 2.3 %collective-permute-start = (bf16[144,1024]{1,0:T(8,128)(2,1)}, bf16[144,1024]{1,0:T(8,128)(2,1)S(1)}, u32[]{:S(2)}, u32[]{:S(2)}) collective-permute-start(bf16[144,1024]{1,0:T(8,128)(2,1)} %constant_dynamic-slice_fusion.1), channel_id=1, source_target_pairs={{0,64},{1,65},{2,66},{3,67},{4,68},{5,69},{6,70},{7,71},{8,72},{9,... | collective-permute-start | bytes 884744 | tf_op jit(solution)/shard_map/ppermute | solution.py:36
  13.2 4.4 %collective-permute-start.7 = (bf16[576,1024]{1,0:T(8,128)(2,1)S(1)}, bf16[576,1024]{1,0:T(8,128)(2,1)}, u32[]{:S(2)}, u32[]{:S(2)}) collective-permute-start(bf16[576,1024]{1,0:T(8,128)(2,1)S(1)} %constant_dynamic-slice_fusion), channel_id=1, source_target_pairs={{0,32},{1,49},{2,34},{3,51},{4,36},{5,53},{6,38},{7,55},{8,40},{9,... | collective-permute-start | bytes 3538952 | tf_op jit(solution)/shard_map/ppermute | solution.py:36
  17.7 9.2 %collective-permute-done = bf16[144,1024]{1,0:T(8,128)(2,1)S(1)} collective-permute-done((bf16[144,1024]{1,0:T(8,128)(2,1)}, bf16[144,1024]{1,0:T(8,128)(2,1)S(1)}, u32[]{:S(2)}, u32[]{:S(2)}) %collective-permute-start) | collective-permute-done | bytes 294944 | tf_op jit(solution)/shard_map/ppermute | solution.py:36
  26.9 6.7 %collective-permute-done.1 = bf16[144,1024]{1,0:T(8,128)(2,1)S(1)} collective-permute-done((bf16[144,1024]{1,0:T(8,128)(2,1)}, bf16[144,1024]{1,0:T(8,128)(2,1)S(1)}, u32[]{:S(2)}, u32[]{:S(2)}) %collective-permute-start.1) | collective-permute-done | bytes 294944 | tf_op jit(solution)/shard_map/ppermute | solution.py:36
  35.6 10.7 %collective-permute-start.3 = (bf16[3,144,1024]{2,1,0:T(8,128)(2,1)S(1)}, bf16[3,144,1024]{2,1,0:T(8,128)(2,1)}, u32[]{:S(2)}, u32[]{:S(2)}) collective-permute-start(bf16[3,144,1024]{2,1,0:T(8,128)(2,1)S(1)} %pad_maximum_fusion.1.own), channel_id=1, source_target_pairs={{0,2},{1,15},{2,4},{3,1},{4,6},{5,3},{6,8},{7,5},{8,10},{9,7},{10,... | collective-permute-start | bytes 2654216 | tf_op jit(solution)/shard_map/ppermute | solution.py:36
  48.2 6.1 %collective-permute-start.13 = (bf16[3,144,1024]{2,1,0:T(8,128)(2,1)S(1)}, bf16[3,144,1024]{2,1,0:T(8,128)(2,1)}, u32[]{:S(2)}, u32[]{:S(2)}) collective-permute-start(bf16[3,144,1024]{2,1,0:T(8,128)(2,1)S(1)} %pad_maximum_fusion.1.own), channel_id=1, source_target_pairs={{0,32},{1,49},{2,34},{3,51},{4,36},{5,53},{6,38},{7,55},{8,40},{9,... | collective-permute-start | bytes 2654216 | tf_op jit(solution)/shard_map/ppermute | solution.py:36
  56.2 4.8 %collective-permute-start.4 = (bf16[3,144,1024]{2,1,0:T(8,128)(2,1)}, bf16[3,144,1024]{2,1,0:T(8,128)(2,1)}, u32[]{:S(2)}, u32[]{:S(2)}) collective-permute-start(bf16[3,144,1024]{2,1,0:T(8,128)(2,1)} %collective-permute-done.3.up), channel_id=1, source_target_pairs={{0,32},{1,49},{2,34},{3,51},{4,36},{5,53},{6,38},{7,55},{8,40},{9,... | collective-permute-start | bytes 2654216 | tf_op jit(solution)/shard_map/ppermute | solution.py:36
  61.0 3.7 %collective-permute-start.5 = (bf16[3,144,1024]{2,1,0:T(8,128)(2,1)}, bf16[3,144,1024]{2,1,0:T(8,128)(2,1)}, u32[]{:S(2)}, u32[]{:S(2)}) collective-permute-start(bf16[3,144,1024]{2,1,0:T(8,128)(2,1)} %collective-permute-done.3.up), channel_id=1, source_target_pairs={{0,2},{1,15},{2,4},{3,1},{4,6},{5,3},{6,8},{7,5},{8,10},{9,7},{10,... | collective-permute-start | bytes 2654216 | tf_op jit(solution)/shard_map/ppermute | solution.py:36
  64.7 2.2 collective-permute-start.8
  68.8 6.7 %all-to-all-start = ((bf16[16,64,128]{2,1,0:T(8,128)(2,1)}), bf16[16,64,128]{2,1,0:T(8,128)(2,1)}, u32[]{:S(2)}, u32[]{:S(2)}) async-start(bf16[16,64,128]{2,1,0:T(8,128)(2,1)} %copy-done.2), calls=%async_computation | async-start | bytes 524288 | tf_op jit(solution)/shard_map/all_to_all | solution.py:267
  75.5 2.5 %collective-permute-start.10 = (bf16[576,1024]{1,0:T(8,128)(2,1)}, bf16[576,1024]{1,0:T(8,128)(2,1)}, u32[]{:S(2)}, u32[]{:S(2)}) collective-permute-start(bf16[576,1024]{1,0:T(8,128)(2,1)} %collective-permute-done.7.beside), channel_id=1, source_target_pairs={{0,1},{1,0},{2,3},{3,2},{4,5},{5,4},{6,7},{7,6},{8,9},{9,8},{10,11... | collective-permute-start | bytes 3538952 | tf_op jit(solution)/shard_map/ppermute | solution.py:36
  80.0 2.4 %collective-permute-start.14 = (bf16[3,144,1024]{2,1,0:T(8,128)(2,1)}, bf16[3,144,1024]{2,1,0:T(8,128)(2,1)}, u32[]{:S(2)}, u32[]{:S(2)}) collective-permute-start(bf16[3,144,1024]{2,1,0:T(8,128)(2,1)} %collective-permute-done.13.side), channel_id=1, source_target_pairs={{0,1},{1,0},{2,3},{3,2},{4,5},{5,4},{6,7},{7,6},{8,9},{9,8},{10,11... | collective-permute-start | bytes 2654216 | tf_op jit(solution)/shard_map/ppermute | solution.py:36
  82.4 4.3 %all-to-all-done.arrived = bf16[16,64,128]{2,1,0:T(8,128)(2,1)} async-done(((bf16[16,64,128]{2,1,0:T(8,128)(2,1)}), bf16[16,64,128]{2,1,0:T(8,128)(2,1)}, u32[]{:S(2)}, u32[]{:S(2)}) %all-to-all-start) | async-done | bytes 262176 | tf_op jit(solution)/shard_map/all_to_all | solution.py:267
  86.7 3.7 %collective-permute-start.16 = (bf16[3,144,1024]{2,1,0:T(8,128)(2,1)}, bf16[3,144,1024]{2,1,0:T(8,128)(2,1)}, u32[]{:S(2)}, u32[]{:S(2)}) collective-permute-start(bf16[3,144,1024]{2,1,0:T(8,128)(2,1)} %collective-permute-done.8.up_more), channel_id=1, source_target_pairs={{0,32},{1,49},{2,34},{3,51},{4,36},{5,53},{6,38},{7,55},{8,40},{9,... | collective-permute-start | bytes 2654216 | tf_op jit(solution)/shard_map/ppermute | solution.py:36
  90.4 2.4 %collective-permute-start.12 = (bf16[3,144,1024]{2,1,0:T(8,128)(2,1)}, bf16[3,144,1024]{2,1,0:T(8,128)(2,1)}, u32[]{:S(2)}, u32[]{:S(2)}) collective-permute-start(bf16[3,144,1024]{2,1,0:T(8,128)(2,1)} %collective-permute-done.8.up_more), channel_id=1, source_target_pairs={{0,1},{1,0},{2,3},{3,2},{4,5},{5,4},{6,7},{7,6},{8,9},{9,8},{10,11... | collective-permute-start | bytes 2654216 | tf_op jit(solution)/shard_map/ppermute | solution.py:36
  92.8 3.3 %collective-permute-start.19 = (bf16[3,144,1024]{2,1,0:T(8,128)(2,1)}, bf16[3,144,1024]{2,1,0:T(8,128)(2,1)}, u32[]{:S(2)}, u32[]{:S(2)}) collective-permute-start(bf16[3,144,1024]{2,1,0:T(8,128)(2,1)} %collective-permute-done.8.up_more), channel_id=1, source_target_pairs={{0,2},{1,15},{2,4},{3,1},{4,6},{5,3},{6,8},{7,5},{8,10},{9,7},{10,... | collective-permute-start | bytes 2654216 | tf_op jit(solution)/shard_map/ppermute | solution.py:36
  96.2 2.5 %collective-permute-start.15 = (bf16[3,144,1024]{2,1,0:T(8,128)(2,1)}, bf16[3,144,1024]{2,1,0:T(8,128)(2,1)}, u32[]{:S(2)}, u32[]{:S(2)}) collective-permute-start(bf16[3,144,1024]{2,1,0:T(8,128)(2,1)} %collective-permute-done.9.side_more), channel_id=1, source_target_pairs={{0,1},{1,0},{2,3},{3,2},{4,5},{5,4},{6,7},{7,6},{8,9},{9,8},{10,11... | collective-permute-start | bytes 2654216 | tf_op jit(solution)/shard_map/ppermute | solution.py:36
  102.3 3.4 %collective-permute-start.18 = (bf16[3,144,1024]{2,1,0:T(8,128)(2,1)}, bf16[3,144,1024]{2,1,0:T(8,128)(2,1)}, u32[]{:S(2)}, u32[]{:S(2)}) collective-permute-start(bf16[3,144,1024]{2,1,0:T(8,128)(2,1)} %collective-permute-done.16.turn_more), channel_id=1, source_target_pairs={{0,1},{1,0},{2,3},{3,2},{4,5},{5,4},{6,7},{7,6},{8,9},{9,8},{10,11... | collective-permute-start | bytes 2654216 | tf_op jit(solution)/shard_map/ppermute | solution.py:36
  105.8 3.5 %place_early_pieces.1.before = bf16[8,1152,1024]{2,1,0:T(8,128)(2,1)S(1)} custom-call(s32[6]{0:T(128)S(1)} %stack.44.place, bf16[1152,1024]{1,0:T(8,128)(2,1)S(1)} %pad_maximum_fusion.pack, bf16[576,1024]{1,0:T(8,128)(2,1)} %collective-permute-done.7.beside, bf16[3,144,1024]{2,1,0:T(8,128)(2,1)S(1)} %pad_maximum_fusion.1.own, ...), custom_call_target="tpu_custom_call" | custom-call | tf_op jit(solution)/shard_map/place_early_pieces/pallas_call | solution.py:279
  111.3 4.7 %place_late_pieces.1.layers.layers_in = bf16[8,1152,1024]{2,1,0:T(8,128)(2,1)S(1)} custom-call(s32[6]{0:T(128)S(1)} %stack.44.place, bf16[576,1024]{1,0:T(8,128)(2,1)} %collective-permute-done.10.beside, bf16[3,144,1024]{2,1,0:T(8,128)(2,1)} %collective-permute-done.11.up, ...), custom_call_target="tpu_custom_call", output_to_operand_aliasing={{}: (12, {})} | custom-call | tf_op jit(solution)/shard_map/place_late_pieces/pallas_call | solution.py:293
  116.0 6.3 %forward_first_stage.1 = (bf16[128,1024]{1,0:T(8,128)(2,1)S(1)}, f32[8,128,1024]{2,1,0:T(8,128)S(1)}, f32[8,128,128]{2,1,0:T(8,128)S(1)}) custom-call(s32[6]{0:T(128)S(1)} %stack.44.place, bf16[16,64,128]{2,1,0:T(8,128)(2,1)} %all-to-all-done.arrived, bf16[8,1152,1024]{2,1,0:T(8,128)(2,1)S(1)} %place_late_pieces.1.layers.layers_in), custom_call_target="tpu_custom_call" | custom-call | flops 2415919104 | bytes 18874368 | tf_op jit(solution)/shard_map/forward_first_stage/pallas_call | solution.py:306
  123.7 6.0 %collective-permute-start.23 = (bf16[2,16,4096]{2,1,0:T(8,128)(2,1)S(1)}, bf16[2,16,4096]{2,1,0:T(8,128)(2,1)S(1)}, u32[]{:S(2)}, u32[]{:S(2)}) collective-permute-start(bf16[2,16,4096]{2,1,0:T(8,128)(2,1)S(1)} %pad_maximum_fusion.3), channel_id=1, source_target_pairs={{0,16},{1,17},{2,18},{3,19},{4,20},{5,21},{6,22},{7,23},{8,24},{9,... | collective-permute-start | bytes 786440 | tf_op jit(solution)/shard_map/ppermute | solution.py:36
  129.7 5.1 %collective-permute-done.20.hidden = bf16[128,1024]{1,0:T(8,128)(2,1)S(1)} collective-permute-done((bf16[128,1024]{1,0:T(8,128)(2,1)S(1)}, bf16[128,1024]{1,0:T(8,128)(2,1)S(1)}, u32[]{:S(2)}, u32[]{:S(2)}) %collective-permute-start.20) | collective-permute-done | bytes 262176 | tf_op jit(solution)/shard_map/ppermute | solution.py:36
  137.1 25.6 %collective-permute-done.21.upstream = bf16[128,1024]{1,0:T(8,128)(2,1)S(1)} collective-permute-done((bf16[128,1024]{1,0:T(8,128)(2,1)S(1)}, bf16[128,1024]{1,0:T(8,128)(2,1)S(1)}, u32[]{:S(2)}, u32[]{:S(2)}) %collective-permute-start.21) | collective-permute-done | bytes 262176 | tf_op jit(solution)/shard_map/ppermute | solution.py:36
  162.7 11.1 %backward_first_stage.1 = bf16[8,64,64]{2,1,0:T(8,128)(2,1)S(1)} custom-call(s32[6]{0:T(128)S(1)} %stack.44.place, bf16[128,1024]{1,0:T(8,128)(2,1)S(1)} %collective-permute-done.21.upstream, f32[8,128,1024]{2,1,0:T(8,128)S(1)} %get-tuple-element.37.slope_in, f32[8,128,128]{2,1,0:T(8,128)S(1)} %get-tuple-element.38.left, ...), custom_call_target="tpu_custom_call" | custom-call | flops 2415919104 | bytes 18874368 | tf_op jit(solution)/shard_map/backward_first_stage/pallas_call | solution.py:329
  176.2 4.3 %all-to-all-start.1 = ((bf16[8,2,2048]{2,1,0:T(2,128)(2,1)}), bf16[8,2,2048]{2,1,0:T(2,128)(2,1)S(1)}, u32[]{:S(2)}, u32[]{:S(2)}) async-start(bf16[8,2,2048]{2,1,0:T(2,128)(2,1)} %reshape.63), calls=%async_computation.1 | async-start | bytes 131072 | tf_op jit(solution)/shard_map/all_to_all | solution.py:347
  180.5 5.9 %all-to-all-done.1 = bf16[8,2,2048]{2,1,0:T(2,128)(2,1)S(1)} async-done(((bf16[8,2,2048]{2,1,0:T(2,128)(2,1)}), bf16[8,2,2048]{2,1,0:T(2,128)(2,1)S(1)}, u32[]{:S(2)}, u32[]{:S(2)}) %all-to-all-start.1) | async-done | bytes 65568 | tf_op jit(solution)/shard_map/all_to_all | solution.py:347
  187.8 4.2 %all-to-all-start.2 = ((bf16[8,2,4096]{2,1,0:T(2,128)(2,1)}), bf16[8,2,4096]{2,1,0:T(2,128)(2,1)S(1)}, u32[]{:S(2)}, u32[]{:S(2)}) async-start(bf16[8,2,4096]{2,1,0:T(2,128)(2,1)} %broadcast_in_dim.10), calls=%async_computation.2 | async-start | bytes 262144 | tf_op jit(solution)/shard_map/all_to_all | solution.py:352
  192.0 8.0 %all-to-all-done.2 = bf16[8,2,4096]{2,1,0:T(2,128)(2,1)S(1)} async-done(((bf16[8,2,4096]{2,1,0:T(2,128)(2,1)}), bf16[8,2,4096]{2,1,0:T(2,128)(2,1)S(1)}, u32[]{:S(2)}, u32[]{:S(2)}) %all-to-all-start.2) | async-done | bytes 131104 | tf_op jit(solution)/shard_map/all_to_all | solution.py:352
  201.0 9.9 %all_to_all.30 = f32[16,1,128]{2,1,0:T(1,128)S(1)} all-to-all(f32[16,1,128]{2,1,0:T(1,128)S(1)} %reshape.65), channel_id=1, replica_groups=mesh['section'=16,'dp'=32] {'section'}, dimensions={0} | all-to-all | bytes 16384 | tf_op jit(solution)/shard_map/all_to_all | solution.py:371
  212.3 13.0 %all_to_all.31 = f32[4,2,16]{2,1,0:T(2,128)S(1)} all-to-all(f32[4,2,16]{2,1,0:T(2,128)S(1)} %copy.19), channel_id=1, replica_groups={{0,1,16,17},{2,3,18,19},{4,5,20,21},{6,7,22,23},{8,9,24,25},{10,11,26,2..., dimensions={0} | all-to-all | bytes 1024 | tf_op jit(solution)/shard_map/all_to_all | solution.py:373
  (86 shorter events, 30.4 us)
Async XLA Ops:
  0.0 17.6 %copy-start = (bf16[2,512,64]{1,2,0:T(8,128)(2,1)S(1)}, bf16[2,512,64]{1,2,0:T(8,128)(2,1)}, u32[]{:S(2)}) copy-start(bf16[2,512,64]{1,2,0:T(8,128)(2,1)} %param.6) | copy-start | bytes 393220
  2.0 15.7 %copy-start.7 = (bf16[2,512,64]{1,2,0:T(8,128)(2,1)S(1)}, bf16[2,512,64]{1,2,0:T(8,128)(2,1)}, u32[]{:S(2)}) copy-start(bf16[2,512,64]{1,2,0:T(8,128)(2,1)} %param.7) | copy-start | bytes 393220
  2.7 24.2 %collective-permute-start.2 = (bf16[144,1024]{1,0:T(8,128)(2,1)}, bf16[144,1024]{1,0:T(8,128)(2,1)S(1)}, u32[]{:S(2)}, u32[]{:S(2)}) collective-permute-start(bf16[144,1024]{1,0:T(8,128)(2,1)} %constant_dynamic-slice_fusion.1), channel_id=1, source_target_pairs={{0,192},{1,193},{2,194},{3,195},{4,196},{5,197},{6,198},{7,199},{8... | collective-permute-start | bytes 884744 | tf_op jit(solution)/shard_map/ppermute | solution.py:36
  8.8 24.8 %collective-permute-start.1 = (bf16[144,1024]{1,0:T(8,128)(2,1)}, bf16[144,1024]{1,0:T(8,128)(2,1)S(1)}, u32[]{:S(2)}, u32[]{:S(2)}) collective-permute-start(bf16[144,1024]{1,0:T(8,128)(2,1)} %constant_dynamic-slice_fusion.1), channel_id=1, source_target_pairs={{0,128},{1,129},{2,130},{3,131},{4,132},{5,133},{6,134},{7,135},{8... | collective-permute-start | bytes 884744 | tf_op jit(solution)/shard_map/ppermute | solution.py:36
  10.7 16.2 %collective-permute-start = (bf16[144,1024]{1,0:T(8,128)(2,1)}, bf16[144,1024]{1,0:T(8,128)(2,1)S(1)}, u32[]{:S(2)}, u32[]{:S(2)}) collective-permute-start(bf16[144,1024]{1,0:T(8,128)(2,1)} %constant_dynamic-slice_fusion.1), channel_id=1, source_target_pairs={{0,64},{1,65},{2,66},{3,67},{4,68},{5,69},{6,70},{7,71},{8,72},{9,... | collective-permute-start | bytes 884744 | tf_op jit(solution)/shard_map/ppermute | solution.py:36
  13.2 51.5 %collective-permute-start.7 = (bf16[576,1024]{1,0:T(8,128)(2,1)S(1)}, bf16[576,1024]{1,0:T(8,128)(2,1)}, u32[]{:S(2)}, u32[]{:S(2)}) collective-permute-start(bf16[576,1024]{1,0:T(8,128)(2,1)S(1)} %constant_dynamic-slice_fusion), channel_id=1, source_target_pairs={{0,32},{1,49},{2,34},{3,51},{4,36},{5,53},{6,38},{7,55},{8,40},{9,... | collective-permute-start | bytes 3538952 | tf_op jit(solution)/shard_map/ppermute | solution.py:36
  17.7 15.9 %copy-start.2 = (bf16[16,64,128]{2,1,0:T(8,128)(2,1)}, bf16[16,64,128]{2,1,0:T(8,128)(2,1)S(1)}, u32[]{:S(2)}) copy-start(bf16[16,64,128]{2,1,0:T(8,128)(2,1)S(1)} %slice_dynamic-update-slice_fusion) | copy-start | bytes 786436
  26.9 6.7 %copy-start.6 = (bf16[144,1024]{1,0:T(8,128)(2,1)}, bf16[144,1024]{1,0:T(8,128)(2,1)S(1)}, u32[]{:S(2)}) copy-start(bf16[144,1024]{1,0:T(8,128)(2,1)S(1)} %collective-permute-done) | copy-start | bytes 884740
  35.6 20.6 %collective-permute-start.3 = (bf16[3,144,1024]{2,1,0:T(8,128)(2,1)S(1)}, bf16[3,144,1024]{2,1,0:T(8,128)(2,1)}, u32[]{:S(2)}, u32[]{:S(2)}) collective-permute-start(bf16[3,144,1024]{2,1,0:T(8,128)(2,1)S(1)} %pad_maximum_fusion.1.own), channel_id=1, source_target_pairs={{0,2},{1,15},{2,4},{3,1},{4,6},{5,3},{6,8},{7,5},{8,10},{9,7},{10,... | collective-permute-start | bytes 2654216 | tf_op jit(solution)/shard_map/ppermute | solution.py:36
  46.2 18.5 %collective-permute-start.6 = (bf16[3,144,1024]{2,1,0:T(8,128)(2,1)S(1)}, bf16[3,144,1024]{2,1,0:T(8,128)(2,1)}, u32[]{:S(2)}, u32[]{:S(2)}) collective-permute-start(bf16[3,144,1024]{2,1,0:T(8,128)(2,1)S(1)} %pad_maximum_fusion.1.own), channel_id=1, source_target_pairs={{0,1},{1,0},{2,3},{3,2},{4,5},{5,4},{6,7},{7,6},{8,9},{9,8},{10,11... | collective-permute-start | bytes 2654216 | tf_op jit(solution)/shard_map/ppermute | solution.py:36
  48.2 27.4 %collective-permute-start.13 = (bf16[3,144,1024]{2,1,0:T(8,128)(2,1)S(1)}, bf16[3,144,1024]{2,1,0:T(8,128)(2,1)}, u32[]{:S(2)}, u32[]{:S(2)}) collective-permute-start(bf16[3,144,1024]{2,1,0:T(8,128)(2,1)S(1)} %pad_maximum_fusion.1.own), channel_id=1, source_target_pairs={{0,32},{1,49},{2,34},{3,51},{4,36},{5,53},{6,38},{7,55},{8,40},{9,... | collective-permute-start | bytes 2654216 | tf_op jit(solution)/shard_map/ppermute | solution.py:36
  56.2 21.8 %collective-permute-start.4 = (bf16[3,144,1024]{2,1,0:T(8,128)(2,1)}, bf16[3,144,1024]{2,1,0:T(8,128)(2,1)}, u32[]{:S(2)}, u32[]{:S(2)}) collective-permute-start(bf16[3,144,1024]{2,1,0:T(8,128)(2,1)} %collective-permute-done.3.up), channel_id=1, source_target_pairs={{0,32},{1,49},{2,34},{3,51},{4,36},{5,53},{6,38},{7,55},{8,40},{9,... | collective-permute-start | bytes 2654216 | tf_op jit(solution)/shard_map/ppermute | solution.py:36
  61.0 18.9 %collective-permute-start.5 = (bf16[3,144,1024]{2,1,0:T(8,128)(2,1)}, bf16[3,144,1024]{2,1,0:T(8,128)(2,1)}, u32[]{:S(2)}, u32[]{:S(2)}) collective-permute-start(bf16[3,144,1024]{2,1,0:T(8,128)(2,1)} %collective-permute-done.3.up), channel_id=1, source_target_pairs={{0,2},{1,15},{2,4},{3,1},{4,6},{5,3},{6,8},{7,5},{8,10},{9,7},{10,... | collective-permute-start | bytes 2654216 | tf_op jit(solution)/shard_map/ppermute | solution.py:36
  64.7 21.9 %collective-permute-start.8 = (bf16[3,144,1024]{2,1,0:T(8,128)(2,1)}, bf16[3,144,1024]{2,1,0:T(8,128)(2,1)}, u32[]{:S(2)}, u32[]{:S(2)}) collective-permute-start(bf16[3,144,1024]{2,1,0:T(8,128)(2,1)} %collective-permute-done.6.own_other), channel_id=1, source_target_pairs={{0,2},{1,15},{2,4},{3,1},{4,6},{5,3},{6,8},{7,5},{8,10},{9,7},{10,... | collective-permute-start | bytes 2654216 | tf_op jit(solution)/shard_map/ppermute | solution.py:36
  66.9 19.7 %collective-permute-start.9 = (bf16[3,144,1024]{2,1,0:T(8,128)(2,1)}, bf16[3,144,1024]{2,1,0:T(8,128)(2,1)}, u32[]{:S(2)}, u32[]{:S(2)}) collective-permute-start(bf16[3,144,1024]{2,1,0:T(8,128)(2,1)} %collective-permute-done.6.own_other), channel_id=1, source_target_pairs={{0,32},{1,49},{2,34},{3,51},{4,36},{5,53},{6,38},{7,55},{8,40},{9,... | collective-permute-start | bytes 2654216 | tf_op jit(solution)/shard_map/ppermute | solution.py:36
  68.8 17.8 %all-to-all-start = ((bf16[16,64,128]{2,1,0:T(8,128)(2,1)}), bf16[16,64,128]{2,1,0:T(8,128)(2,1)}, u32[]{:S(2)}, u32[]{:S(2)}) async-start(bf16[16,64,128]{2,1,0:T(8,128)(2,1)} %copy-done.2), calls=%async_computation | async-start | bytes 524288 | tf_op jit(solution)/shard_map/all_to_all | solution.py:267
  75.5 23.2 %collective-permute-start.10 = (bf16[576,1024]{1,0:T(8,128)(2,1)}, bf16[576,1024]{1,0:T(8,128)(2,1)}, u32[]{:S(2)}, u32[]{:S(2)}) collective-permute-start(bf16[576,1024]{1,0:T(8,128)(2,1)} %collective-permute-done.7.beside), channel_id=1, source_target_pairs={{0,1},{1,0},{2,3},{3,2},{4,5},{5,4},{6,7},{7,6},{8,9},{9,8},{10,11... | collective-permute-start | bytes 3538952 | tf_op jit(solution)/shard_map/ppermute | solution.py:36
  78.0 14.8 %collective-permute-start.11 = (bf16[3,144,1024]{2,1,0:T(8,128)(2,1)}, bf16[3,144,1024]{2,1,0:T(8,128)(2,1)}, u32[]{:S(2)}, u32[]{:S(2)}) collective-permute-start(bf16[3,144,1024]{2,1,0:T(8,128)(2,1)} %collective-permute-done.3.up), channel_id=1, source_target_pairs={{0,1},{1,0},{2,3},{3,2},{4,5},{5,4},{6,7},{7,6},{8,9},{9,8},{10,11... | collective-permute-start | bytes 2654216 | tf_op jit(solution)/shard_map/ppermute | solution.py:36
  80.0 16.2 %collective-permute-start.14 = (bf16[3,144,1024]{2,1,0:T(8,128)(2,1)}, bf16[3,144,1024]{2,1,0:T(8,128)(2,1)}, u32[]{:S(2)}, u32[]{:S(2)}) collective-permute-start(bf16[3,144,1024]{2,1,0:T(8,128)(2,1)} %collective-permute-done.13.side), channel_id=1, source_target_pairs={{0,1},{1,0},{2,3},{3,2},{4,5},{5,4},{6,7},{7,6},{8,9},{9,8},{10,11... | collective-permute-start | bytes 2654216 | tf_op jit(solution)/shard_map/ppermute | solution.py:36
  86.7 15.6 %collective-permute-start.16 = (bf16[3,144,1024]{2,1,0:T(8,128)(2,1)}, bf16[3,144,1024]{2,1,0:T(8,128)(2,1)}, u32[]{:S(2)}, u32[]{:S(2)}) collective-permute-start(bf16[3,144,1024]{2,1,0:T(8,128)(2,1)} %collective-permute-done.8.up_more), channel_id=1, source_target_pairs={{0,32},{1,49},{2,34},{3,51},{4,36},{5,53},{6,38},{7,55},{8,40},{9,... | collective-permute-start | bytes 2654216 | tf_op jit(solution)/shard_map/ppermute | solution.py:36
  90.4 18.9 %collective-permute-start.12 = (bf16[3,144,1024]{2,1,0:T(8,128)(2,1)}, bf16[3,144,1024]{2,1,0:T(8,128)(2,1)}, u32[]{:S(2)}, u32[]{:S(2)}) collective-permute-start(bf16[3,144,1024]{2,1,0:T(8,128)(2,1)} %collective-permute-done.8.up_more), channel_id=1, source_target_pairs={{0,1},{1,0},{2,3},{3,2},{4,5},{5,4},{6,7},{7,6},{8,9},{9,8},{10,11... | collective-permute-start | bytes 2654216 | tf_op jit(solution)/shard_map/ppermute | solution.py:36
  92.8 18.5 %collective-permute-start.19 = (bf16[3,144,1024]{2,1,0:T(8,128)(2,1)}, bf16[3,144,1024]{2,1,0:T(8,128)(2,1)}, u32[]{:S(2)}, u32[]{:S(2)}) collective-permute-start(bf16[3,144,1024]{2,1,0:T(8,128)(2,1)} %collective-permute-done.8.up_more), channel_id=1, source_target_pairs={{0,2},{1,15},{2,4},{3,1},{4,6},{5,3},{6,8},{7,5},{8,10},{9,7},{10,... | collective-permute-start | bytes 2654216 | tf_op jit(solution)/shard_map/ppermute | solution.py:36
  96.2 15.1 %collective-permute-start.15 = (bf16[3,144,1024]{2,1,0:T(8,128)(2,1)}, bf16[3,144,1024]{2,1,0:T(8,128)(2,1)}, u32[]{:S(2)}, u32[]{:S(2)}) collective-permute-start(bf16[3,144,1024]{2,1,0:T(8,128)(2,1)} %collective-permute-done.9.side_more), channel_id=1, source_target_pairs={{0,1},{1,0},{2,3},{3,2},{4,5},{5,4},{6,7},{7,6},{8,9},{9,8},{10,11... | collective-permute-start | bytes 2654216 | tf_op jit(solution)/shard_map/ppermute | solution.py:36
  98.7 12.5 %collective-permute-start.17 = (bf16[3,144,1024]{2,1,0:T(8,128)(2,1)}, bf16[3,144,1024]{2,1,0:T(8,128)(2,1)}, u32[]{:S(2)}, u32[]{:S(2)}) collective-permute-start(bf16[3,144,1024]{2,1,0:T(8,128)(2,1)} %collective-permute-done.4.turn), channel_id=1, source_target_pairs={{0,1},{1,0},{2,3},{3,2},{4,5},{5,4},{6,7},{7,6},{8,9},{9,8},{10,11... | collective-permute-start | bytes 2654216 | tf_op jit(solution)/shard_map/ppermute | solution.py:36
  102.3 9.0 %collective-permute-start.18 = (bf16[3,144,1024]{2,1,0:T(8,128)(2,1)}, bf16[3,144,1024]{2,1,0:T(8,128)(2,1)}, u32[]{:S(2)}, u32[]{:S(2)}) collective-permute-start(bf16[3,144,1024]{2,1,0:T(8,128)(2,1)} %collective-permute-done.16.turn_more), channel_id=1, source_target_pairs={{0,1},{1,0},{2,3},{3,2},{4,5},{5,4},{6,7},{7,6},{8,9},{9,8},{10,11... | collective-permute-start | bytes 2654216 | tf_op jit(solution)/shard_map/ppermute | solution.py:36
  109.3 14.3 %collective-permute-start.22 = (bf16[1,16,4096]{2,1,0:T(8,128)(2,1)S(1)}, bf16[1,16,4096]{2,1,0:T(8,128)(2,1)S(1)}, u32[]{:S(2)}, u32[]{:S(2)}) collective-permute-start(bf16[1,16,4096]{2,1,0:T(8,128)(2,1)S(1)} %copy-done.3), channel_id=1, source_target_pairs={{0,1},{1,0},{2,3},{3,2},{4,5},{5,4},{6,7},{7,6},{8,9},{9,8},{10,11... | collective-permute-start | bytes 393224 | tf_op jit(solution)/shard_map/ppermute | solution.py:36
  116.0 18.8 %copy-start.1 = (bf16[8,1152,1024]{2,1,0:T(8,128)(2,1)}, bf16[8,1152,1024]{2,1,0:T(8,128)(2,1)S(1)}, u32[]{:S(2)}) copy-start(bf16[8,1152,1024]{2,1,0:T(8,128)(2,1)S(1)} %place_late_pieces.1.layers.layers_in) | copy-start | bytes 56623108
  122.3 12.4 %collective-permute-start.20 = (bf16[128,1024]{1,0:T(8,128)(2,1)S(1)}, bf16[128,1024]{1,0:T(8,128)(2,1)S(1)}, u32[]{:S(2)}, u32[]{:S(2)}) collective-permute-start(bf16[128,1024]{1,0:T(8,128)(2,1)S(1)} %get-tuple-element.33), channel_id=1, source_target_pairs={{0,448},{1,449},{2,450},{3,451},{4,452},{5,453},{6,454},{7,455},{8... | collective-permute-start | bytes 786440 | tf_op jit(solution)/shard_map/ppermute | solution.py:36
  123.7 13.3 %collective-permute-start.23 = (bf16[2,16,4096]{2,1,0:T(8,128)(2,1)S(1)}, bf16[2,16,4096]{2,1,0:T(8,128)(2,1)S(1)}, u32[]{:S(2)}, u32[]{:S(2)}) collective-permute-start(bf16[2,16,4096]{2,1,0:T(8,128)(2,1)S(1)} %pad_maximum_fusion.3), channel_id=1, source_target_pairs={{0,16},{1,17},{2,18},{3,19},{4,20},{5,21},{6,22},{7,23},{8,24},{9,... | collective-permute-start | bytes 786440 | tf_op jit(solution)/shard_map/ppermute | solution.py:36
  135.7 27.0 %collective-permute-start.21 = (bf16[128,1024]{1,0:T(8,128)(2,1)S(1)}, bf16[128,1024]{1,0:T(8,128)(2,1)S(1)}, u32[]{:S(2)}, u32[]{:S(2)}) collective-permute-start(bf16[128,1024]{1,0:T(8,128)(2,1)S(1)} %get-tuple-element.34), channel_id=1, source_target_pairs={{256,192},{257,193},{258,194},{259,195},{260,196},{261,197},{262,1... | collective-permute-start | bytes 786440 | tf_op jit(solution)/shard_map/ppermute | solution.py:36
  176.2 10.2 %all-to-all-start.1 = ((bf16[8,2,2048]{2,1,0:T(2,128)(2,1)}), bf16[8,2,2048]{2,1,0:T(2,128)(2,1)S(1)}, u32[]{:S(2)}, u32[]{:S(2)}) async-start(bf16[8,2,2048]{2,1,0:T(2,128)(2,1)} %reshape.63), calls=%async_computation.1 | async-start | bytes 131072 | tf_op jit(solution)/shard_map/all_to_all | solution.py:347
  187.8 12.2 %all-to-all-start.2 = ((bf16[8,2,4096]{2,1,0:T(2,128)(2,1)}), bf16[8,2,4096]{2,1,0:T(2,128)(2,1)S(1)}, u32[]{:S(2)}, u32[]{:S(2)}) async-start(bf16[8,2,4096]{2,1,0:T(2,128)(2,1)} %broadcast_in_dim.10), calls=%async_computation.2 | async-start | bytes 262144 | tf_op jit(solution)/shard_map/all_to_all | solution.py:352
  (3 other events, 10.9 us)

commit v3 on v2

v3 whole, which is shorter than its diff:
```python
import functools

import jax
import jax.numpy as jnp
from jax import lax
from jax.experimental import pallas as pl
from jax.experimental.pallas import tpu as pltpu
from jax.sharding import PartitionSpec as P

AXES = ("section", "dp")
TOK = 128
STAGE = 8
D = 1024
RANK = 64
PACK = D + 2 * RANK
PIECE = PACK // 8


def flat(x, y, z, c):
    return (y % 8 * 2 + x % 2) * 32 + ((x % 4 // 2) * 8 + z % 8) * 2 + c


def pairs(target):
    out = []
    for x in range(4):
        for y in range(8):
            for z in range(8):
                for c in range(2):
                    to = target(x, y, z, c)
                    if to is not None:
                        out.append((flat(x, y, z, c), flat(*to)))
    return out


def move(value, target):
    return lax.ppermute(value, AXES, pairs(target))


def swap_core(value):
    return move(value, lambda x, y, z, c: (x, y, z, 1 - c))


def gather_rows(pack, core, quarter):
    piece = lax.dynamic_slice_in_dim(pack, (core * 4 + quarter) * PIECE, PIECE, 0)
    rows = [
        move(piece, lambda x, y, z, c, r=r: (x, y // 4 * 4 + (y + r) % 4, z, c)) for r in (1, 2, 3)
    ]
    half = lax.dynamic_slice_in_dim(pack, core * (PACK // 2), PACK // 2, 0)
    beside = move(half, lambda x, y, z, c: (x + 1 if c == 0 else x - 1, y, z, c))
    return rows, beside


def along_z(value):
    return move(value, lambda x, y, z, c: (x, y, z + 1 - 2 * (c ^ (x // 2)), c))


def along_x(value):
    return move(value, lambda x, y, z, c: (x ^ 1 if c == 0 else 3 - x, y, z, c))


def assemble(place, pieces, beside, whole, extra, layers, sems):
    row, col, core = (place[k] for k in range(3))
    copies = []

    def put(source, target):
        copies.append(pltpu.make_async_copy(source, target, sems.at[len(copies)]))

    def rows(piece):
        return pl.ds(pl.multiple_of(piece * PIECE, PIECE), PIECE)

    if whole is not None:
        put(whole, layers.at[row * 2 + col])
    half, refs = beside
    for k in range(4):
        put(refs[k // 2].at[k % 2], layers.at[row * 2 + 1 - col, rows(half * 4 + k)])
    for distance in (1, 2, 3):
        source_row = (row - distance) & 3
        for ref, index, other_col, other_core, quarter in pieces:
            slot = source_row * 2 + (1 - col if other_col else col)
            half = 1 - core if other_core else core
            put(ref.at[index + distance - 1], layers.at[slot, rows(half * 4 + (quarter & 3))])
    for source, target in extra:
        put(source, target)
    for copy in copies:
        copy.start()
    for copy in copies:
        copy.wait()


def early_kernel(place, pack, beside, own, up, side, layers, first, second, sems):
    core, quarter, way = (place[k] for k in (2, 3, 4))
    pieces = []
    for k in (0, 1):
        pieces.append((own.at[k], 0, 0, k, quarter))
        pieces.append((up, 3 * k, 0, k, quarter - way))
        pieces.append((side, 3 * k, 1, k, quarter + 2 * core))
    extra = [
        (beside.at[pl.ds(0, 2)], first.at[pl.ds(0, 2)]),
        (beside.at[pl.ds(2, 2)], second.at[pl.ds(0, 2)]),
        (up, first.at[pl.ds(2, 6)]),
        (side, second.at[pl.ds(2, 6)]),
    ]
    assemble(place, pieces, (core, (beside.at[pl.ds(0, 2)], beside.at[pl.ds(2, 2)])), pack, extra, layers, sems)


def late_kernel(place, first, second, turn, turn_other, two, before, layers, sems):
    core, quarter, way = (place[k] for k in (2, 3, 4))
    pieces = []
    for k in (0, 1):
        pieces.append((first, 2 + 3 * k, 0, 1 - k, quarter + way))
        pieces.append((second, 2 + 3 * k, 1, 1 - k, quarter + 2 * (1 - core)))
        pieces.append((two.at[k], 0, 0, k, quarter + 2))
        pieces.append((turn.at[k], 0, 1, k, quarter - way))
        pieces.append((turn_other.at[k], 0, 1, 1 - k, quarter + way))
    assemble(place, pieces, (1 - core, (first, second)), None, (), layers, sems)


CHUNK = 256


def forward_one(slot, current, layers, slope, left):
    hidden = current[...]
    left[slot] = lax.dot_general(
        layers[slot, D:], hidden, (((1,), (1,)), ((), ())), preferred_element_type=jnp.float32
    )
    for start in range(0, D, CHUNK):
        cols = slice(start, start + CHUNK)
        preact = jnp.dot(hidden, layers[slot, :D, cols], preferred_element_type=jnp.float32)
        sig = jax.nn.sigmoid(preact)
        slope[slot, :, cols] = sig * (1.0 + preact * (1.0 - sig))
        current[:, cols] = (hidden[:, cols].astype(jnp.float32) + preact * sig).astype(jnp.bfloat16)


def backward_one(slot, current, layers, slope, right):
    upstream = current[...].astype(jnp.float32)
    grad = (upstream * slope[slot]).astype(jnp.bfloat16)
    nt = (((1,), (1,)), ((), ()))
    right[slot] = lax.dot_general(grad, layers[slot, D:], nt, preferred_element_type=jnp.float32)
    for start in range(0, D, CHUNK):
        cols = slice(start, start + CHUNK)
        carried = lax.dot_general(
            grad, layers[slot, cols], nt, preferred_element_type=jnp.float32
        )
        current[:, cols] = (upstream[:, cols] + carried).astype(jnp.bfloat16)


def finish(left, right, factor):
    for slot in range(STAGE):
        product = jnp.dot(
            left[slot],
            right[slot],
            precision=lax.Precision.HIGHEST,
            preferred_element_type=jnp.float32,
        )
        product = product[:RANK, RANK:].astype(jnp.bfloat16)
        factor[slot] = jnp.concatenate([product[: RANK // 2], product[RANK // 2 :]], axis=1)


def rows_of(arrived):
    return arrived[...].reshape(D, TOK).T


def first_kernel(place, arrived, layers, current, slope_out, left, slope, sems):
    def keep(slot):
        return pltpu.make_async_copy(slope.at[slot], slope_out.at[slot], sems.at[slot])

    @pl.when(place[5] == 0)
    def _():
        current[...] = rows_of(arrived)

        def body(slot, carry):
            forward_one(slot, current, layers, slope, left)
            keep(slot).start()
            return carry

        lax.fori_loop(0, STAGE, body, 0)
        for slot in range(STAGE):
            keep(slot).wait()


def middle_kernel(place, hidden, arrived, layers, upstream, factor, current, slope, left, right):
    @pl.when(place[5] == 1)
    def _():
        current[...] = hidden[...]
        upstream[...] = rows_of(arrived)

        def ahead(slot, carry):
            forward_one(slot, current, layers, slope, left)
            return carry

        lax.fori_loop(0, STAGE, ahead, 0)

        def back(step, carry):
            backward_one(STAGE - 1 - step, upstream, layers, slope, right)
            return carry

        lax.fori_loop(0, STAGE, back, 0)
        finish(left, right, factor)


def last_kernel(place, upstream, slope_in, left, late, layers_in, factor, current, slope, right, layers, sems):
    def fetch(slot):
        return (
            pltpu.make_async_copy(slope_in.at[slot], slope.at[slot], sems.at[0, slot]),
            pltpu.make_async_copy(layers_in.at[slot], layers.at[slot], sems.at[1, slot]),
        )

    @pl.when(place[5] == 0)
    def _():
        for slot in reversed(range(STAGE)):
            for copy in fetch(slot):
                copy.start()
        current[...] = upstream[...]

        def back(step, carry):
            slot = STAGE - 1 - step
            for copy in fetch(slot):
                copy.wait()
            backward_one(slot, current, layers, slope, right)
            return carry

        lax.fori_loop(0, STAGE, back, 0)
        finish(left, right, factor)

    @pl.when(place[5] == 1)
    def _():
        factor[...] = late[...]


VMEM = pl.BlockSpec(memory_space=pltpu.VMEM)
SMEM = pl.BlockSpec(memory_space=pltpu.SMEM)
ANY = pl.BlockSpec(memory_space=pl.ANY)
HBM = pl.BlockSpec(memory_space=pltpu.HBM)
PARAMS = pltpu.CompilerParams(vmem_limit_bytes=8 * 1024 * 1024)
SMALL = pltpu.CompilerParams(vmem_limit_bytes=2 * 1024 * 1024)
LARGE = pltpu.CompilerParams(vmem_limit_bytes=30 * 1024 * 1024)
TOKENS = jax.ShapeDtypeStruct((TOK, D), jnp.bfloat16)
SLOPE = jax.ShapeDtypeStruct((STAGE, TOK, D), jnp.float32)
LEFT = jax.ShapeDtypeStruct((STAGE, 2 * RANK, TOK), jnp.float32)
RIGHT = jax.ShapeDtypeStruct((STAGE, TOK, 2 * RANK), jnp.float32)
FACTOR = jax.ShapeDtypeStruct((STAGE, RANK // 2, 2 * RANK), jnp.bfloat16)
LAYERS = jax.ShapeDtypeStruct((STAGE, PACK, D), jnp.bfloat16)
BUNDLE = jax.ShapeDtypeStruct((8, PIECE, D), jnp.bfloat16)


def scratch(shape):
    return pltpu.VMEM(shape.shape, shape.dtype)


def in_hbm(value):
    return pltpu.with_memory_space_constraint(value, pltpu.HBM)


def cost(passes):
    return pl.CostEstimate(
        flops=2 * passes * STAGE * TOK * D * PACK,
        bytes_accessed=STAGE * D * PACK * 2,
        transcendentals=STAGE * TOK * D,
    )


def on_device(inputs, cotangent, weights, proj_in, proj_out, query_factors):
    section, dp = lax.axis_index("section"), lax.axis_index("dp")
    y, col = section // 2, section % 2
    x_hi, z, core = dp // 16, dp // 2 % 8, dp % 2
    stage = y // 4
    quarter = (z + 2 * x_hi) % 4
    way = 1 - 2 * (core ^ x_hi)
    place = jnp.stack([y % 4, col, core, quarter, way, stage]).astype(jnp.int32)

    pack = jnp.concatenate([weights[0], proj_in[0].T, proj_out[0].T])
    rows, beside = gather_rows(pack, core, quarter)

    ahead, seeds = (
        value.reshape(2, 4, TOK, -1).transpose(0, 1, 3, 2).reshape(STAGE, -1, TOK)
        for value in (inputs, cotangent)
    )
    order = [ahead, seeds[4:], seeds[:4]]
    rows[0], order = lax.optimization_barrier((rows[0], jnp.concatenate(order)))
    arrived = lax.all_to_all(order, "section", 0, 0, tiled=True)

    own = jnp.stack(rows)
    own = jnp.stack([own, swap_core(own)])
    queries = query_factors
    queries = jnp.concatenate([queries, swap_core(queries)])
    own, beside, queries = lax.optimization_barrier((own, beside, queries))
    up, side = along_z(own), along_x(own)
    up, side, arrived = lax.optimization_barrier((up, side, arrived))
    turn, two = along_x(up), along_z(up)
    layers, first, second = pl.pallas_call(
        early_kernel,
        out_shape=(LAYERS, BUNDLE, BUNDLE),
        in_specs=[SMEM] + [ANY] * 5,
        out_specs=(VMEM, ANY, ANY),
        scratch_shapes=[pltpu.SemaphoreType.DMA((27,))],
        compiler_params=SMALL,
        cost_estimate=cost(1),
        name="place_early_pieces",
    )(
        place,
        pack,
        in_hbm(beside.reshape(4, PIECE, D)),
        in_hbm(own),
        in_hbm(up.reshape(6, PIECE, D)),
        in_hbm(side.reshape(6, PIECE, D)),
    )
    first, second = swap_core(first), swap_core(second)
    turn, two = lax.optimization_barrier((turn, two))
    turn_other = swap_core(turn)
    layers = pl.pallas_call(
        late_kernel,
        out_shape=LAYERS,
        in_specs=[SMEM] + [ANY] * 5 + [VMEM],
        out_specs=VMEM,
        scratch_shapes=[pltpu.SemaphoreType.DMA((34,))],
        input_output_aliases={6: 0},
        compiler_params=SMALL,
        name="place_late_pieces",
    )(place, first, second, in_hbm(turn), turn_other, in_hbm(two), layers)

    hidden, slope, left = pl.pallas_call(
        first_kernel,
        out_shape=(TOKENS, SLOPE, LEFT),
        in_specs=[SMEM, VMEM, VMEM],
        out_specs=(VMEM, HBM, VMEM),
        scratch_shapes=[scratch(SLOPE), pltpu.SemaphoreType.DMA((STAGE,))],
        compiler_params=PARAMS,
        cost_estimate=cost(1),
        name="forward_first_stage",
    )(place, arrived, layers)
    hidden = move(hidden, lambda x, y, z, c: (x, (y + 2 if y > 1 else y + 6), z, c) if y < 4 else None)
    left, queries = lax.optimization_barrier((left, queries))
    queries = jnp.concatenate([queries, move(queries, lambda x, y, z, c: (x ^ 2, y, z, c))])
    upstream, factor_late = pl.pallas_call(
        middle_kernel,
        out_shape=(TOKENS, FACTOR),
        in_specs=[SMEM, VMEM, VMEM, VMEM],
        out_specs=(VMEM, VMEM),
        scratch_shapes=[scratch(TOKENS), scratch(SLOPE), scratch(LEFT), scratch(RIGHT)],
        compiler_params=PARAMS,
        cost_estimate=cost(2),
        name="second_stage",
    )(place, hidden, arrived, layers)
    upstream = move(upstream, lambda x, y, z, c: (x, (y - 2 if y < 6 else y - 6), z, c) if y > 3 else None)
    upstream, queries = lax.optimization_barrier((upstream, queries))
    factor = pl.pallas_call(
        last_kernel,
        out_shape=FACTOR,
        in_specs=[SMEM, VMEM, HBM, VMEM, VMEM, HBM],
        out_specs=VMEM,
        scratch_shapes=[
            scratch(TOKENS),
            scratch(SLOPE),
            scratch(RIGHT),
            scratch(LAYERS),
            pltpu.SemaphoreType.DMA((2, STAGE)),
        ],
        compiler_params=LARGE,
        cost_estimate=cost(1),
        name="backward_first_stage",
    )(place, upstream, slope, left, factor_late, in_hbm(layers))

    groups = [list(range(8)), list(range(8, 16))]
    parts = lax.all_to_all(factor, "section", 0, 0, tiled=True, axis_index_groups=groups)
    low, high = parts.reshape(2, 4, RANK // 2, 2 * RANK).astype(jnp.float32).sum(1)
    along = [[(h * 8 + k) * 2 + c for k in range(8)] for h in range(2) for c in range(2)]
    sums = jnp.stack([jnp.where(stage == 0, low, high), jnp.where(stage == 0, high, low)])
    sums = sums.astype(jnp.bfloat16)
    sums = lax.all_to_all(
        jnp.broadcast_to(sums[None], (8,) + sums.shape),
        "dp",
        0,
        0,
        tiled=True,
        axis_index_groups=along,
    ).reshape(16, RANK // 2, 2, RANK)
    sums = sums.transpose(0, 2, 1, 3).reshape(16, -1)
    table = lax.dot_general(
        sums, queries.reshape(-1, sums.shape[1]), (((1,), (1,)), ((), ())),
        preferred_element_type=jnp.float32,
    ).reshape(16, 2, 2, -1)
    table = jnp.where(x_hi == 0, table, table[:, ::-1])
    table = jnp.where(core == 0, table, table[:, :, ::-1]).reshape(8, 2, -1)

    outgoing = lax.dynamic_update_slice_in_dim(
        jnp.zeros((16,) + table.shape[1:], jnp.float32), table, x_hi * 8, 0
    )
    scores = lax.all_to_all(outgoing, "section", 0, 0, tiled=True).sum(0)
    scores = scores.reshape(2, 2, 2, -1).transpose(1, 2, 0, 3)

    def part(far, other):
        value = jnp.where((x_hi ^ far) == 0, scores[0], scores[1])
        return jnp.where((core ^ other) == 0, value[0], value[1])

    def send(far, other):
        def target(x, y, z, c):
            holder = x // 2 == (y % 8 * 2 + x % 2) // 8
            return (x ^ 2 if far else x, y, z, c ^ other) if holder else None

        return move(part(far, other), target)

    near, across, diagonal = send(0, 1), send(1, 0), send(1, 1)
    holds = x_hi == section // 8
    mine = jnp.where(holds, part(0, 0), across)
    theirs = jnp.where(holds, near, diagonal)
    return jnp.where(core == 0, jnp.concatenate([mine, theirs]), jnp.concatenate([theirs, mine]))


def solution(mesh):
    placed = (
        P("dp", None, "section"),
        P("dp", None, "section"),
        P("section", None, None),
        P("section", None, None),
        P("section", None, None),
        P("section", "dp", None),
    )
    return jax.shard_map(
        on_device, mesh=mesh, in_specs=placed, out_specs=P("section", "dp"), check_vma=False
    )
```

time: 227 us -> 221 us (0.974)
  starting transfers between devices: 95.8 us -> 86.9 us
  waiting for transfers between devices: 68.3 us -> 74.8 us
    ppermute x24 -> x19, starting transfers between devices: 80.6 us -> 72.8 us  [move(): return lax.ppermute(value, AXES, pairs(target))]
    ppermute x24 -> x19, waiting for transfers between devices: 50.1 us -> 53.9 us  [move(): return lax.ppermute(value, AXES, pairs(target))]
    all_to_all x1, starting transfers between devices: 6.67 us -> 3.5 us  [on_device(): scores = lax.all_to_all(outgoing, 'section', 0, 0, tiled=True).sum(0)]
    all_to_all x1, waiting for transfers between devices: 4.26 us -> 7.26 us  [on_device(): scores = lax.all_to_all(outgoing, 'section', 0, 0, tiled=True).sum(0)]
    all_to_all x2 -> x1, blocking collectives: 22.8 us -> 22.5 us  [on_device(): arrived = lax.all_to_all(order, 'section', 0, 0, tiled=True)]
  transfers between devices with their start and end apart: 27 -> 22, of which waited for: 9 -> 12; matrix products, arithmetic and copies ran while one was open for 1% -> 1% of each run, Pallas kernels for 7% -> 3%
where the time goes in v3:
time: 221 us; the launch traced here: 220 us
  starting transfers between devices  86.9 us (39%)
  waiting for transfers between devices  74.8 us (34%)
  Pallas kernels  25.8 us (12%)
  blocking collectives  22.5 us (10%)
  other arithmetic  4.7 us (2%)
  local copies, waits for them, and re-layouts  4.17 us (2%)
    ppermute x19, starting transfers between devices, move(): return lax.ppermute(value, AXES, pairs(target))  72.8 us
    ppermute x19, waiting for transfers between devices, move(): return lax.ppermute(value, AXES, pairs(target))  53.9 us
    all_to_all x1, blocking collectives, on_device(): arrived = lax.all_to_all(order, 'section', 0, 0, tiled=True)  22.5 us
    pallas_call x1, Pallas kernels, on_device(): pl.pallas_call(last_kernel, out_shape=FACTOR, in_specs=[SMEM, VMEM, HBM,...  10.8 us
    all_to_all x1, waiting for transfers between devices, on_device(): lax.all_to_all(jnp.broadcast_to(sums[None], (8,) + sums.shape), 'dp', 0,...  7.93 us
    all_to_all x1, waiting for transfers between devices, on_device(): scores = lax.all_to_all(outgoing, 'section', 0, 0, tiled=True).sum(0)  7.26 us
    all_to_all x1, waiting for transfers between devices, on_device(): lax.all_to_all(factor, 'section', 0, 0, tiled=True, axis_index_groups=gro...  5.76 us
    pallas_call x1, Pallas kernels, on_device(): pl.pallas_call(first_kernel, out_shape=(TOKENS, SLOPE, LEFT), in_specs=[S...  5.75 us
  transfers between devices with their start and end apart: 22, of which 12 were waited for; matrix products, arithmetic and copies ran while one was open for 1% of the time, Pallas kernels for 3%

profile of v3, /device:TPU:1, one launch (start us, length us, event | category | flops | bytes accessed | tf_op | source)
XLA Modules:
  0.0 220.2 jit_solution(18231653699402992769)
XLA Ops:
  2.0 4.2 %collective-permute-start = (bf16[144,1024]{1,0:T(8,128)(2,1)S(1)}, bf16[144,1024]{1,0:T(8,128)(2,1)S(1)}, u32[]{:S(2)}, u32[]{:S(2)}) collective-permute-start(bf16[144,1024]{1,0:T(8,128)(2,1)S(1)} %constant_dynamic-slice_fusion.1), channel_id=1, source_target_pairs={{0,64},{1,65},{2,66},{3,67},{4,68},{5,69},{6,70},{7,71},{8,72},{9,... | collective-permute-start | bytes 884744 | tf_op jit(solution)/shard_map/ppermute | solution.py:36
  6.2 4.2 %collective-permute-start.1 = (bf16[144,1024]{1,0:T(8,128)(2,1)S(1)}, bf16[144,1024]{1,0:T(8,128)(2,1)S(1)}, u32[]{:S(2)}, u32[]{:S(2)}) collective-permute-start(bf16[144,1024]{1,0:T(8,128)(2,1)S(1)} %constant_dynamic-slice_fusion.1), channel_id=1, source_target_pairs={{0,128},{1,129},{2,130},{3,131},{4,132},{5,133},{6,134},{7,135},{8... | collective-permute-start | bytes 884744 | tf_op jit(solution)/shard_map/ppermute | solution.py:36
  10.4 3.0 %collective-permute-start.2 = (bf16[144,1024]{1,0:T(8,128)(2,1)S(1)}, bf16[144,1024]{1,0:T(8,128)(2,1)}, u32[]{:S(2)}, u32[]{:S(2)}) collective-permute-start(bf16[144,1024]{1,0:T(8,128)(2,1)S(1)} %constant_dynamic-slice_fusion.1), channel_id=1, source_target_pairs={{0,192},{1,193},{2,194},{3,195},{4,196},{5,197},{6,198},{7,199},{8... | collective-permute-start | bytes 884744 | tf_op jit(solution)/shard_map/ppermute | solution.py:36
  13.5 4.5 %collective-permute-start.4 = (bf16[576,1024]{1,0:T(8,128)(2,1)S(1)}, bf16[576,1024]{1,0:T(8,128)(2,1)S(1)}, u32[]{:S(2)}, u32[]{:S(2)}) collective-permute-start(bf16[576,1024]{1,0:T(8,128)(2,1)S(1)} %constant_dynamic-slice_fusion), channel_id=1, source_target_pairs={{0,32},{1,49},{2,34},{3,51},{4,36},{5,53},{6,38},{7,55},{8,40},{9,... | collective-permute-start | bytes 3538952 | tf_op jit(solution)/shard_map/ppermute | solution.py:36
  18.2 9.6 %collective-permute-done.1 = bf16[144,1024]{1,0:T(8,128)(2,1)S(1)} collective-permute-done((bf16[144,1024]{1,0:T(8,128)(2,1)S(1)}, bf16[144,1024]{1,0:T(8,128)(2,1)S(1)}, u32[]{:S(2)}, u32[]{:S(2)}) %collective-permute-start.1) | collective-permute-done | bytes 294944 | tf_op jit(solution)/shard_map/ppermute | solution.py:36
  27.8 2.0 collective-permute-done.2
  30.9 3.3 %collective-permute-start.3 = (bf16[3,144,1024]{2,1,0:T(8,128)(2,1)S(1)}, bf16[3,144,1024]{2,1,0:T(8,128)(2,1)S(1)}, u32[]{:S(2)}, u32[]{:S(2)}) collective-permute-start(bf16[3,144,1024]{2,1,0:T(8,128)(2,1)S(1)} %get-tuple-element.50), channel_id=1, source_target_pairs={{0,1},{1,0},{2,3},{3,2},{4,5},{5,4},{6,7},{7,6},{8,9},{9,8},{10,11... | collective-permute-start | bytes 2654216 | tf_op jit(solution)/shard_map/ppermute | solution.py:36
  37.7 8.4 %collective-permute-start.6 = (bf16[2,3,144,1024]{3,2,1,0:T(8,128)(2,1)S(1)}, bf16[2,3,144,1024]{3,2,1,0:T(8,128)(2,1)}, u32[]{:S(2)}, u32[]{:S(2)}) collective-permute-start(bf16[2,3,144,1024]{3,2,1,0:T(8,128)(2,1)S(1)} %pad_maximum_fusion.1.own), channel_id=1, source_target_pairs={{0,2},{1,15},{2,4},{3,1},{4,6},{5,3},{6,8},{7,5},{8,10},{9,7},{10,... | collective-permute-start | bytes 5308424 | tf_op jit(solution)/shard_map/ppermute | solution.py:36
  48.1 22.5 %all_to_all.20.arrived = bf16[16,64,128]{2,1,0:T(8,128)(2,1)S(1)} all-to-all(bf16[16,64,128]{2,1,0:T(8,128)(2,1)S(1)} %pad_maximum_fusion.4), channel_id=1, replica_groups=mesh['section'=16,'dp'=32] {'section'}, dimensions={0} | all-to-all | bytes 524288 | tf_op jit(solution)/shard_map/all_to_all | solution.py:280
  71.9 4.1 %collective-permute-start.10 = (bf16[2,3,144,1024]{3,2,1,0:T(8,128)(2,1)}, bf16[2,3,144,1024]{3,2,1,0:T(8,128)(2,1)}, u32[]{:S(2)}, u32[]{:S(2)}) collective-permute-start(bf16[2,3,144,1024]{3,2,1,0:T(8,128)(2,1)} %collective-permute-done.6), channel_id=1, source_target_pairs={{0,32},{1,49},{2,34},{3,51},{4,36},{5,53},{6,38},{7,55},{8,40},{9,... | collective-permute-start | bytes 5308424 | tf_op jit(solution)/shard_map/ppermute | solution.py:36
  76.0 4.3 %collective-permute-start.11 = (bf16[2,3,144,1024]{3,2,1,0:T(8,128)(2,1)}, bf16[2,3,144,1024]{3,2,1,0:T(8,128)(2,1)}, u32[]{:S(2)}, u32[]{:S(2)}) collective-permute-start(bf16[2,3,144,1024]{3,2,1,0:T(8,128)(2,1)} %collective-permute-done.6), channel_id=1, source_target_pairs={{0,2},{1,15},{2,4},{3,1},{4,6},{5,3},{6,8},{7,5},{8,10},{9,7},{10,... | collective-permute-start | bytes 5308424 | tf_op jit(solution)/shard_map/ppermute | solution.py:36
  80.4 5.2 %place_early_pieces.1 = (bf16[8,1152,1024]{2,1,0:T(8,128)(2,1)S(1)}, bf16[8,144,1024]{2,1,0:T(8,128)(2,1)S(1)}, bf16[8,144,1024]{2,1,0:T(8,128)(2,1)S(1)}) custom-call(s32[6]{0:T(128)S(1)} %stack.53.place, bf16[1152,1024]{1,0:T(8,128)(2,1)S(1)} %pad_maximum_fusion.pack, bf16[4,144,1024]{2,1,0:T(8,128)(2,1)} %bitcast.74, bf16[2,3,144,1024]{3,2,1,0:T(8,128)(2,1)} %copy-done.2, ...), custom_call_target="tpu_custom_call" | custom-call | flops 2415919104 | bytes 18874368 | tf_op jit(solution)/shard_map/place_early_pieces/pallas_call | solution.py:290
  87.6 2.4 %collective-permute-start.9 = (bf16[8,144,1024]{2,1,0:T(8,128)(2,1)S(1)}, bf16[8,144,1024]{2,1,0:T(8,128)(2,1)S(1)}, u32[]{:S(2)}, u32[]{:S(2)}) collective-permute-start(bf16[8,144,1024]{2,1,0:T(8,128)(2,1)S(1)} %get-tuple-element.35), channel_id=1, source_target_pairs={{0,1},{1,0},{2,3},{3,2},{4,5},{5,4},{6,7},{7,6},{8,9},{9,8},{10,11... | collective-permute-start | bytes 7077896 | tf_op jit(solution)/shard_map/ppermute | solution.py:36
  90.0 7.0 %collective-permute-done.10.turn = bf16[2,3,144,1024]{3,2,1,0:T(8,128)(2,1)} collective-permute-done((bf16[2,3,144,1024]{3,2,1,0:T(8,128)(2,1)}, bf16[2,3,144,1024]{3,2,1,0:T(8,128)(2,1)}, u32[]{:S(2)}, u32[]{:S(2)}) %collective-permute-start.10) | collective-permute-done | bytes 1769504 | tf_op jit(solution)/shard_map/ppermute | solution.py:36
  97.0 3.1 %collective-permute-done.11.two = bf16[2,3,144,1024]{3,2,1,0:T(8,128)(2,1)} collective-permute-done((bf16[2,3,144,1024]{3,2,1,0:T(8,128)(2,1)}, bf16[2,3,144,1024]{3,2,1,0:T(8,128)(2,1)}, u32[]{:S(2)}, u32[]{:S(2)}) %collective-permute-start.11) | collective-permute-done | bytes 1769504 | tf_op jit(solution)/shard_map/ppermute | solution.py:36
  100.1 3.4 %collective-permute-start.12 = (bf16[2,3,144,1024]{3,2,1,0:T(8,128)(2,1)}, bf16[2,3,144,1024]{3,2,1,0:T(8,128)(2,1)S(1)}, u32[]{:S(2)}, u32[]{:S(2)}) collective-permute-start(bf16[2,3,144,1024]{3,2,1,0:T(8,128)(2,1)} %collective-permute-done.10.turn), channel_id=1, source_target_pairs={{0,1},{1,0},{2,3},{3,2},{4,5},{5,4},{6,7},{7,6},{8,9},{9,8},{10,11... | collective-permute-start | bytes 5308424 | tf_op jit(solution)/shard_map/ppermute | solution.py:36
  103.5 3.5 %collective-permute-done.12.turn_other = bf16[2,3,144,1024]{3,2,1,0:T(8,128)(2,1)S(1)} collective-permute-done((bf16[2,3,144,1024]{3,2,1,0:T(8,128)(2,1)}, bf16[2,3,144,1024]{3,2,1,0:T(8,128)(2,1)S(1)}, u32[]{:S(2)}, u32[]{:S(2)}) %collective-permute-start.12) | collective-permute-done | bytes 1769504 | tf_op jit(solution)/shard_map/ppermute | solution.py:36
  107.0 3.5 %place_late_pieces.1.layers.layers_in = bf16[8,1152,1024]{2,1,0:T(8,128)(2,1)S(1)} custom-call(s32[6]{0:T(128)S(1)} %stack.53.place, bf16[8,144,1024]{2,1,0:T(8,128)(2,1)S(1)} %collective-permute-done.8.first, bf16[8,144,1024]{2,1,0:T(8,128)(2,1)S(1)} %collective-permute-done.9.second, ...), custom_call_target="tpu_custom_call", output_to_operand_aliasing={{}: (6, {})} | custom-call | tf_op jit(solution)/shard_map/place_late_pieces/pallas_call | solution.py:310
  110.5 5.7 %forward_first_stage.1 = (bf16[128,1024]{1,0:T(8,128)(2,1)S(1)}, f32[8,128,1024]{2,1,0:T(8,128)S(1)}, f32[8,128,128]{2,1,0:T(8,128)S(1)}) custom-call(s32[6]{0:T(128)S(1)} %stack.53.place, bf16[16,64,128]{2,1,0:T(8,128)(2,1)S(1)} %all_to_all.20.arrived, bf16[8,1152,1024]{2,1,0:T(8,128)(2,1)S(1)} %place_late_pieces.1.layers.layers_in), custom_call_target="tpu_custom_call" | custom-call | flops 2415919104 | bytes 18874368 | tf_op jit(solution)/shard_map/forward_first_stage/pallas_call | solution.py:321
  116.2 5.3 %collective-permute-start.13 = (bf16[128,1024]{1,0:T(8,128)(2,1)S(1)}, bf16[128,1024]{1,0:T(8,128)(2,1)S(1)}, u32[]{:S(2)}, u32[]{:S(2)}) collective-permute-start(bf16[128,1024]{1,0:T(8,128)(2,1)S(1)} %get-tuple-element.39), channel_id=1, source_target_pairs={{0,384},{1,385},{2,386},{3,387},{4,388},{5,389},{6,390},{7,391},{8... | collective-permute-start | bytes 786440 | tf_op jit(solution)/shard_map/ppermute | solution.py:36
  121.5 6.4 %collective-permute-start.15 = (bf16[2,16,4096]{2,1,0:T(8,128)(2,1)S(1)}, bf16[2,16,4096]{2,1,0:T(8,128)(2,1)S(1)}, u32[]{:S(2)}, u32[]{:S(2)}) collective-permute-start(bf16[2,16,4096]{2,1,0:T(8,128)(2,1)S(1)} %pad_maximum_fusion.5), channel_id=1, source_target_pairs={{0,16},{1,17},{2,18},{3,19},{4,20},{5,21},{6,22},{7,23},{8,24},{9,... | collective-permute-start | bytes 786440 | tf_op jit(solution)/shard_map/ppermute | solution.py:36
  127.9 4.5 %collective-permute-done.13.hidden = bf16[128,1024]{1,0:T(8,128)(2,1)S(1)} collective-permute-done((bf16[128,1024]{1,0:T(8,128)(2,1)S(1)}, bf16[128,1024]{1,0:T(8,128)(2,1)S(1)}, u32[]{:S(2)}, u32[]{:S(2)}) %collective-permute-start.13) | collective-permute-done | bytes 262176 | tf_op jit(solution)/shard_map/ppermute | solution.py:36
  134.3 22.2 %collective-permute-done.14.upstream = bf16[128,1024]{1,0:T(8,128)(2,1)S(1)} collective-permute-done((bf16[128,1024]{1,0:T(8,128)(2,1)S(1)}, bf16[128,1024]{1,0:T(8,128)(2,1)S(1)}, u32[]{:S(2)}, u32[]{:S(2)}) %collective-permute-start.14) | collective-permute-done | bytes 262176 | tf_op jit(solution)/shard_map/ppermute | solution.py:36
  156.5 10.8 %backward_first_stage.1 = bf16[8,32,128]{2,1,0:T(8,128)(2,1)} custom-call(s32[6]{0:T(128)S(1)} %stack.53.place, bf16[128,1024]{1,0:T(8,128)(2,1)S(1)} %collective-permute-done.14.upstream, f32[8,128,1024]{2,1,0:T(8,128)S(1)} %get-tuple-element.45.slope_in, f32[8,128,128]{2,1,0:T(8,128)S(1)} %get-tuple-element.46.left, ...), custom_call_target="tpu_custom_call" | custom-call | flops 2415919104 | bytes 18874368 | tf_op jit(solution)/shard_map/backward_first_stage/pallas_call | solution.py:346
  167.3 4.9 %all-to-all-start.1 = ((bf16[8,32,128]{2,1,0:T(8,128)(2,1)}), bf16[8,32,128]{2,1,0:T(8,128)(2,1)S(1)}, u32[]{:S(2)}, u32[]{:S(2)}) async-start(bf16[8,32,128]{2,1,0:T(8,128)(2,1)} %backward_first_stage.1), calls=%async_computation.1 | async-start | bytes 131072 | tf_op jit(solution)/shard_map/all_to_all | solution.py:364
  172.2 5.8 %all-to-all-done.1 = bf16[8,32,128]{2,1,0:T(8,128)(2,1)S(1)} async-done(((bf16[8,32,128]{2,1,0:T(8,128)(2,1)}), bf16[8,32,128]{2,1,0:T(8,128)(2,1)S(1)}, u32[]{:S(2)}, u32[]{:S(2)}) %all-to-all-start.1) | async-done | bytes 65568 | tf_op jit(solution)/shard_map/all_to_all | solution.py:364
  178.7 5.7 %all-to-all-start.2 = ((bf16[8,2,32,128]{3,2,1,0:T(8,128)(2,1)}), bf16[8,2,32,128]{3,2,1,0:T(8,128)(2,1)S(1)}, u32[]{:S(2)}, u32[]{:S(2)}) async-start(bf16[8,2,32,128]{3,2,1,0:T(8,128)(2,1)} %broadcast_in_dim.10), calls=%async_computation.2 | async-start | bytes 262144 | tf_op jit(solution)/shard_map/all_to_all | solution.py:369
  184.4 7.9 %all-to-all-done.2 = bf16[8,2,32,128]{3,2,1,0:T(8,128)(2,1)S(1)} async-done(((bf16[8,2,32,128]{3,2,1,0:T(8,128)(2,1)}), bf16[8,2,32,128]{3,2,1,0:T(8,128)(2,1)S(1)}, u32[]{:S(2)}, u32[]{:S(2)}) %all-to-all-start.2) | async-done | bytes 131104 | tf_op jit(solution)/shard_map/all_to_all | solution.py:369
  194.4 3.5 %all-to-all-start.3 = ((f32[16,1,128]{2,1,0:T(1,128)}), f32[16,1,128]{2,1,0:T(1,128)S(1)}, u32[]{:S(2)}, u32[]{:S(2)}) async-start(f32[16,1,128]{2,1,0:T(1,128)} %reshape.96), calls=%async_computation.3 | async-start | bytes 16384 | tf_op jit(solution)/shard_map/all_to_all | solution.py:388
  197.9 7.3 %all-to-all-done.3 = f32[16,1,128]{2,1,0:T(1,128)S(1)} async-done(((f32[16,1,128]{2,1,0:T(1,128)}), f32[16,1,128]{2,1,0:T(1,128)S(1)}, u32[]{:S(2)}, u32[]{:S(2)}) %all-to-all-start.3) | async-done | bytes 8224 | tf_op jit(solution)/shard_map/all_to_all | solution.py:388
  206.5 4.2 %collective-permute-start.16 = (f32[2,16]{1,0:T(2,128)S(1)}, f32[2,16]{1,0:T(2,128)S(1)}, u32[]{:S(2)}, u32[]{:S(2)}) collective-permute-start(f32[2,16]{1,0:T(2,128)S(1)} %bitcast.72), channel_id=1, source_target_pairs={{0,16},{1,17},{2,18},{3,19},{4,20},{5,21},{6,22},{7,23},{8,24},{9,... | collective-permute-start | bytes 392 | tf_op jit(solution)/shard_map/ppermute | solution.py:36
  210.7 6.9 %collective-permute-start.17 = (f32[2,16]{1,0:T(2,128)S(1)}, f32[2,16]{1,0:T(2,128)S(1)}, u32[]{:S(2)}, u32[]{:S(2)}) collective-permute-start(f32[2,16]{1,0:T(2,128)S(1)} %bitcast.71), channel_id=1, source_target_pairs={{0,1},{1,0},{2,3},{3,2},{4,5},{5,4},{6,7},{7,6},{8,9},{9,8},{10,11... | collective-permute-start | bytes 392 | tf_op jit(solution)/shard_map/ppermute | solution.py:36
  (69 shorter events, 20.5 us)
Async XLA Ops:
  0.0 18.1 %copy-start = (bf16[2,512,64]{1,2,0:T(8,128)(2,1)S(1)}, bf16[2,512,64]{1,2,0:T(8,128)(2,1)}, u32[]{:S(2)}) copy-start(bf16[2,512,64]{1,2,0:T(8,128)(2,1)} %param.7) | copy-start | bytes 393220
  2.0 16.1 %copy-start.3 = (bf16[2,512,64]{1,2,0:T(8,128)(2,1)S(1)}, bf16[2,512,64]{1,2,0:T(8,128)(2,1)}, u32[]{:S(2)}) copy-start(bf16[2,512,64]{1,2,0:T(8,128)(2,1)} %param.6) | copy-start | bytes 393220
  2.0 16.2 %collective-permute-start = (bf16[144,1024]{1,0:T(8,128)(2,1)S(1)}, bf16[144,1024]{1,0:T(8,128)(2,1)S(1)}, u32[]{:S(2)}, u32[]{:S(2)}) collective-permute-start(bf16[144,1024]{1,0:T(8,128)(2,1)S(1)} %constant_dynamic-slice_fusion.1), channel_id=1, source_target_pairs={{0,64},{1,65},{2,66},{3,67},{4,68},{5,69},{6,70},{7,71},{8,72},{9,... | collective-permute-start | bytes 884744 | tf_op jit(solution)/shard_map/ppermute | solution.py:36
  6.2 21.6 %collective-permute-start.1 = (bf16[144,1024]{1,0:T(8,128)(2,1)S(1)}, bf16[144,1024]{1,0:T(8,128)(2,1)S(1)}, u32[]{:S(2)}, u32[]{:S(2)}) collective-permute-start(bf16[144,1024]{1,0:T(8,128)(2,1)S(1)} %constant_dynamic-slice_fusion.1), channel_id=1, source_target_pairs={{0,128},{1,129},{2,130},{3,131},{4,132},{5,133},{6,134},{7,135},{8... | collective-permute-start | bytes 884744 | tf_op jit(solution)/shard_map/ppermute | solution.py:36
  10.4 19.4 %collective-permute-start.2 = (bf16[144,1024]{1,0:T(8,128)(2,1)S(1)}, bf16[144,1024]{1,0:T(8,128)(2,1)}, u32[]{:S(2)}, u32[]{:S(2)}) collective-permute-start(bf16[144,1024]{1,0:T(8,128)(2,1)S(1)} %constant_dynamic-slice_fusion.1), channel_id=1, source_target_pairs={{0,192},{1,193},{2,194},{3,195},{4,196},{5,197},{6,198},{7,199},{8... | collective-permute-start | bytes 884744 | tf_op jit(solution)/shard_map/ppermute | solution.py:36
  13.5 20.7 %copy-start.4 = (bf16[1,16,4096]{2,1,0:T(8,128)(2,1)S(1)}, bf16[1,16,4096]{2,1,0:T(8,128)(2,1)}, u32[]{:S(2)}) copy-start(bf16[1,16,4096]{2,1,0:T(8,128)(2,1)} %param.11) | copy-start | bytes 393220
  13.5 24.2 %collective-permute-start.4 = (bf16[576,1024]{1,0:T(8,128)(2,1)S(1)}, bf16[576,1024]{1,0:T(8,128)(2,1)S(1)}, u32[]{:S(2)}, u32[]{:S(2)}) collective-permute-start(bf16[576,1024]{1,0:T(8,128)(2,1)S(1)} %constant_dynamic-slice_fusion), channel_id=1, source_target_pairs={{0,32},{1,49},{2,34},{3,51},{4,36},{5,53},{6,38},{7,55},{8,40},{9,... | collective-permute-start | bytes 3538952 | tf_op jit(solution)/shard_map/ppermute | solution.py:36
  30.9 6.6 %collective-permute-start.3 = (bf16[3,144,1024]{2,1,0:T(8,128)(2,1)S(1)}, bf16[3,144,1024]{2,1,0:T(8,128)(2,1)S(1)}, u32[]{:S(2)}, u32[]{:S(2)}) collective-permute-start(bf16[3,144,1024]{2,1,0:T(8,128)(2,1)S(1)} %get-tuple-element.50), channel_id=1, source_target_pairs={{0,1},{1,0},{2,3},{3,2},{4,5},{5,4},{6,7},{7,6},{8,9},{9,8},{10,11... | collective-permute-start | bytes 2654216 | tf_op jit(solution)/shard_map/ppermute | solution.py:36
  34.3 3.2 %collective-permute-start.5 = (bf16[1,16,4096]{2,1,0:T(8,128)(2,1)S(1)}, bf16[1,16,4096]{2,1,0:T(8,128)(2,1)S(1)}, u32[]{:S(2)}, u32[]{:S(2)}) collective-permute-start(bf16[1,16,4096]{2,1,0:T(8,128)(2,1)S(1)} %copy-done.4), channel_id=1, source_target_pairs={{0,1},{1,0},{2,3},{3,2},{4,5},{5,4},{6,7},{7,6},{8,9},{9,8},{10,11... | collective-permute-start | bytes 393224 | tf_op jit(solution)/shard_map/ppermute | solution.py:36
  37.7 8.5 %copy-start.2 = (bf16[2,3,144,1024]{3,2,1,0:T(8,128)(2,1)}, bf16[2,3,144,1024]{3,2,1,0:T(8,128)(2,1)S(1)}, u32[]{:S(2)}) copy-start(bf16[2,3,144,1024]{3,2,1,0:T(8,128)(2,1)S(1)} %pad_maximum_fusion.1.own) | copy-start | bytes 5308420
  37.7 38.3 %copy-start.6 = (bf16[576,1024]{1,0:T(8,128)(2,1)}, bf16[576,1024]{1,0:T(8,128)(2,1)S(1)}, u32[]{:S(2)}) copy-start(bf16[576,1024]{1,0:T(8,128)(2,1)S(1)} %collective-permute-done.4) | copy-start | bytes 3538948
  37.7 32.9 %collective-permute-start.6 = (bf16[2,3,144,1024]{3,2,1,0:T(8,128)(2,1)S(1)}, bf16[2,3,144,1024]{3,2,1,0:T(8,128)(2,1)}, u32[]{:S(2)}, u32[]{:S(2)}) collective-permute-start(bf16[2,3,144,1024]{3,2,1,0:T(8,128)(2,1)S(1)} %pad_maximum_fusion.1.own), channel_id=1, source_target_pairs={{0,2},{1,15},{2,4},{3,1},{4,6},{5,3},{6,8},{7,5},{8,10},{9,7},{10,... | collective-permute-start | bytes 5308424 | tf_op jit(solution)/shard_map/ppermute | solution.py:36
  46.2 24.5 %collective-permute-start.7 = (bf16[2,3,144,1024]{3,2,1,0:T(8,128)(2,1)S(1)}, bf16[2,3,144,1024]{3,2,1,0:T(8,128)(2,1)S(1)}, u32[]{:S(2)}, u32[]{:S(2)}) collective-permute-start(bf16[2,3,144,1024]{3,2,1,0:T(8,128)(2,1)S(1)} %pad_maximum_fusion.1.own), channel_id=1, source_target_pairs={{0,32},{1,49},{2,34},{3,51},{4,36},{5,53},{6,38},{7,55},{8,40},{9,... | collective-permute-start | bytes 5308424 | tf_op jit(solution)/shard_map/ppermute | solution.py:36
  70.7 1.3 copy-start.5
  71.9 25.1 %collective-permute-start.10 = (bf16[2,3,144,1024]{3,2,1,0:T(8,128)(2,1)}, bf16[2,3,144,1024]{3,2,1,0:T(8,128)(2,1)}, u32[]{:S(2)}, u32[]{:S(2)}) collective-permute-start(bf16[2,3,144,1024]{3,2,1,0:T(8,128)(2,1)} %collective-permute-done.6), channel_id=1, source_target_pairs={{0,32},{1,49},{2,34},{3,51},{4,36},{5,53},{6,38},{7,55},{8,40},{9,... | collective-permute-start | bytes 5308424 | tf_op jit(solution)/shard_map/ppermute | solution.py:36
  76.0 24.1 %collective-permute-start.11 = (bf16[2,3,144,1024]{3,2,1,0:T(8,128)(2,1)}, bf16[2,3,144,1024]{3,2,1,0:T(8,128)(2,1)}, u32[]{:S(2)}, u32[]{:S(2)}) collective-permute-start(bf16[2,3,144,1024]{3,2,1,0:T(8,128)(2,1)} %collective-permute-done.6), channel_id=1, source_target_pairs={{0,2},{1,15},{2,4},{3,1},{4,6},{5,3},{6,8},{7,5},{8,10},{9,7},{10,... | collective-permute-start | bytes 5308424 | tf_op jit(solution)/shard_map/ppermute | solution.py:36
  85.7 17.8 %collective-permute-start.8 = (bf16[8,144,1024]{2,1,0:T(8,128)(2,1)S(1)}, bf16[8,144,1024]{2,1,0:T(8,128)(2,1)S(1)}, u32[]{:S(2)}, u32[]{:S(2)}) collective-permute-start(bf16[8,144,1024]{2,1,0:T(8,128)(2,1)S(1)} %get-tuple-element.34), channel_id=1, source_target_pairs={{0,1},{1,0},{2,3},{3,2},{4,5},{5,4},{6,7},{7,6},{8,9},{9,8},{10,11... | collective-permute-start | bytes 7077896 | tf_op jit(solution)/shard_map/ppermute | solution.py:36
  87.6 15.9 %collective-permute-start.9 = (bf16[8,144,1024]{2,1,0:T(8,128)(2,1)S(1)}, bf16[8,144,1024]{2,1,0:T(8,128)(2,1)S(1)}, u32[]{:S(2)}, u32[]{:S(2)}) collective-permute-start(bf16[8,144,1024]{2,1,0:T(8,128)(2,1)S(1)} %get-tuple-element.35), channel_id=1, source_target_pairs={{0,1},{1,0},{2,3},{3,2},{4,5},{5,4},{6,7},{7,6},{8,9},{9,8},{10,11... | collective-permute-start | bytes 7077896 | tf_op jit(solution)/shard_map/ppermute | solution.py:36
  100.1 6.9 %collective-permute-start.12 = (bf16[2,3,144,1024]{3,2,1,0:T(8,128)(2,1)}, bf16[2,3,144,1024]{3,2,1,0:T(8,128)(2,1)S(1)}, u32[]{:S(2)}, u32[]{:S(2)}) collective-permute-start(bf16[2,3,144,1024]{3,2,1,0:T(8,128)(2,1)} %collective-permute-done.10.turn), channel_id=1, source_target_pairs={{0,1},{1,0},{2,3},{3,2},{4,5},{5,4},{6,7},{7,6},{8,9},{9,8},{10,11... | collective-permute-start | bytes 5308424 | tf_op jit(solution)/shard_map/ppermute | solution.py:36
  110.5 21.9 %copy-start.1 = (bf16[8,1152,1024]{2,1,0:T(8,128)(2,1)}, bf16[8,1152,1024]{2,1,0:T(8,128)(2,1)S(1)}, u32[]{:S(2)}) copy-start(bf16[8,1152,1024]{2,1,0:T(8,128)(2,1)S(1)} %place_late_pieces.1.layers.layers_in) | copy-start | bytes 56623108
  116.2 16.2 %collective-permute-start.13 = (bf16[128,1024]{1,0:T(8,128)(2,1)S(1)}, bf16[128,1024]{1,0:T(8,128)(2,1)S(1)}, u32[]{:S(2)}, u32[]{:S(2)}) collective-permute-start(bf16[128,1024]{1,0:T(8,128)(2,1)S(1)} %get-tuple-element.39), channel_id=1, source_target_pairs={{0,384},{1,385},{2,386},{3,387},{4,388},{5,389},{6,390},{7,391},{8... | collective-permute-start | bytes 786440 | tf_op jit(solution)/shard_map/ppermute | solution.py:36
  121.5 12.8 %collective-permute-start.15 = (bf16[2,16,4096]{2,1,0:T(8,128)(2,1)S(1)}, bf16[2,16,4096]{2,1,0:T(8,128)(2,1)S(1)}, u32[]{:S(2)}, u32[]{:S(2)}) collective-permute-start(bf16[2,16,4096]{2,1,0:T(8,128)(2,1)S(1)} %pad_maximum_fusion.5), channel_id=1, source_target_pairs={{0,16},{1,17},{2,18},{3,19},{4,20},{5,21},{6,22},{7,23},{8,24},{9,... | collective-permute-start | bytes 786440 | tf_op jit(solution)/shard_map/ppermute | solution.py:36
  133.0 23.5 %collective-permute-start.14 = (bf16[128,1024]{1,0:T(8,128)(2,1)S(1)}, bf16[128,1024]{1,0:T(8,128)(2,1)S(1)}, u32[]{:S(2)}, u32[]{:S(2)}) collective-permute-start(bf16[128,1024]{1,0:T(8,128)(2,1)S(1)} %get-tuple-element.40), channel_id=1, source_target_pairs={{256,128},{257,129},{258,130},{259,131},{260,132},{261,133},{262,1... | collective-permute-start | bytes 786440 | tf_op jit(solution)/shard_map/ppermute | solution.py:36
  167.3 10.6 %all-to-all-start.1 = ((bf16[8,32,128]{2,1,0:T(8,128)(2,1)}), bf16[8,32,128]{2,1,0:T(8,128)(2,1)S(1)}, u32[]{:S(2)}, u32[]{:S(2)}) async-start(bf16[8,32,128]{2,1,0:T(8,128)(2,1)} %backward_first_stage.1), calls=%async_computation.1 | async-start | bytes 131072 | tf_op jit(solution)/shard_map/all_to_all | solution.py:364
  178.7 13.7 %all-to-all-start.2 = ((bf16[8,2,32,128]{3,2,1,0:T(8,128)(2,1)}), bf16[8,2,32,128]{3,2,1,0:T(8,128)(2,1)S(1)}, u32[]{:S(2)}, u32[]{:S(2)}) async-start(bf16[8,2,32,128]{3,2,1,0:T(8,128)(2,1)} %broadcast_in_dim.10), calls=%async_computation.2 | async-start | bytes 262144 | tf_op jit(solution)/shard_map/all_to_all | solution.py:369
  194.4 10.8 %all-to-all-start.3 = ((f32[16,1,128]{2,1,0:T(1,128)}), f32[16,1,128]{2,1,0:T(1,128)S(1)}, u32[]{:S(2)}, u32[]{:S(2)}) async-start(f32[16,1,128]{2,1,0:T(1,128)} %reshape.96), calls=%async_computation.3 | async-start | bytes 16384 | tf_op jit(solution)/shard_map/all_to_all | solution.py:388
  206.5 12.4 %collective-permute-start.16 = (f32[2,16]{1,0:T(2,128)S(1)}, f32[2,16]{1,0:T(2,128)S(1)}, u32[]{:S(2)}, u32[]{:S(2)}) collective-permute-start(f32[2,16]{1,0:T(2,128)S(1)} %bitcast.72), channel_id=1, source_target_pairs={{0,16},{1,17},{2,18},{3,19},{4,20},{5,21},{6,22},{7,23},{8,24},{9,... | collective-permute-start | bytes 392 | tf_op jit(solution)/shard_map/ppermute | solution.py:36
  210.7 8.2 %collective-permute-start.17 = (f32[2,16]{1,0:T(2,128)S(1)}, f32[2,16]{1,0:T(2,128)S(1)}, u32[]{:S(2)}, u32[]{:S(2)}) collective-permute-start(f32[2,16]{1,0:T(2,128)S(1)} %bitcast.71), channel_id=1, source_target_pairs={{0,1},{1,0},{2,3},{3,2},{4,5},{5,4},{6,7},{7,6},{8,9},{9,8},{10,11... | collective-permute-start | bytes 392 | tf_op jit(solution)/shard_map/ppermute | solution.py:36
  217.6 2.0 collective-permute-start.18

commit v4 on v3

--- a/solution.py
+++ b/solution.py
@@ -382,28 +382,16 @@
     table = jnp.where(x_hi == 0, table, table[:, ::-1])
     table = jnp.where(core == 0, table, table[:, :, ::-1]).reshape(8, 2, -1)
 
+    table = table.reshape(8, 2, 4, -1).transpose(0, 2, 1, 3)
     outgoing = lax.dynamic_update_slice_in_dim(
         jnp.zeros((16,) + table.shape[1:], jnp.float32), table, x_hi * 8, 0
-    )
-    scores = lax.all_to_all(outgoing, "section", 0, 0, tiled=True).sum(0)
-    scores = scores.reshape(2, 2, 2, -1).transpose(1, 2, 0, 3)
-
-    def part(far, other):
-        value = jnp.where((x_hi ^ far) == 0, scores[0], scores[1])
-        return jnp.where((core ^ other) == 0, value[0], value[1])
-
-    def send(far, other):
-        def target(x, y, z, c):
-            holder = x // 2 == (y % 8 * 2 + x % 2) // 8
-            return (x ^ 2 if far else x, y, z, c ^ other) if holder else None
-
-        return move(part(far, other), target)
-
-    near, across, diagonal = send(0, 1), send(1, 0), send(1, 1)
-    holds = x_hi == section // 8
-    mine = jnp.where(holds, part(0, 0), across)
-    theirs = jnp.where(holds, near, diagonal)
-    return jnp.where(core == 0, jnp.concatenate([mine, theirs]), jnp.concatenate([theirs, mine]))
+    ).reshape(64, -1)
+    plane = [
+        [s * 32 + (h * 8 + k) * 2 + c for s in range(16) for h in range(2) for c in range(2)]
+        for k in range(8)
+    ]
+    scores = lax.all_to_all(outgoing, AXES, 0, 0, tiled=True, axis_index_groups=plane)
+    return scores.reshape(32, 4, -1).sum(0).reshape(4, -1)
 
 
 def solution(mesh):

time: 221 us -> 214 us (0.968)
  blocking collectives: 22.5 us -> 39.8 us
  starting transfers between devices: 86.9 us -> 71 us
  waiting for transfers between devices: 74.8 us -> 66.8 us
    all_to_all x0 -> x1, blocking collectives: none -> 17.2 us  [on_device(): lax.all_to_all(outgoing, AXES, 0, 0, tiled=True, axis_index_groups=plane)]
    ppermute x19 -> x16, starting transfers between devices: 72.8 us -> 60.5 us  [move(): return lax.ppermute(value, AXES, pairs(target))]
    all_to_all x1 -> x0, waiting for transfers between devices: 7.26 us -> none  [on_device(): scores = lax.all_to_all(outgoing, 'section', 0, 0, tiled=True).sum(0)]
    all_to_all x1 -> x0, starting transfers between devices: 3.5 us -> none  [on_device(): scores = lax.all_to_all(outgoing, 'section', 0, 0, tiled=True).sum(0)]
    ppermute x19 -> x16, waiting for transfers between devices: 53.9 us -> 53.1 us  [move(): return lax.ppermute(value, AXES, pairs(target))]
  transfers between devices with their start and end apart: 22 -> 18, of which waited for: 12 -> 10; matrix products, arithmetic and copies ran while one was open for 1% -> 1% of each run, Pallas kernels for 3% -> 3%
where the time goes in v4:
time: 214 us; the launch traced here: 213 us
  starting transfers between devices  71 us (33%)
  waiting for transfers between devices  66.8 us (31%)
  blocking collectives  39.8 us (19%)
  Pallas kernels  25.8 us (12%)
  other arithmetic  4.73 us (2%)
  local copies, waits for them, and re-layouts  3.45 us (2%)
    ppermute x16, starting transfers between devices, move(): return lax.ppermute(value, AXES, pairs(target))  60.5 us
    ppermute x16, waiting for transfers between devices, move(): return lax.ppermute(value, AXES, pairs(target))  53.1 us
    all_to_all x1, blocking collectives, on_device(): arrived = lax.all_to_all(order, 'section', 0, 0, tiled=True)  22.5 us
    all_to_all x1, blocking collectives, on_device(): lax.all_to_all(outgoing, AXES, 0, 0, tiled=True, axis_index_groups=plane)  17.2 us
    pallas_call x1, Pallas kernels, on_device(): pl.pallas_call(last_kernel, out_shape=FACTOR, in_specs=[SMEM, VMEM, HBM,...  10.8 us
    all_to_all x1, waiting for transfers between devices, on_device(): lax.all_to_all(jnp.broadcast_to(sums[None], (8,) + sums.shape), 'dp', 0,...  7.93 us
    all_to_all x1, waiting for transfers between devices, on_device(): lax.all_to_all(factor, 'section', 0, 0, tiled=True, axis_index_groups=gro...  5.76 us
    pallas_call x1, Pallas kernels, on_device(): pl.pallas_call(first_kernel, out_shape=(TOKENS, SLOPE, LEFT), in_specs=[S...  5.75 us
  transfers between devices with their start and end apart: 18, of which 10 were waited for; matrix products, arithmetic and copies ran while one was open for 1% of the time, Pallas kernels for 3%

profile of v4, /device:TPU:1, one launch (start us, length us, event | category | flops | bytes accessed | tf_op | source)
XLA Modules:
  0.0 212.9 jit_solution(17635324986908002295)
XLA Ops:
  0.0 2.0 pad_maximum_fusion.pack
  2.0 4.2 %collective-permute-start = (bf16[144,1024]{1,0:T(8,128)(2,1)S(1)}, bf16[144,1024]{1,0:T(8,128)(2,1)S(1)}, u32[]{:S(2)}, u32[]{:S(2)}) collective-permute-start(bf16[144,1024]{1,0:T(8,128)(2,1)S(1)} %constant_dynamic-slice_fusion.1), channel_id=1, source_target_pairs={{0,64},{1,65},{2,66},{3,67},{4,68},{5,69},{6,70},{7,71},{8,72},{9,... | collective-permute-start | bytes 884744 | tf_op jit(solution)/shard_map/ppermute | solution.py:36
  6.2 4.2 %collective-permute-start.1 = (bf16[144,1024]{1,0:T(8,128)(2,1)S(1)}, bf16[144,1024]{1,0:T(8,128)(2,1)S(1)}, u32[]{:S(2)}, u32[]{:S(2)}) collective-permute-start(bf16[144,1024]{1,0:T(8,128)(2,1)S(1)} %constant_dynamic-slice_fusion.1), channel_id=1, source_target_pairs={{0,128},{1,129},{2,130},{3,131},{4,132},{5,133},{6,134},{7,135},{8... | collective-permute-start | bytes 884744 | tf_op jit(solution)/shard_map/ppermute | solution.py:36
  10.4 3.0 %collective-permute-start.2 = (bf16[144,1024]{1,0:T(8,128)(2,1)S(1)}, bf16[144,1024]{1,0:T(8,128)(2,1)}, u32[]{:S(2)}, u32[]{:S(2)}) collective-permute-start(bf16[144,1024]{1,0:T(8,128)(2,1)S(1)} %constant_dynamic-slice_fusion.1), channel_id=1, source_target_pairs={{0,192},{1,193},{2,194},{3,195},{4,196},{5,197},{6,198},{7,199},{8... | collective-permute-start | bytes 884744 | tf_op jit(solution)/shard_map/ppermute | solution.py:36
  13.5 4.5 %collective-permute-start.4 = (bf16[576,1024]{1,0:T(8,128)(2,1)S(1)}, bf16[576,1024]{1,0:T(8,128)(2,1)S(1)}, u32[]{:S(2)}, u32[]{:S(2)}) collective-permute-start(bf16[576,1024]{1,0:T(8,128)(2,1)S(1)} %constant_dynamic-slice_fusion), channel_id=1, source_target_pairs={{0,32},{1,49},{2,34},{3,51},{4,36},{5,53},{6,38},{7,55},{8,40},{9,... | collective-permute-start | bytes 3538952 | tf_op jit(solution)/shard_map/ppermute | solution.py:36
  18.2 9.6 %collective-permute-done.1 = bf16[144,1024]{1,0:T(8,128)(2,1)S(1)} collective-permute-done((bf16[144,1024]{1,0:T(8,128)(2,1)S(1)}, bf16[144,1024]{1,0:T(8,128)(2,1)S(1)}, u32[]{:S(2)}, u32[]{:S(2)}) %collective-permute-start.1) | collective-permute-done | bytes 294944 | tf_op jit(solution)/shard_map/ppermute | solution.py:36
  27.8 2.0 collective-permute-done.2
  30.9 3.3 %collective-permute-start.3 = (bf16[3,144,1024]{2,1,0:T(8,128)(2,1)S(1)}, bf16[3,144,1024]{2,1,0:T(8,128)(2,1)S(1)}, u32[]{:S(2)}, u32[]{:S(2)}) collective-permute-start(bf16[3,144,1024]{2,1,0:T(8,128)(2,1)S(1)} %get-tuple-element.50), channel_id=1, source_target_pairs={{0,1},{1,0},{2,3},{3,2},{4,5},{5,4},{6,7},{7,6},{8,9},{9,8},{10,11... | collective-permute-start | bytes 2654216 | tf_op jit(solution)/shard_map/ppermute | solution.py:36
  37.7 8.4 %collective-permute-start.6 = (bf16[2,3,144,1024]{3,2,1,0:T(8,128)(2,1)S(1)}, bf16[2,3,144,1024]{3,2,1,0:T(8,128)(2,1)}, u32[]{:S(2)}, u32[]{:S(2)}) collective-permute-start(bf16[2,3,144,1024]{3,2,1,0:T(8,128)(2,1)S(1)} %pad_maximum_fusion.1.own), channel_id=1, source_target_pairs={{0,2},{1,15},{2,4},{3,1},{4,6},{5,3},{6,8},{7,5},{8,10},{9,7},{10,... | collective-permute-start | bytes 5308424 | tf_op jit(solution)/shard_map/ppermute | solution.py:36
  46.2 1.9 collective-permute-start.7
  48.1 22.5 %all_to_all.24.arrived = bf16[16,64,128]{2,1,0:T(8,128)(2,1)S(1)} all-to-all(bf16[16,64,128]{2,1,0:T(8,128)(2,1)S(1)} %pad_maximum_fusion.4), channel_id=1, replica_groups=mesh['section'=16,'dp'=32] {'section'}, dimensions={0} | all-to-all | bytes 524288 | tf_op jit(solution)/shard_map/all_to_all | solution.py:280
  72.0 4.1 %collective-permute-start.10 = (bf16[2,3,144,1024]{3,2,1,0:T(8,128)(2,1)}, bf16[2,3,144,1024]{3,2,1,0:T(8,128)(2,1)}, u32[]{:S(2)}, u32[]{:S(2)}) collective-permute-start(bf16[2,3,144,1024]{3,2,1,0:T(8,128)(2,1)} %collective-permute-done.6), channel_id=1, source_target_pairs={{0,32},{1,49},{2,34},{3,51},{4,36},{5,53},{6,38},{7,55},{8,40},{9,... | collective-permute-start | bytes 5308424 | tf_op jit(solution)/shard_map/ppermute | solution.py:36
  76.0 4.3 %collective-permute-start.11 = (bf16[2,3,144,1024]{3,2,1,0:T(8,128)(2,1)}, bf16[2,3,144,1024]{3,2,1,0:T(8,128)(2,1)}, u32[]{:S(2)}, u32[]{:S(2)}) collective-permute-start(bf16[2,3,144,1024]{3,2,1,0:T(8,128)(2,1)} %collective-permute-done.6), channel_id=1, source_target_pairs={{0,2},{1,15},{2,4},{3,1},{4,6},{5,3},{6,8},{7,5},{8,10},{9,7},{10,... | collective-permute-start | bytes 5308424 | tf_op jit(solution)/shard_map/ppermute | solution.py:36
  80.5 5.2 %place_early_pieces.1 = (bf16[8,1152,1024]{2,1,0:T(8,128)(2,1)S(1)}, bf16[8,144,1024]{2,1,0:T(8,128)(2,1)S(1)}, bf16[8,144,1024]{2,1,0:T(8,128)(2,1)S(1)}) custom-call(s32[6]{0:T(128)S(1)} %stack.53.place, bf16[1152,1024]{1,0:T(8,128)(2,1)S(1)} %pad_maximum_fusion.pack, bf16[4,144,1024]{2,1,0:T(8,128)(2,1)} %bitcast.70, bf16[2,3,144,1024]{3,2,1,0:T(8,128)(2,1)} %copy-done.2, ...), custom_call_target="tpu_custom_call" | custom-call | flops 2415919104 | bytes 18874368 | tf_op jit(solution)/shard_map/place_early_pieces/pallas_call | solution.py:290
  85.7 1.9 collective-permute-start.8
  87.7 2.4 %collective-permute-start.9 = (bf16[8,144,1024]{2,1,0:T(8,128)(2,1)S(1)}, bf16[8,144,1024]{2,1,0:T(8,128)(2,1)S(1)}, u32[]{:S(2)}, u32[]{:S(2)}) collective-permute-start(bf16[8,144,1024]{2,1,0:T(8,128)(2,1)S(1)} %get-tuple-element.35), channel_id=1, source_target_pairs={{0,1},{1,0},{2,3},{3,2},{4,5},{5,4},{6,7},{7,6},{8,9},{9,8},{10,11... | collective-permute-start | bytes 7077896 | tf_op jit(solution)/shard_map/ppermute | solution.py:36
  90.1 7.0 %collective-permute-done.10.turn = bf16[2,3,144,1024]{3,2,1,0:T(8,128)(2,1)} collective-permute-done((bf16[2,3,144,1024]{3,2,1,0:T(8,128)(2,1)}, bf16[2,3,144,1024]{3,2,1,0:T(8,128)(2,1)}, u32[]{:S(2)}, u32[]{:S(2)}) %collective-permute-start.10) | collective-permute-done | bytes 1769504 | tf_op jit(solution)/shard_map/ppermute | solution.py:36
  97.0 3.1 %collective-permute-done.11.two = bf16[2,3,144,1024]{3,2,1,0:T(8,128)(2,1)} collective-permute-done((bf16[2,3,144,1024]{3,2,1,0:T(8,128)(2,1)}, bf16[2,3,144,1024]{3,2,1,0:T(8,128)(2,1)}, u32[]{:S(2)}, u32[]{:S(2)}) %collective-permute-start.11) | collective-permute-done | bytes 1769504 | tf_op jit(solution)/shard_map/ppermute | solution.py:36
  100.1 3.4 %collective-permute-start.12 = (bf16[2,3,144,1024]{3,2,1,0:T(8,128)(2,1)}, bf16[2,3,144,1024]{3,2,1,0:T(8,128)(2,1)S(1)}, u32[]{:S(2)}, u32[]{:S(2)}) collective-permute-start(bf16[2,3,144,1024]{3,2,1,0:T(8,128)(2,1)} %collective-permute-done.10.turn), channel_id=1, source_target_pairs={{0,1},{1,0},{2,3},{3,2},{4,5},{5,4},{6,7},{7,6},{8,9},{9,8},{10,11... | collective-permute-start | bytes 5308424 | tf_op jit(solution)/shard_map/ppermute | solution.py:36
  103.6 3.5 %collective-permute-done.12.turn_other = bf16[2,3,144,1024]{3,2,1,0:T(8,128)(2,1)S(1)} collective-permute-done((bf16[2,3,144,1024]{3,2,1,0:T(8,128)(2,1)}, bf16[2,3,144,1024]{3,2,1,0:T(8,128)(2,1)S(1)}, u32[]{:S(2)}, u32[]{:S(2)}) %collective-permute-start.12) | collective-permute-done | bytes 1769504 | tf_op jit(solution)/shard_map/ppermute | solution.py:36
  107.0 3.5 %place_late_pieces.1.layers.layers_in = bf16[8,1152,1024]{2,1,0:T(8,128)(2,1)S(1)} custom-call(s32[6]{0:T(128)S(1)} %stack.53.place, bf16[8,144,1024]{2,1,0:T(8,128)(2,1)S(1)} %collective-permute-done.8.first, bf16[8,144,1024]{2,1,0:T(8,128)(2,1)S(1)} %collective-permute-done.9.second, ...), custom_call_target="tpu_custom_call", output_to_operand_aliasing={{}: (6, {})} | custom-call | tf_op jit(solution)/shard_map/place_late_pieces/pallas_call | solution.py:310
  110.5 5.7 %forward_first_stage.1 = (bf16[128,1024]{1,0:T(8,128)(2,1)S(1)}, f32[8,128,1024]{2,1,0:T(8,128)S(1)}, f32[8,128,128]{2,1,0:T(8,128)S(1)}) custom-call(s32[6]{0:T(128)S(1)} %stack.53.place, bf16[16,64,128]{2,1,0:T(8,128)(2,1)S(1)} %all_to_all.24.arrived, bf16[8,1152,1024]{2,1,0:T(8,128)(2,1)S(1)} %place_late_pieces.1.layers.layers_in), custom_call_target="tpu_custom_call" | custom-call | flops 2415919104 | bytes 18874368 | tf_op jit(solution)/shard_map/forward_first_stage/pallas_call | solution.py:321
  116.3 5.3 %collective-permute-start.13 = (bf16[128,1024]{1,0:T(8,128)(2,1)S(1)}, bf16[128,1024]{1,0:T(8,128)(2,1)S(1)}, u32[]{:S(2)}, u32[]{:S(2)}) collective-permute-start(bf16[128,1024]{1,0:T(8,128)(2,1)S(1)} %get-tuple-element.39), channel_id=1, source_target_pairs={{0,384},{1,385},{2,386},{3,387},{4,388},{5,389},{6,390},{7,391},{8... | collective-permute-start | bytes 786440 | tf_op jit(solution)/shard_map/ppermute | solution.py:36
  121.5 6.4 %collective-permute-start.15 = (bf16[2,16,4096]{2,1,0:T(8,128)(2,1)S(1)}, bf16[2,16,4096]{2,1,0:T(8,128)(2,1)S(1)}, u32[]{:S(2)}, u32[]{:S(2)}) collective-permute-start(bf16[2,16,4096]{2,1,0:T(8,128)(2,1)S(1)} %pad_maximum_fusion.5), channel_id=1, source_target_pairs={{0,16},{1,17},{2,18},{3,19},{4,20},{5,21},{6,22},{7,23},{8,24},{9,... | collective-permute-start | bytes 786440 | tf_op jit(solution)/shard_map/ppermute | solution.py:36
  127.9 4.5 %collective-permute-done.13.hidden = bf16[128,1024]{1,0:T(8,128)(2,1)S(1)} collective-permute-done((bf16[128,1024]{1,0:T(8,128)(2,1)S(1)}, bf16[128,1024]{1,0:T(8,128)(2,1)S(1)}, u32[]{:S(2)}, u32[]{:S(2)}) %collective-permute-start.13) | collective-permute-done | bytes 262176 | tf_op jit(solution)/shard_map/ppermute | solution.py:36
  134.4 22.1 %collective-permute-done.14.upstream = bf16[128,1024]{1,0:T(8,128)(2,1)S(1)} collective-permute-done((bf16[128,1024]{1,0:T(8,128)(2,1)S(1)}, bf16[128,1024]{1,0:T(8,128)(2,1)S(1)}, u32[]{:S(2)}, u32[]{:S(2)}) %collective-permute-start.14) | collective-permute-done | bytes 262176 | tf_op jit(solution)/shard_map/ppermute | solution.py:36
  156.5 10.8 %backward_first_stage.1 = bf16[8,32,128]{2,1,0:T(8,128)(2,1)} custom-call(s32[6]{0:T(128)S(1)} %stack.53.place, bf16[128,1024]{1,0:T(8,128)(2,1)S(1)} %collective-permute-done.14.upstream, f32[8,128,1024]{2,1,0:T(8,128)S(1)} %get-tuple-element.45.slope_in, f32[8,128,128]{2,1,0:T(8,128)S(1)} %get-tuple-element.46.left, ...), custom_call_target="tpu_custom_call" | custom-call | flops 2415919104 | bytes 18874368 | tf_op jit(solution)/shard_map/backward_first_stage/pallas_call | solution.py:346
  167.3 4.9 %all-to-all-start.1 = ((bf16[8,32,128]{2,1,0:T(8,128)(2,1)}), bf16[8,32,128]{2,1,0:T(8,128)(2,1)S(1)}, u32[]{:S(2)}, u32[]{:S(2)}) async-start(bf16[8,32,128]{2,1,0:T(8,128)(2,1)} %backward_first_stage.1), calls=%async_computation.1 | async-start | bytes 131072 | tf_op jit(solution)/shard_map/all_to_all | solution.py:364
  172.2 5.8 %all-to-all-done.1 = bf16[8,32,128]{2,1,0:T(8,128)(2,1)S(1)} async-done(((bf16[8,32,128]{2,1,0:T(8,128)(2,1)}), bf16[8,32,128]{2,1,0:T(8,128)(2,1)S(1)}, u32[]{:S(2)}, u32[]{:S(2)}) %all-to-all-start.1) | async-done | bytes 65568 | tf_op jit(solution)/shard_map/all_to_all | solution.py:364
  178.7 5.7 %all-to-all-start.2 = ((bf16[8,2,32,128]{3,2,1,0:T(8,128)(2,1)}), bf16[8,2,32,128]{3,2,1,0:T(8,128)(2,1)S(1)}, u32[]{:S(2)}, u32[]{:S(2)}) async-start(bf16[8,2,32,128]{3,2,1,0:T(8,128)(2,1)} %broadcast_in_dim.10), calls=%async_computation.2 | async-start | bytes 262144 | tf_op jit(solution)/shard_map/all_to_all | solution.py:369
  184.4 7.9 %all-to-all-done.2 = bf16[8,2,32,128]{3,2,1,0:T(8,128)(2,1)S(1)} async-done(((bf16[8,2,32,128]{3,2,1,0:T(8,128)(2,1)}), bf16[8,2,32,128]{3,2,1,0:T(8,128)(2,1)S(1)}, u32[]{:S(2)}, u32[]{:S(2)}) %all-to-all-start.2) | async-done | bytes 131104 | tf_op jit(solution)/shard_map/all_to_all | solution.py:369
  193.7 17.2 %all_to_all.25 = f32[64,1,32]{2,1,0:T(1,128)S(1)} all-to-all(f32[64,1,32]{2,1,0:T(1,128)S(1)} %bitcast.67), channel_id=1, replica_groups={{0,1,16,17,32,33,48,49,64,65,80,81,96,97,112,113,128,129,144,145,160,16..., dimensions={0} | all-to-all | bytes 16384 | tf_op jit(solution)/shard_map/all_to_all | solution.py:393
  (54 shorter events, 12.0 us)
Async XLA Ops:
  0.0 18.1 %copy-start = (bf16[2,512,64]{1,2,0:T(8,128)(2,1)S(1)}, bf16[2,512,64]{1,2,0:T(8,128)(2,1)}, u32[]{:S(2)}) copy-start(bf16[2,512,64]{1,2,0:T(8,128)(2,1)} %param.7) | copy-start | bytes 393220
  2.0 16.1 %copy-start.3 = (bf16[2,512,64]{1,2,0:T(8,128)(2,1)S(1)}, bf16[2,512,64]{1,2,0:T(8,128)(2,1)}, u32[]{:S(2)}) copy-start(bf16[2,512,64]{1,2,0:T(8,128)(2,1)} %param.6) | copy-start | bytes 393220
  2.0 16.2 %collective-permute-start = (bf16[144,1024]{1,0:T(8,128)(2,1)S(1)}, bf16[144,1024]{1,0:T(8,128)(2,1)S(1)}, u32[]{:S(2)}, u32[]{:S(2)}) collective-permute-start(bf16[144,1024]{1,0:T(8,128)(2,1)S(1)} %constant_dynamic-slice_fusion.1), channel_id=1, source_target_pairs={{0,64},{1,65},{2,66},{3,67},{4,68},{5,69},{6,70},{7,71},{8,72},{9,... | collective-permute-start | bytes 884744 | tf_op jit(solution)/shard_map/ppermute | solution.py:36
  6.2 21.6 %collective-permute-start.1 = (bf16[144,1024]{1,0:T(8,128)(2,1)S(1)}, bf16[144,1024]{1,0:T(8,128)(2,1)S(1)}, u32[]{:S(2)}, u32[]{:S(2)}) collective-permute-start(bf16[144,1024]{1,0:T(8,128)(2,1)S(1)} %constant_dynamic-slice_fusion.1), channel_id=1, source_target_pairs={{0,128},{1,129},{2,130},{3,131},{4,132},{5,133},{6,134},{7,135},{8... | collective-permute-start | bytes 884744 | tf_op jit(solution)/shard_map/ppermute | solution.py:36
  10.4 19.4 %collective-permute-start.2 = (bf16[144,1024]{1,0:T(8,128)(2,1)S(1)}, bf16[144,1024]{1,0:T(8,128)(2,1)}, u32[]{:S(2)}, u32[]{:S(2)}) collective-permute-start(bf16[144,1024]{1,0:T(8,128)(2,1)S(1)} %constant_dynamic-slice_fusion.1), channel_id=1, source_target_pairs={{0,192},{1,193},{2,194},{3,195},{4,196},{5,197},{6,198},{7,199},{8... | collective-permute-start | bytes 884744 | tf_op jit(solution)/shard_map/ppermute | solution.py:36
  13.5 20.7 %copy-start.4 = (bf16[1,16,4096]{2,1,0:T(8,128)(2,1)S(1)}, bf16[1,16,4096]{2,1,0:T(8,128)(2,1)}, u32[]{:S(2)}) copy-start(bf16[1,16,4096]{2,1,0:T(8,128)(2,1)} %param.11) | copy-start | bytes 393220
  13.5 24.2 %collective-permute-start.4 = (bf16[576,1024]{1,0:T(8,128)(2,1)S(1)}, bf16[576,1024]{1,0:T(8,128)(2,1)S(1)}, u32[]{:S(2)}, u32[]{:S(2)}) collective-permute-start(bf16[576,1024]{1,0:T(8,128)(2,1)S(1)} %constant_dynamic-slice_fusion), channel_id=1, source_target_pairs={{0,32},{1,49},{2,34},{3,51},{4,36},{5,53},{6,38},{7,55},{8,40},{9,... | collective-permute-start | bytes 3538952 | tf_op jit(solution)/shard_map/ppermute | solution.py:36
  30.9 6.6 %collective-permute-start.3 = (bf16[3,144,1024]{2,1,0:T(8,128)(2,1)S(1)}, bf16[3,144,1024]{2,1,0:T(8,128)(2,1)S(1)}, u32[]{:S(2)}, u32[]{:S(2)}) collective-permute-start(bf16[3,144,1024]{2,1,0:T(8,128)(2,1)S(1)} %get-tuple-element.50), channel_id=1, source_target_pairs={{0,1},{1,0},{2,3},{3,2},{4,5},{5,4},{6,7},{7,6},{8,9},{9,8},{10,11... | collective-permute-start | bytes 2654216 | tf_op jit(solution)/shard_map/ppermute | solution.py:36
  34.3 3.2 %collective-permute-start.5 = (bf16[1,16,4096]{2,1,0:T(8,128)(2,1)S(1)}, bf16[1,16,4096]{2,1,0:T(8,128)(2,1)S(1)}, u32[]{:S(2)}, u32[]{:S(2)}) collective-permute-start(bf16[1,16,4096]{2,1,0:T(8,128)(2,1)S(1)} %copy-done.4), channel_id=1, source_target_pairs={{0,1},{1,0},{2,3},{3,2},{4,5},{5,4},{6,7},{7,6},{8,9},{9,8},{10,11... | collective-permute-start | bytes 393224 | tf_op jit(solution)/shard_map/ppermute | solution.py:36
  37.7 8.5 %copy-start.2 = (bf16[2,3,144,1024]{3,2,1,0:T(8,128)(2,1)}, bf16[2,3,144,1024]{3,2,1,0:T(8,128)(2,1)S(1)}, u32[]{:S(2)}) copy-start(bf16[2,3,144,1024]{3,2,1,0:T(8,128)(2,1)S(1)} %pad_maximum_fusion.1.own) | copy-start | bytes 5308420
  37.7 38.3 %copy-start.6 = (bf16[576,1024]{1,0:T(8,128)(2,1)}, bf16[576,1024]{1,0:T(8,128)(2,1)S(1)}, u32[]{:S(2)}) copy-start(bf16[576,1024]{1,0:T(8,128)(2,1)S(1)} %collective-permute-done.4) | copy-start | bytes 3538948
  37.7 32.9 %collective-permute-start.6 = (bf16[2,3,144,1024]{3,2,1,0:T(8,128)(2,1)S(1)}, bf16[2,3,144,1024]{3,2,1,0:T(8,128)(2,1)}, u32[]{:S(2)}, u32[]{:S(2)}) collective-permute-start(bf16[2,3,144,1024]{3,2,1,0:T(8,128)(2,1)S(1)} %pad_maximum_fusion.1.own), channel_id=1, source_target_pairs={{0,2},{1,15},{2,4},{3,1},{4,6},{5,3},{6,8},{7,5},{8,10},{9,7},{10,... | collective-permute-start | bytes 5308424 | tf_op jit(solution)/shard_map/ppermute | solution.py:36
  46.2 24.5 %collective-permute-start.7 = (bf16[2,3,144,1024]{3,2,1,0:T(8,128)(2,1)S(1)}, bf16[2,3,144,1024]{3,2,1,0:T(8,128)(2,1)S(1)}, u32[]{:S(2)}, u32[]{:S(2)}) collective-permute-start(bf16[2,3,144,1024]{3,2,1,0:T(8,128)(2,1)S(1)} %pad_maximum_fusion.1.own), channel_id=1, source_target_pairs={{0,32},{1,49},{2,34},{3,51},{4,36},{5,53},{6,38},{7,55},{8,40},{9,... | collective-permute-start | bytes 5308424 | tf_op jit(solution)/shard_map/ppermute | solution.py:36
  70.7 1.3 copy-start.5
  72.0 25.1 %collective-permute-start.10 = (bf16[2,3,144,1024]{3,2,1,0:T(8,128)(2,1)}, bf16[2,3,144,1024]{3,2,1,0:T(8,128)(2,1)}, u32[]{:S(2)}, u32[]{:S(2)}) collective-permute-start(bf16[2,3,144,1024]{3,2,1,0:T(8,128)(2,1)} %collective-permute-done.6), channel_id=1, source_target_pairs={{0,32},{1,49},{2,34},{3,51},{4,36},{5,53},{6,38},{7,55},{8,40},{9,... | collective-permute-start | bytes 5308424 | tf_op jit(solution)/shard_map/ppermute | solution.py:36
  76.0 24.1 %collective-permute-start.11 = (bf16[2,3,144,1024]{3,2,1,0:T(8,128)(2,1)}, bf16[2,3,144,1024]{3,2,1,0:T(8,128)(2,1)}, u32[]{:S(2)}, u32[]{:S(2)}) collective-permute-start(bf16[2,3,144,1024]{3,2,1,0:T(8,128)(2,1)} %collective-permute-done.6), channel_id=1, source_target_pairs={{0,2},{1,15},{2,4},{3,1},{4,6},{5,3},{6,8},{7,5},{8,10},{9,7},{10,... | collective-permute-start | bytes 5308424 | tf_op jit(solution)/shard_map/ppermute | solution.py:36
  85.7 17.8 %collective-permute-start.8 = (bf16[8,144,1024]{2,1,0:T(8,128)(2,1)S(1)}, bf16[8,144,1024]{2,1,0:T(8,128)(2,1)S(1)}, u32[]{:S(2)}, u32[]{:S(2)}) collective-permute-start(bf16[8,144,1024]{2,1,0:T(8,128)(2,1)S(1)} %get-tuple-element.34), channel_id=1, source_target_pairs={{0,1},{1,0},{2,3},{3,2},{4,5},{5,4},{6,7},{7,6},{8,9},{9,8},{10,11... | collective-permute-start | bytes 7077896 | tf_op jit(solution)/shard_map/ppermute | solution.py:36
  87.7 15.9 %collective-permute-start.9 = (bf16[8,144,1024]{2,1,0:T(8,128)(2,1)S(1)}, bf16[8,144,1024]{2,1,0:T(8,128)(2,1)S(1)}, u32[]{:S(2)}, u32[]{:S(2)}) collective-permute-start(bf16[8,144,1024]{2,1,0:T(8,128)(2,1)S(1)} %get-tuple-element.35), channel_id=1, source_target_pairs={{0,1},{1,0},{2,3},{3,2},{4,5},{5,4},{6,7},{7,6},{8,9},{9,8},{10,11... | collective-permute-start | bytes 7077896 | tf_op jit(solution)/shard_map/ppermute | solution.py:36
  100.1 6.9 %collective-permute-start.12 = (bf16[2,3,144,1024]{3,2,1,0:T(8,128)(2,1)}, bf16[2,3,144,1024]{3,2,1,0:T(8,128)(2,1)S(1)}, u32[]{:S(2)}, u32[]{:S(2)}) collective-permute-start(bf16[2,3,144,1024]{3,2,1,0:T(8,128)(2,1)} %collective-permute-done.10.turn), channel_id=1, source_target_pairs={{0,1},{1,0},{2,3},{3,2},{4,5},{5,4},{6,7},{7,6},{8,9},{9,8},{10,11... | collective-permute-start | bytes 5308424 | tf_op jit(solution)/shard_map/ppermute | solution.py:36
  110.5 21.9 %copy-start.1 = (bf16[8,1152,1024]{2,1,0:T(8,128)(2,1)}, bf16[8,1152,1024]{2,1,0:T(8,128)(2,1)S(1)}, u32[]{:S(2)}) copy-start(bf16[8,1152,1024]{2,1,0:T(8,128)(2,1)S(1)} %place_late_pieces.1.layers.layers_in) | copy-start | bytes 56623108
  116.3 16.2 %collective-permute-start.13 = (bf16[128,1024]{1,0:T(8,128)(2,1)S(1)}, bf16[128,1024]{1,0:T(8,128)(2,1)S(1)}, u32[]{:S(2)}, u32[]{:S(2)}) collective-permute-start(bf16[128,1024]{1,0:T(8,128)(2,1)S(1)} %get-tuple-element.39), channel_id=1, source_target_pairs={{0,384},{1,385},{2,386},{3,387},{4,388},{5,389},{6,390},{7,391},{8... | collective-permute-start | bytes 786440 | tf_op jit(solution)/shard_map/ppermute | solution.py:36
  121.5 12.8 %collective-permute-start.15 = (bf16[2,16,4096]{2,1,0:T(8,128)(2,1)S(1)}, bf16[2,16,4096]{2,1,0:T(8,128)(2,1)S(1)}, u32[]{:S(2)}, u32[]{:S(2)}) collective-permute-start(bf16[2,16,4096]{2,1,0:T(8,128)(2,1)S(1)} %pad_maximum_fusion.5), channel_id=1, source_target_pairs={{0,16},{1,17},{2,18},{3,19},{4,20},{5,21},{6,22},{7,23},{8,24},{9,... | collective-permute-start | bytes 786440 | tf_op jit(solution)/shard_map/ppermute | solution.py:36
  133.0 23.5 %collective-permute-start.14 = (bf16[128,1024]{1,0:T(8,128)(2,1)S(1)}, bf16[128,1024]{1,0:T(8,128)(2,1)S(1)}, u32[]{:S(2)}, u32[]{:S(2)}) collective-permute-start(bf16[128,1024]{1,0:T(8,128)(2,1)S(1)} %get-tuple-element.40), channel_id=1, source_target_pairs={{256,128},{257,129},{258,130},{259,131},{260,132},{261,133},{262,1... | collective-permute-start | bytes 786440 | tf_op jit(solution)/shard_map/ppermute | solution.py:36
  167.3 10.7 %all-to-all-start.1 = ((bf16[8,32,128]{2,1,0:T(8,128)(2,1)}), bf16[8,32,128]{2,1,0:T(8,128)(2,1)S(1)}, u32[]{:S(2)}, u32[]{:S(2)}) async-start(bf16[8,32,128]{2,1,0:T(8,128)(2,1)} %backward_first_stage.1), calls=%async_computation.1 | async-start | bytes 131072 | tf_op jit(solution)/shard_map/all_to_all | solution.py:364
  178.7 13.6 %all-to-all-start.2 = ((bf16[8,2,32,128]{3,2,1,0:T(8,128)(2,1)}), bf16[8,2,32,128]{3,2,1,0:T(8,128)(2,1)S(1)}, u32[]{:S(2)}, u32[]{:S(2)}) async-start(bf16[8,2,32,128]{3,2,1,0:T(8,128)(2,1)} %broadcast_in_dim.10), calls=%async_computation.2 | async-start | bytes 262144 | tf_op jit(solution)/shard_map/all_to_all | solution.py:369

commit v5 on v4

--- a/solution.py
+++ b/solution.py
@@ -103,18 +103,6 @@
     assemble(place, pieces, (core, (beside.at[pl.ds(0, 2)], beside.at[pl.ds(2, 2)])), pack, extra, layers, sems)
 
 
-def late_kernel(place, first, second, turn, turn_other, two, before, layers, sems):
-    core, quarter, way = (place[k] for k in (2, 3, 4))
-    pieces = []
-    for k in (0, 1):
-        pieces.append((first, 2 + 3 * k, 0, 1 - k, quarter + way))
-        pieces.append((second, 2 + 3 * k, 1, 1 - k, quarter + 2 * (1 - core)))
-        pieces.append((two.at[k], 0, 0, k, quarter + 2))
-        pieces.append((turn.at[k], 0, 1, k, quarter - way))
-        pieces.append((turn_other.at[k], 0, 1, 1 - k, quarter + way))
-    assemble(place, pieces, (1 - core, (first, second)), None, (), layers, sems)
-
-
 CHUNK = 256
 
 
@@ -160,7 +148,49 @@
     return arrived[...].reshape(D, TOK).T
 
 
-def first_kernel(place, arrived, layers, current, slope_out, left, slope, sems):
+def first_kernel(
+    place, arrived, first, second, turn, turn_other, two, before,
+    current, slope_out, left, layers, slope, sems, late_sems
+):
+    row, col, core, quarter, way = (place[k] for k in range(5))
+
+    def rows(piece):
+        return pl.ds(pl.multiple_of(piece * PIECE, PIECE), PIECE)
+
+    pieces = []
+    for k in (0, 1):
+        pieces.append((first, 2 + 3 * k, 0, 1 - k, quarter + way))
+        pieces.append((second, 2 + 3 * k, 1, 1 - k, quarter + 2 * (1 - core)))
+        pieces.append((two.at[k], 0, 0, k, quarter + 2))
+        pieces.append((turn.at[k], 0, 1, k, quarter - way))
+        pieces.append((turn_other.at[k], 0, 1, 1 - k, quarter + way))
+    for k in range(4):
+        target = layers.at[row * 2 + 1 - col, rows((1 - core) * 4 + k)]
+        pltpu.make_async_copy((first, second)[k // 2].at[k % 2], target, late_sems.at[0, k]).start()
+    for distance in (1, 2, 3):
+        source_row = (row - distance) & 3
+        for k, (ref, index, other_col, other_core, which) in enumerate(pieces):
+            slot = source_row * 2 + (1 - col if other_col else col)
+            half = 1 - core if other_core else core
+            target = layers.at[slot, rows(half * 4 + (which & 3))]
+            source = ref.at[index + distance - 1]
+            pltpu.make_async_copy(source, target, late_sems.at[distance, k]).start()
+
+    def await_row(source_row):
+        distance = (row - source_row) & 3
+
+        def done(k):
+            target = layers.at[0, pl.ds(0, PIECE)]
+            pltpu.make_async_copy(first.at[0], target, late_sems.at[distance, k]).wait()
+
+        for k in range(4):
+            done(k)
+
+        @pl.when(distance > 0)
+        def _():
+            for k in range(4, len(pieces)):
+                done(k)
+
     def keep(slot):
         return pltpu.make_async_copy(slope.at[slot], slope_out.at[slot], sems.at[slot])
 
@@ -169,6 +199,10 @@
         current[...] = rows_of(arrived)
 
         def body(slot, carry):
+            @pl.when((slot & 1) == 0)
+            def _():
+                await_row(slot >> 1)
+
             forward_one(slot, current, layers, slope, left)
             keep(slot).start()
             return carry
@@ -176,6 +210,11 @@
         lax.fori_loop(0, STAGE, body, 0)
         for slot in range(STAGE):
             keep(slot).wait()
+
+    @pl.when(place[5] == 1)
+    def _():
+        for source_row in range(4):
+            await_row(source_row)
 
 
 def middle_kernel(place, hidden, arrived, layers, upstream, factor, current, slope, left, right):
@@ -307,27 +346,21 @@
     first, second = swap_core(first), swap_core(second)
     turn, two = lax.optimization_barrier((turn, two))
     turn_other = swap_core(turn)
-    layers = pl.pallas_call(
-        late_kernel,
-        out_shape=LAYERS,
-        in_specs=[SMEM] + [ANY] * 5 + [VMEM],
-        out_specs=VMEM,
-        scratch_shapes=[pltpu.SemaphoreType.DMA((34,))],
-        input_output_aliases={6: 0},
-        compiler_params=SMALL,
-        name="place_late_pieces",
-    )(place, first, second, in_hbm(turn), turn_other, in_hbm(two), layers)
-
-    hidden, slope, left = pl.pallas_call(
+    hidden, slope, left, layers = pl.pallas_call(
         first_kernel,
-        out_shape=(TOKENS, SLOPE, LEFT),
-        in_specs=[SMEM, VMEM, VMEM],
-        out_specs=(VMEM, HBM, VMEM),
-        scratch_shapes=[scratch(SLOPE), pltpu.SemaphoreType.DMA((STAGE,))],
+        out_shape=(TOKENS, SLOPE, LEFT, LAYERS),
+        in_specs=[SMEM, VMEM] + [ANY] * 5 + [VMEM],
+        out_specs=(VMEM, HBM, VMEM, VMEM),
+        scratch_shapes=[
+            scratch(SLOPE),
+            pltpu.SemaphoreType.DMA((STAGE,)),
+            pltpu.SemaphoreType.DMA((4, 10)),
+        ],
+        input_output_aliases={7: 3},
         compiler_params=PARAMS,
         cost_estimate=cost(1),
         name="forward_first_stage",
-    )(place, arrived, layers)
+    )(place, arrived, first, second, in_hbm(turn), turn_other, in_hbm(two), layers)
     hidden = move(hidden, lambda x, y, z, c: (x, (y + 2 if y > 1 else y + 6), z, c) if y < 4 else None)
     left, queries = lax.optimization_barrier((left, queries))
     queries = jnp.concatenate([queries, move(queries, lambda x, y, z, c: (x ^ 2, y, z, c))])

time: 214 us -> 213 us (level)
    pallas_call x2 -> x1, Pallas kernels: 9.21 us -> 7.81 us  [on_device(): pl.pallas_call(first_kernel, out_shape=(TOKENS, SLOPE, LEFT, LAYERS), in_...]
where the time goes in v5:
time: 213 us; the launch traced here: 212 us
  starting transfers between devices  71.5 us (34%)
  waiting for transfers between devices  66.9 us (31%)
  blocking collectives  39.8 us (19%)
  Pallas kernels  24.4 us (11%)
  other arithmetic  4.73 us (2%)
  local copies, waits for them, and re-layouts  3.45 us (2%)
    ppermute x16, starting transfers between devices, move(): return lax.ppermute(value, AXES, pairs(target))  61.4 us
    ppermute x16, waiting for transfers between devices, move(): return lax.ppermute(value, AXES, pairs(target))  53.3 us
    all_to_all x1, blocking collectives, on_device(): arrived = lax.all_to_all(order, 'section', 0, 0, tiled=True)  22.5 us
    all_to_all x1, blocking collectives, on_device(): lax.all_to_all(outgoing, AXES, 0, 0, tiled=True, axis_index_groups=plane)  17.3 us
    pallas_call x1, Pallas kernels, on_device(): pl.pallas_call(last_kernel, out_shape=FACTOR, in_specs=[SMEM, VMEM, HBM,...  10.8 us
    all_to_all x1, waiting for transfers between devices, on_device(): lax.all_to_all(jnp.broadcast_to(sums[None], (8,) + sums.shape), 'dp', 0,...  7.93 us
    pallas_call x1, Pallas kernels, on_device(): pl.pallas_call(first_kernel, out_shape=(TOKENS, SLOPE, LEFT, LAYERS), in_...  7.81 us
    all_to_all x1, waiting for transfers between devices, on_device(): lax.all_to_all(factor, 'section', 0, 0, tiled=True, axis_index_groups=gro...  5.76 us
  transfers between devices with their start and end apart: 18, of which 10 were waited for; matrix products, arithmetic and copies ran while one was open for 1% of the time, Pallas kernels for 3%

profile of v5, /device:TPU:1, one launch (start us, length us, event | category | flops | bytes accessed | tf_op | source)
XLA Modules:
  0.0 212.1 jit_solution(7629347145965819604)
XLA Ops:
  0.0 2.0 pad_maximum_fusion.pack
  2.0 4.2 %collective-permute-start = (bf16[144,1024]{1,0:T(8,128)(2,1)S(1)}, bf16[144,1024]{1,0:T(8,128)(2,1)S(1)}, u32[]{:S(2)}, u32[]{:S(2)}) collective-permute-start(bf16[144,1024]{1,0:T(8,128)(2,1)S(1)} %constant_dynamic-slice_fusion.1), channel_id=1, source_target_pairs={{0,64},{1,65},{2,66},{3,67},{4,68},{5,69},{6,70},{7,71},{8,72},{9,... | collective-permute-start | bytes 884744 | tf_op jit(solution)/shard_map/ppermute | solution.py:36
  6.2 4.2 %collective-permute-start.1 = (bf16[144,1024]{1,0:T(8,128)(2,1)S(1)}, bf16[144,1024]{1,0:T(8,128)(2,1)S(1)}, u32[]{:S(2)}, u32[]{:S(2)}) collective-permute-start(bf16[144,1024]{1,0:T(8,128)(2,1)S(1)} %constant_dynamic-slice_fusion.1), channel_id=1, source_target_pairs={{0,128},{1,129},{2,130},{3,131},{4,132},{5,133},{6,134},{7,135},{8... | collective-permute-start | bytes 884744 | tf_op jit(solution)/shard_map/ppermute | solution.py:36
  10.4 3.0 %collective-permute-start.2 = (bf16[144,1024]{1,0:T(8,128)(2,1)S(1)}, bf16[144,1024]{1,0:T(8,128)(2,1)}, u32[]{:S(2)}, u32[]{:S(2)}) collective-permute-start(bf16[144,1024]{1,0:T(8,128)(2,1)S(1)} %constant_dynamic-slice_fusion.1), channel_id=1, source_target_pairs={{0,192},{1,193},{2,194},{3,195},{4,196},{5,197},{6,198},{7,199},{8... | collective-permute-start | bytes 884744 | tf_op jit(solution)/shard_map/ppermute | solution.py:36
  13.5 4.5 %collective-permute-start.4 = (bf16[576,1024]{1,0:T(8,128)(2,1)S(1)}, bf16[576,1024]{1,0:T(8,128)(2,1)S(1)}, u32[]{:S(2)}, u32[]{:S(2)}) collective-permute-start(bf16[576,1024]{1,0:T(8,128)(2,1)S(1)} %constant_dynamic-slice_fusion), channel_id=1, source_target_pairs={{0,32},{1,49},{2,34},{3,51},{4,36},{5,53},{6,38},{7,55},{8,40},{9,... | collective-permute-start | bytes 3538952 | tf_op jit(solution)/shard_map/ppermute | solution.py:36
  18.2 9.6 %collective-permute-done.1 = bf16[144,1024]{1,0:T(8,128)(2,1)S(1)} collective-permute-done((bf16[144,1024]{1,0:T(8,128)(2,1)S(1)}, bf16[144,1024]{1,0:T(8,128)(2,1)S(1)}, u32[]{:S(2)}, u32[]{:S(2)}) %collective-permute-start.1) | collective-permute-done | bytes 294944 | tf_op jit(solution)/shard_map/ppermute | solution.py:36
  27.8 2.0 collective-permute-done.2
  30.9 3.3 %collective-permute-start.3 = (bf16[3,144,1024]{2,1,0:T(8,128)(2,1)S(1)}, bf16[3,144,1024]{2,1,0:T(8,128)(2,1)S(1)}, u32[]{:S(2)}, u32[]{:S(2)}) collective-permute-start(bf16[3,144,1024]{2,1,0:T(8,128)(2,1)S(1)} %get-tuple-element.52), channel_id=1, source_target_pairs={{0,1},{1,0},{2,3},{3,2},{4,5},{5,4},{6,7},{7,6},{8,9},{9,8},{10,11... | collective-permute-start | bytes 2654216 | tf_op jit(solution)/shard_map/ppermute | solution.py:36
  34.3 1.9 collective-permute-start.5
  37.7 8.4 %collective-permute-start.6 = (bf16[2,3,144,1024]{3,2,1,0:T(8,128)(2,1)S(1)}, bf16[2,3,144,1024]{3,2,1,0:T(8,128)(2,1)}, u32[]{:S(2)}, u32[]{:S(2)}) collective-permute-start(bf16[2,3,144,1024]{3,2,1,0:T(8,128)(2,1)S(1)} %pad_maximum_fusion.1.own), channel_id=1, source_target_pairs={{0,2},{1,15},{2,4},{3,1},{4,6},{5,3},{6,8},{7,5},{8,10},{9,7},{10,... | collective-permute-start | bytes 5308424 | tf_op jit(solution)/shard_map/ppermute | solution.py:36
  46.2 1.9 collective-permute-start.7
  48.1 22.5 %all_to_all.24.arrived = bf16[16,64,128]{2,1,0:T(8,128)(2,1)S(1)} all-to-all(bf16[16,64,128]{2,1,0:T(8,128)(2,1)S(1)} %pad_maximum_fusion.4), channel_id=1, replica_groups=mesh['section'=16,'dp'=32] {'section'}, dimensions={0} | all-to-all | bytes 524288 | tf_op jit(solution)/shard_map/all_to_all | solution.py:319
  72.0 4.1 %collective-permute-start.10 = (bf16[2,3,144,1024]{3,2,1,0:T(8,128)(2,1)}, bf16[2,3,144,1024]{3,2,1,0:T(8,128)(2,1)}, u32[]{:S(2)}, u32[]{:S(2)}) collective-permute-start(bf16[2,3,144,1024]{3,2,1,0:T(8,128)(2,1)} %collective-permute-done.6), channel_id=1, source_target_pairs={{0,32},{1,49},{2,34},{3,51},{4,36},{5,53},{6,38},{7,55},{8,40},{9,... | collective-permute-start | bytes 5308424 | tf_op jit(solution)/shard_map/ppermute | solution.py:36
  76.0 4.3 %collective-permute-start.11 = (bf16[2,3,144,1024]{3,2,1,0:T(8,128)(2,1)}, bf16[2,3,144,1024]{3,2,1,0:T(8,128)(2,1)}, u32[]{:S(2)}, u32[]{:S(2)}) collective-permute-start(bf16[2,3,144,1024]{3,2,1,0:T(8,128)(2,1)} %collective-permute-done.6), channel_id=1, source_target_pairs={{0,2},{1,15},{2,4},{3,1},{4,6},{5,3},{6,8},{7,5},{8,10},{9,7},{10,... | collective-permute-start | bytes 5308424 | tf_op jit(solution)/shard_map/ppermute | solution.py:36
  80.5 5.2 %place_early_pieces.1 = (bf16[8,1152,1024]{2,1,0:T(8,128)(2,1)S(1)}, bf16[8,144,1024]{2,1,0:T(8,128)(2,1)S(1)}, bf16[8,144,1024]{2,1,0:T(8,128)(2,1)S(1)}) custom-call(s32[6]{0:T(128)S(1)} %stack.53.place, bf16[1152,1024]{1,0:T(8,128)(2,1)S(1)} %pad_maximum_fusion.pack, bf16[4,144,1024]{2,1,0:T(8,128)(2,1)} %bitcast.70, bf16[2,3,144,1024]{3,2,1,0:T(8,128)(2,1)} %copy-done.2, ...), custom_call_target="tpu_custom_call" | custom-call | flops 2415919104 | bytes 18874368 | tf_op jit(solution)/shard_map/place_early_pieces/pallas_call | solution.py:329
  85.7 1.9 collective-permute-start.8
  87.7 2.4 %collective-permute-start.9 = (bf16[8,144,1024]{2,1,0:T(8,128)(2,1)S(1)}, bf16[8,144,1024]{2,1,0:T(8,128)(2,1)S(1)}, u32[]{:S(2)}, u32[]{:S(2)}) collective-permute-start(bf16[8,144,1024]{2,1,0:T(8,128)(2,1)S(1)} %get-tuple-element.36), channel_id=1, source_target_pairs={{0,1},{1,0},{2,3},{3,2},{4,5},{5,4},{6,7},{7,6},{8,9},{9,8},{10,11... | collective-permute-start | bytes 7077896 | tf_op jit(solution)/shard_map/ppermute | solution.py:36
  90.1 7.0 %collective-permute-done.10.turn = bf16[2,3,144,1024]{3,2,1,0:T(8,128)(2,1)} collective-permute-done((bf16[2,3,144,1024]{3,2,1,0:T(8,128)(2,1)}, bf16[2,3,144,1024]{3,2,1,0:T(8,128)(2,1)}, u32[]{:S(2)}, u32[]{:S(2)}) %collective-permute-start.10) | collective-permute-done | bytes 1769504 | tf_op jit(solution)/shard_map/ppermute | solution.py:36
  97.0 3.1 %collective-permute-done.11.two = bf16[2,3,144,1024]{3,2,1,0:T(8,128)(2,1)} collective-permute-done((bf16[2,3,144,1024]{3,2,1,0:T(8,128)(2,1)}, bf16[2,3,144,1024]{3,2,1,0:T(8,128)(2,1)}, u32[]{:S(2)}, u32[]{:S(2)}) %collective-permute-start.11) | collective-permute-done | bytes 1769504 | tf_op jit(solution)/shard_map/ppermute | solution.py:36
  100.1 3.4 %collective-permute-start.12 = (bf16[2,3,144,1024]{3,2,1,0:T(8,128)(2,1)}, bf16[2,3,144,1024]{3,2,1,0:T(8,128)(2,1)S(1)}, u32[]{:S(2)}, u32[]{:S(2)}) collective-permute-start(bf16[2,3,144,1024]{3,2,1,0:T(8,128)(2,1)} %collective-permute-done.10.turn), channel_id=1, source_target_pairs={{0,1},{1,0},{2,3},{3,2},{4,5},{5,4},{6,7},{7,6},{8,9},{9,8},{10,11... | collective-permute-start | bytes 5308424 | tf_op jit(solution)/shard_map/ppermute | solution.py:36
  103.6 3.5 %collective-permute-done.12.turn_other = bf16[2,3,144,1024]{3,2,1,0:T(8,128)(2,1)S(1)} collective-permute-done((bf16[2,3,144,1024]{3,2,1,0:T(8,128)(2,1)}, bf16[2,3,144,1024]{3,2,1,0:T(8,128)(2,1)S(1)}, u32[]{:S(2)}, u32[]{:S(2)}) %collective-permute-start.12) | collective-permute-done | bytes 1769504 | tf_op jit(solution)/shard_map/ppermute | solution.py:36
  107.0 7.8 %forward_first_stage.1 = (bf16[128,1024]{1,0:T(8,128)(2,1)S(1)}, f32[8,128,1024]{2,1,0:T(8,128)S(1)}, f32[8,128,128]{2,1,0:T(8,128)S(1)}, bf16[8,1152,1024]{2,1,0:T(8,128)(2,1)S(1)}) custom-call(s32[6]{0:T(128)S(1)} %stack.53.place, bf16[16,64,128]{2,1,0:T(8,128)(2,1)S(1)} %all_to_all.24.arrived, ...), custom_call_target="tpu_custom_call", output_to_operand_aliasing={{3}: (7, {})} | custom-call | flops 2415919104 | bytes 18874368 | tf_op jit(solution)/shard_map/forward_first_stage/pallas_call | solution.py:349
  114.9 6.2 %collective-permute-start.13 = (bf16[128,1024]{1,0:T(8,128)(2,1)S(1)}, bf16[128,1024]{1,0:T(8,128)(2,1)S(1)}, u32[]{:S(2)}, u32[]{:S(2)}) collective-permute-start(bf16[128,1024]{1,0:T(8,128)(2,1)S(1)} %get-tuple-element.40), channel_id=1, source_target_pairs={{0,384},{1,385},{2,386},{3,387},{4,388},{5,389},{6,390},{7,391},{8... | collective-permute-start | bytes 786440 | tf_op jit(solution)/shard_map/ppermute | solution.py:36
  121.0 6.4 %collective-permute-start.15 = (bf16[2,16,4096]{2,1,0:T(8,128)(2,1)S(1)}, bf16[2,16,4096]{2,1,0:T(8,128)(2,1)S(1)}, u32[]{:S(2)}, u32[]{:S(2)}) collective-permute-start(bf16[2,16,4096]{2,1,0:T(8,128)(2,1)S(1)} %pad_maximum_fusion.5), channel_id=1, source_target_pairs={{0,16},{1,17},{2,18},{3,19},{4,20},{5,21},{6,22},{7,23},{8,24},{9,... | collective-permute-start | bytes 786440 | tf_op jit(solution)/shard_map/ppermute | solution.py:36
  127.4 4.5 %collective-permute-done.13.hidden = bf16[128,1024]{1,0:T(8,128)(2,1)S(1)} collective-permute-done((bf16[128,1024]{1,0:T(8,128)(2,1)S(1)}, bf16[128,1024]{1,0:T(8,128)(2,1)S(1)}, u32[]{:S(2)}, u32[]{:S(2)}) %collective-permute-start.13) | collective-permute-done | bytes 262176 | tf_op jit(solution)/shard_map/ppermute | solution.py:36
  133.9 22.3 %collective-permute-done.14.upstream = bf16[128,1024]{1,0:T(8,128)(2,1)S(1)} collective-permute-done((bf16[128,1024]{1,0:T(8,128)(2,1)S(1)}, bf16[128,1024]{1,0:T(8,128)(2,1)S(1)}, u32[]{:S(2)}, u32[]{:S(2)}) %collective-permute-start.14) | collective-permute-done | bytes 262176 | tf_op jit(solution)/shard_map/ppermute | solution.py:36
  156.1 10.8 %backward_first_stage.1 = bf16[8,32,128]{2,1,0:T(8,128)(2,1)} custom-call(s32[6]{0:T(128)S(1)} %stack.53.place, bf16[128,1024]{1,0:T(8,128)(2,1)S(1)} %collective-permute-done.14.upstream, f32[8,128,1024]{2,1,0:T(8,128)S(1)} %get-tuple-element.47.slope_in, f32[8,128,128]{2,1,0:T(8,128)S(1)} %get-tuple-element.48.left, ...), custom_call_target="tpu_custom_call" | custom-call | flops 2415919104 | bytes 18874368 | tf_op jit(solution)/shard_map/backward_first_stage/pallas_call | solution.py:379
  166.9 4.4 %all-to-all-start.1 = ((bf16[8,32,128]{2,1,0:T(8,128)(2,1)}), bf16[8,32,128]{2,1,0:T(8,128)(2,1)S(1)}, u32[]{:S(2)}, u32[]{:S(2)}) async-start(bf16[8,32,128]{2,1,0:T(8,128)(2,1)} %backward_first_stage.1), calls=%async_computation.1 | async-start | bytes 131072 | tf_op jit(solution)/shard_map/all_to_all | solution.py:397
  171.4 5.8 %all-to-all-done.1 = bf16[8,32,128]{2,1,0:T(8,128)(2,1)S(1)} async-done(((bf16[8,32,128]{2,1,0:T(8,128)(2,1)}), bf16[8,32,128]{2,1,0:T(8,128)(2,1)S(1)}, u32[]{:S(2)}, u32[]{:S(2)}) %all-to-all-start.1) | async-done | bytes 65568 | tf_op jit(solution)/shard_map/all_to_all | solution.py:397
  177.8 5.7 %all-to-all-start.2 = ((bf16[8,2,32,128]{3,2,1,0:T(8,128)(2,1)}), bf16[8,2,32,128]{3,2,1,0:T(8,128)(2,1)S(1)}, u32[]{:S(2)}, u32[]{:S(2)}) async-start(bf16[8,2,32,128]{3,2,1,0:T(8,128)(2,1)} %broadcast_in_dim.10), calls=%async_computation.2 | async-start | bytes 262144 | tf_op jit(solution)/shard_map/all_to_all | solution.py:402
  183.5 7.9 %all-to-all-done.2 = bf16[8,2,32,128]{3,2,1,0:T(8,128)(2,1)S(1)} async-done(((bf16[8,2,32,128]{3,2,1,0:T(8,128)(2,1)}), bf16[8,2,32,128]{3,2,1,0:T(8,128)(2,1)S(1)}, u32[]{:S(2)}, u32[]{:S(2)}) %all-to-all-start.2) | async-done | bytes 131104 | tf_op jit(solution)/shard_map/all_to_all | solution.py:402
  192.8 17.3 %all_to_all.25 = f32[64,1,32]{2,1,0:T(1,128)S(1)} all-to-all(f32[64,1,32]{2,1,0:T(1,128)S(1)} %bitcast.67), channel_id=1, replica_groups={{0,1,16,17,32,33,48,49,64,65,80,81,96,97,112,113,128,129,144,145,160,16..., dimensions={0} | all-to-all | bytes 16384 | tf_op jit(solution)/shard_map/all_to_all | solution.py:426
  (53 shorter events, 10.1 us)
Async XLA Ops:
  0.0 18.1 %copy-start = (bf16[2,512,64]{1,2,0:T(8,128)(2,1)S(1)}, bf16[2,512,64]{1,2,0:T(8,128)(2,1)}, u32[]{:S(2)}) copy-start(bf16[2,512,64]{1,2,0:T(8,128)(2,1)} %param.7) | copy-start | bytes 393220
  2.0 16.1 %copy-start.3 = (bf16[2,512,64]{1,2,0:T(8,128)(2,1)S(1)}, bf16[2,512,64]{1,2,0:T(8,128)(2,1)}, u32[]{:S(2)}) copy-start(bf16[2,512,64]{1,2,0:T(8,128)(2,1)} %param.6) | copy-start | bytes 393220
  2.0 16.2 %collective-permute-start = (bf16[144,1024]{1,0:T(8,128)(2,1)S(1)}, bf16[144,1024]{1,0:T(8,128)(2,1)S(1)}, u32[]{:S(2)}, u32[]{:S(2)}) collective-permute-start(bf16[144,1024]{1,0:T(8,128)(2,1)S(1)} %constant_dynamic-slice_fusion.1), channel_id=1, source_target_pairs={{0,64},{1,65},{2,66},{3,67},{4,68},{5,69},{6,70},{7,71},{8,72},{9,... | collective-permute-start | bytes 884744 | tf_op jit(solution)/shard_map/ppermute | solution.py:36
  6.2 21.6 %collective-permute-start.1 = (bf16[144,1024]{1,0:T(8,128)(2,1)S(1)}, bf16[144,1024]{1,0:T(8,128)(2,1)S(1)}, u32[]{:S(2)}, u32[]{:S(2)}) collective-permute-start(bf16[144,1024]{1,0:T(8,128)(2,1)S(1)} %constant_dynamic-slice_fusion.1), channel_id=1, source_target_pairs={{0,128},{1,129},{2,130},{3,131},{4,132},{5,133},{6,134},{7,135},{8... | collective-permute-start | bytes 884744 | tf_op jit(solution)/shard_map/ppermute | solution.py:36
  10.4 19.4 %collective-permute-start.2 = (bf16[144,1024]{1,0:T(8,128)(2,1)S(1)}, bf16[144,1024]{1,0:T(8,128)(2,1)}, u32[]{:S(2)}, u32[]{:S(2)}) collective-permute-start(bf16[144,1024]{1,0:T(8,128)(2,1)S(1)} %constant_dynamic-slice_fusion.1), channel_id=1, source_target_pairs={{0,192},{1,193},{2,194},{3,195},{4,196},{5,197},{6,198},{7,199},{8... | collective-permute-start | bytes 884744 | tf_op jit(solution)/shard_map/ppermute | solution.py:36
  13.5 20.7 %copy-start.4 = (bf16[1,16,4096]{2,1,0:T(8,128)(2,1)S(1)}, bf16[1,16,4096]{2,1,0:T(8,128)(2,1)}, u32[]{:S(2)}) copy-start(bf16[1,16,4096]{2,1,0:T(8,128)(2,1)} %param.11) | copy-start | bytes 393220
  13.5 24.2 %collective-permute-start.4 = (bf16[576,1024]{1,0:T(8,128)(2,1)S(1)}, bf16[576,1024]{1,0:T(8,128)(2,1)S(1)}, u32[]{:S(2)}, u32[]{:S(2)}) collective-permute-start(bf16[576,1024]{1,0:T(8,128)(2,1)S(1)} %constant_dynamic-slice_fusion), channel_id=1, source_target_pairs={{0,32},{1,49},{2,34},{3,51},{4,36},{5,53},{6,38},{7,55},{8,40},{9,... | collective-permute-start | bytes 3538952 | tf_op jit(solution)/shard_map/ppermute | solution.py:36
  30.9 6.6 %collective-permute-start.3 = (bf16[3,144,1024]{2,1,0:T(8,128)(2,1)S(1)}, bf16[3,144,1024]{2,1,0:T(8,128)(2,1)S(1)}, u32[]{:S(2)}, u32[]{:S(2)}) collective-permute-start(bf16[3,144,1024]{2,1,0:T(8,128)(2,1)S(1)} %get-tuple-element.52), channel_id=1, source_target_pairs={{0,1},{1,0},{2,3},{3,2},{4,5},{5,4},{6,7},{7,6},{8,9},{9,8},{10,11... | collective-permute-start | bytes 2654216 | tf_op jit(solution)/shard_map/ppermute | solution.py:36
  34.3 3.2 %collective-permute-start.5 = (bf16[1,16,4096]{2,1,0:T(8,128)(2,1)S(1)}, bf16[1,16,4096]{2,1,0:T(8,128)(2,1)S(1)}, u32[]{:S(2)}, u32[]{:S(2)}) collective-permute-start(bf16[1,16,4096]{2,1,0:T(8,128)(2,1)S(1)} %copy-done.4), channel_id=1, source_target_pairs={{0,1},{1,0},{2,3},{3,2},{4,5},{5,4},{6,7},{7,6},{8,9},{9,8},{10,11... | collective-permute-start | bytes 393224 | tf_op jit(solution)/shard_map/ppermute | solution.py:36
  37.7 8.5 %copy-start.2 = (bf16[2,3,144,1024]{3,2,1,0:T(8,128)(2,1)}, bf16[2,3,144,1024]{3,2,1,0:T(8,128)(2,1)S(1)}, u32[]{:S(2)}) copy-start(bf16[2,3,144,1024]{3,2,1,0:T(8,128)(2,1)S(1)} %pad_maximum_fusion.1.own) | copy-start | bytes 5308420
  37.7 38.3 %copy-start.6 = (bf16[576,1024]{1,0:T(8,128)(2,1)}, bf16[576,1024]{1,0:T(8,128)(2,1)S(1)}, u32[]{:S(2)}) copy-start(bf16[576,1024]{1,0:T(8,128)(2,1)S(1)} %collective-permute-done.4) | copy-start | bytes 3538948
  37.7 32.9 %collective-permute-start.6 = (bf16[2,3,144,1024]{3,2,1,0:T(8,128)(2,1)S(1)}, bf16[2,3,144,1024]{3,2,1,0:T(8,128)(2,1)}, u32[]{:S(2)}, u32[]{:S(2)}) collective-permute-start(bf16[2,3,144,1024]{3,2,1,0:T(8,128)(2,1)S(1)} %pad_maximum_fusion.1.own), channel_id=1, source_target_pairs={{0,2},{1,15},{2,4},{3,1},{4,6},{5,3},{6,8},{7,5},{8,10},{9,7},{10,... | collective-permute-start | bytes 5308424 | tf_op jit(solution)/shard_map/ppermute | solution.py:36
  46.2 24.5 %collective-permute-start.7 = (bf16[2,3,144,1024]{3,2,1,0:T(8,128)(2,1)S(1)}, bf16[2,3,144,1024]{3,2,1,0:T(8,128)(2,1)S(1)}, u32[]{:S(2)}, u32[]{:S(2)}) collective-permute-start(bf16[2,3,144,1024]{3,2,1,0:T(8,128)(2,1)S(1)} %pad_maximum_fusion.1.own), channel_id=1, source_target_pairs={{0,32},{1,49},{2,34},{3,51},{4,36},{5,53},{6,38},{7,55},{8,40},{9,... | collective-permute-start | bytes 5308424 | tf_op jit(solution)/shard_map/ppermute | solution.py:36
  70.7 1.3 copy-start.5
  72.0 25.1 %collective-permute-start.10 = (bf16[2,3,144,1024]{3,2,1,0:T(8,128)(2,1)}, bf16[2,3,144,1024]{3,2,1,0:T(8,128)(2,1)}, u32[]{:S(2)}, u32[]{:S(2)}) collective-permute-start(bf16[2,3,144,1024]{3,2,1,0:T(8,128)(2,1)} %collective-permute-done.6), channel_id=1, source_target_pairs={{0,32},{1,49},{2,34},{3,51},{4,36},{5,53},{6,38},{7,55},{8,40},{9,... | collective-permute-start | bytes 5308424 | tf_op jit(solution)/shard_map/ppermute | solution.py:36
  76.0 24.1 %collective-permute-start.11 = (bf16[2,3,144,1024]{3,2,1,0:T(8,128)(2,1)}, bf16[2,3,144,1024]{3,2,1,0:T(8,128)(2,1)}, u32[]{:S(2)}, u32[]{:S(2)}) collective-permute-start(bf16[2,3,144,1024]{3,2,1,0:T(8,128)(2,1)} %collective-permute-done.6), channel_id=1, source_target_pairs={{0,2},{1,15},{2,4},{3,1},{4,6},{5,3},{6,8},{7,5},{8,10},{9,7},{10,... | collective-permute-start | bytes 5308424 | tf_op jit(solution)/shard_map/ppermute | solution.py:36
  85.7 17.8 %collective-permute-start.8 = (bf16[8,144,1024]{2,1,0:T(8,128)(2,1)S(1)}, bf16[8,144,1024]{2,1,0:T(8,128)(2,1)S(1)}, u32[]{:S(2)}, u32[]{:S(2)}) collective-permute-start(bf16[8,144,1024]{2,1,0:T(8,128)(2,1)S(1)} %get-tuple-element.35), channel_id=1, source_target_pairs={{0,1},{1,0},{2,3},{3,2},{4,5},{5,4},{6,7},{7,6},{8,9},{9,8},{10,11... | collective-permute-start | bytes 7077896 | tf_op jit(solution)/shard_map/ppermute | solution.py:36
  87.7 15.9 %collective-permute-start.9 = (bf16[8,144,1024]{2,1,0:T(8,128)(2,1)S(1)}, bf16[8,144,1024]{2,1,0:T(8,128)(2,1)S(1)}, u32[]{:S(2)}, u32[]{:S(2)}) collective-permute-start(bf16[8,144,1024]{2,1,0:T(8,128)(2,1)S(1)} %get-tuple-element.36), channel_id=1, source_target_pairs={{0,1},{1,0},{2,3},{3,2},{4,5},{5,4},{6,7},{7,6},{8,9},{9,8},{10,11... | collective-permute-start | bytes 7077896 | tf_op jit(solution)/shard_map/ppermute | solution.py:36
  100.1 6.9 %collective-permute-start.12 = (bf16[2,3,144,1024]{3,2,1,0:T(8,128)(2,1)}, bf16[2,3,144,1024]{3,2,1,0:T(8,128)(2,1)S(1)}, u32[]{:S(2)}, u32[]{:S(2)}) collective-permute-start(bf16[2,3,144,1024]{3,2,1,0:T(8,128)(2,1)} %collective-permute-done.10.turn), channel_id=1, source_target_pairs={{0,1},{1,0},{2,3},{3,2},{4,5},{5,4},{6,7},{7,6},{8,9},{9,8},{10,11... | collective-permute-start | bytes 5308424 | tf_op jit(solution)/shard_map/ppermute | solution.py:36
  114.9 17.6 %copy-start.1 = (bf16[8,1152,1024]{2,1,0:T(8,128)(2,1)}, bf16[8,1152,1024]{2,1,0:T(8,128)(2,1)S(1)}, u32[]{:S(2)}) copy-start(bf16[8,1152,1024]{2,1,0:T(8,128)(2,1)S(1)} %get-tuple-element.41.layers.layers_in) | copy-start | bytes 56623108
  114.9 17.1 %collective-permute-start.13 = (bf16[128,1024]{1,0:T(8,128)(2,1)S(1)}, bf16[128,1024]{1,0:T(8,128)(2,1)S(1)}, u32[]{:S(2)}, u32[]{:S(2)}) collective-permute-start(bf16[128,1024]{1,0:T(8,128)(2,1)S(1)} %get-tuple-element.40), channel_id=1, source_target_pairs={{0,384},{1,385},{2,386},{3,387},{4,388},{5,389},{6,390},{7,391},{8... | collective-permute-start | bytes 786440 | tf_op jit(solution)/shard_map/ppermute | solution.py:36
  121.0 12.8 %collective-permute-start.15 = (bf16[2,16,4096]{2,1,0:T(8,128)(2,1)S(1)}, bf16[2,16,4096]{2,1,0:T(8,128)(2,1)S(1)}, u32[]{:S(2)}, u32[]{:S(2)}) collective-permute-start(bf16[2,16,4096]{2,1,0:T(8,128)(2,1)S(1)} %pad_maximum_fusion.5), channel_id=1, source_target_pairs={{0,16},{1,17},{2,18},{3,19},{4,20},{5,21},{6,22},{7,23},{8,24},{9,... | collective-permute-start | bytes 786440 | tf_op jit(solution)/shard_map/ppermute | solution.py:36
  132.5 23.6 %collective-permute-start.14 = (bf16[128,1024]{1,0:T(8,128)(2,1)S(1)}, bf16[128,1024]{1,0:T(8,128)(2,1)S(1)}, u32[]{:S(2)}, u32[]{:S(2)}) collective-permute-start(bf16[128,1024]{1,0:T(8,128)(2,1)S(1)} %get-tuple-element.42), channel_id=1, source_target_pairs={{256,128},{257,129},{258,130},{259,131},{260,132},{261,133},{262,1... | collective-permute-start | bytes 786440 | tf_op jit(solution)/shard_map/ppermute | solution.py:36
  166.9 10.2 %all-to-all-start.1 = ((bf16[8,32,128]{2,1,0:T(8,128)(2,1)}), bf16[8,32,128]{2,1,0:T(8,128)(2,1)S(1)}, u32[]{:S(2)}, u32[]{:S(2)}) async-start(bf16[8,32,128]{2,1,0:T(8,128)(2,1)} %backward_first_stage.1), calls=%async_computation.1 | async-start | bytes 131072 | tf_op jit(solution)/shard_map/all_to_all | solution.py:397
  177.8 13.6 %all-to-all-start.2 = ((bf16[8,2,32,128]{3,2,1,0:T(8,128)(2,1)}), bf16[8,2,32,128]{3,2,1,0:T(8,128)(2,1)S(1)}, u32[]{:S(2)}, u32[]{:S(2)}) async-start(bf16[8,2,32,128]{3,2,1,0:T(8,128)(2,1)} %broadcast_in_dim.10), calls=%async_computation.2 | async-start | bytes 262144 | tf_op jit(solution)/shard_map/all_to_all | solution.py:402

commit v6 on v5

--- a/solution.py
+++ b/solution.py
@@ -124,8 +124,8 @@
     grad = (upstream * slope[slot]).astype(jnp.bfloat16)
     nt = (((1,), (1,)), ((), ()))
     right[slot] = lax.dot_general(grad, layers[slot, D:], nt, preferred_element_type=jnp.float32)
-    for start in range(0, D, CHUNK):
-        cols = slice(start, start + CHUNK)
+    for start in range(0, D, CHUNK // 2):
+        cols = slice(start, start + CHUNK // 2)
         carried = lax.dot_general(
             grad, layers[slot, cols], nt, preferred_element_type=jnp.float32
         )

time: 213 us -> 211 us (level)
  no operation moved by 1% of the time
where the time goes in v6:
time: 211 us; the launch traced here: 210 us
  starting transfers between devices  71.5 us (34%)
  waiting for transfers between devices  66.1 us (31%)
  blocking collectives  39.8 us (19%)
  Pallas kernels  23.6 us (11%)
  other arithmetic  4.73 us (2%)
  local copies, waits for them, and re-layouts  3.45 us (2%)
    ppermute x16, starting transfers between devices, move(): return lax.ppermute(value, AXES, pairs(target))  61.4 us
    ppermute x16, waiting for transfers between devices, move(): return lax.ppermute(value, AXES, pairs(target))  52.4 us
    all_to_all x1, blocking collectives, on_device(): arrived = lax.all_to_all(order, 'section', 0, 0, tiled=True)  22.5 us
    all_to_all x1, blocking collectives, on_device(): lax.all_to_all(outgoing, AXES, 0, 0, tiled=True, axis_index_groups=plane)  17.3 us
    pallas_call x1, Pallas kernels, on_device(): pl.pallas_call(last_kernel, out_shape=FACTOR, in_specs=[SMEM, VMEM, HBM,...  9.99 us
    all_to_all x1, waiting for transfers between devices, on_device(): lax.all_to_all(jnp.broadcast_to(sums[None], (8,) + sums.shape), 'dp', 0,...  7.93 us
    pallas_call x1, Pallas kernels, on_device(): pl.pallas_call(first_kernel, out_shape=(TOKENS, SLOPE, LEFT, LAYERS), in_...  7.81 us
    all_to_all x1, waiting for transfers between devices, on_device(): lax.all_to_all(factor, 'section', 0, 0, tiled=True, axis_index_groups=gro...  5.76 us
  transfers between devices with their start and end apart: 18, of which 10 were waited for; matrix products, arithmetic and copies ran while one was open for 1% of the time, Pallas kernels for 3%

profile of v6, /device:TPU:1, one launch (start us, length us, event | category | flops | bytes accessed | tf_op | source)
XLA Modules:
  0.0 210.4 jit_solution(2200042806164678862)
XLA Ops:
  0.0 2.0 pad_maximum_fusion.pack
  2.0 4.2 %collective-permute-start = (bf16[144,1024]{1,0:T(8,128)(2,1)S(1)}, bf16[144,1024]{1,0:T(8,128)(2,1)S(1)}, u32[]{:S(2)}, u32[]{:S(2)}) collective-permute-start(bf16[144,1024]{1,0:T(8,128)(2,1)S(1)} %constant_dynamic-slice_fusion.1), channel_id=1, source_target_pairs={{0,64},{1,65},{2,66},{3,67},{4,68},{5,69},{6,70},{7,71},{8,72},{9,... | collective-permute-start | bytes 884744 | tf_op jit(solution)/shard_map/ppermute | solution.py:36
  6.2 4.2 %collective-permute-start.1 = (bf16[144,1024]{1,0:T(8,128)(2,1)S(1)}, bf16[144,1024]{1,0:T(8,128)(2,1)S(1)}, u32[]{:S(2)}, u32[]{:S(2)}) collective-permute-start(bf16[144,1024]{1,0:T(8,128)(2,1)S(1)} %constant_dynamic-slice_fusion.1), channel_id=1, source_target_pairs={{0,128},{1,129},{2,130},{3,131},{4,132},{5,133},{6,134},{7,135},{8... | collective-permute-start | bytes 884744 | tf_op jit(solution)/shard_map/ppermute | solution.py:36
  10.4 3.0 %collective-permute-start.2 = (bf16[144,1024]{1,0:T(8,128)(2,1)S(1)}, bf16[144,1024]{1,0:T(8,128)(2,1)}, u32[]{:S(2)}, u32[]{:S(2)}) collective-permute-start(bf16[144,1024]{1,0:T(8,128)(2,1)S(1)} %constant_dynamic-slice_fusion.1), channel_id=1, source_target_pairs={{0,192},{1,193},{2,194},{3,195},{4,196},{5,197},{6,198},{7,199},{8... | collective-permute-start | bytes 884744 | tf_op jit(solution)/shard_map/ppermute | solution.py:36
  13.5 4.5 %collective-permute-start.4 = (bf16[576,1024]{1,0:T(8,128)(2,1)S(1)}, bf16[576,1024]{1,0:T(8,128)(2,1)S(1)}, u32[]{:S(2)}, u32[]{:S(2)}) collective-permute-start(bf16[576,1024]{1,0:T(8,128)(2,1)S(1)} %constant_dynamic-slice_fusion), channel_id=1, source_target_pairs={{0,32},{1,49},{2,34},{3,51},{4,36},{5,53},{6,38},{7,55},{8,40},{9,... | collective-permute-start | bytes 3538952 | tf_op jit(solution)/shard_map/ppermute | solution.py:36
  18.2 9.6 %collective-permute-done.1 = bf16[144,1024]{1,0:T(8,128)(2,1)S(1)} collective-permute-done((bf16[144,1024]{1,0:T(8,128)(2,1)S(1)}, bf16[144,1024]{1,0:T(8,128)(2,1)S(1)}, u32[]{:S(2)}, u32[]{:S(2)}) %collective-permute-start.1) | collective-permute-done | bytes 294944 | tf_op jit(solution)/shard_map/ppermute | solution.py:36
  27.8 2.0 collective-permute-done.2
  30.9 3.3 %collective-permute-start.3 = (bf16[3,144,1024]{2,1,0:T(8,128)(2,1)S(1)}, bf16[3,144,1024]{2,1,0:T(8,128)(2,1)S(1)}, u32[]{:S(2)}, u32[]{:S(2)}) collective-permute-start(bf16[3,144,1024]{2,1,0:T(8,128)(2,1)S(1)} %get-tuple-element.52), channel_id=1, source_target_pairs={{0,1},{1,0},{2,3},{3,2},{4,5},{5,4},{6,7},{7,6},{8,9},{9,8},{10,11... | collective-permute-start | bytes 2654216 | tf_op jit(solution)/shard_map/ppermute | solution.py:36
  34.3 1.9 collective-permute-start.5
  37.7 8.4 %collective-permute-start.6 = (bf16[2,3,144,1024]{3,2,1,0:T(8,128)(2,1)S(1)}, bf16[2,3,144,1024]{3,2,1,0:T(8,128)(2,1)}, u32[]{:S(2)}, u32[]{:S(2)}) collective-permute-start(bf16[2,3,144,1024]{3,2,1,0:T(8,128)(2,1)S(1)} %pad_maximum_fusion.1.own), channel_id=1, source_target_pairs={{0,2},{1,15},{2,4},{3,1},{4,6},{5,3},{6,8},{7,5},{8,10},{9,7},{10,... | collective-permute-start | bytes 5308424 | tf_op jit(solution)/shard_map/ppermute | solution.py:36
  46.2 1.9 collective-permute-start.7
  48.1 22.5 %all_to_all.24.arrived = bf16[16,64,128]{2,1,0:T(8,128)(2,1)S(1)} all-to-all(bf16[16,64,128]{2,1,0:T(8,128)(2,1)S(1)} %pad_maximum_fusion.4), channel_id=1, replica_groups=mesh['section'=16,'dp'=32] {'section'}, dimensions={0} | all-to-all | bytes 524288 | tf_op jit(solution)/shard_map/all_to_all | solution.py:319
  72.0 4.1 %collective-permute-start.10 = (bf16[2,3,144,1024]{3,2,1,0:T(8,128)(2,1)}, bf16[2,3,144,1024]{3,2,1,0:T(8,128)(2,1)}, u32[]{:S(2)}, u32[]{:S(2)}) collective-permute-start(bf16[2,3,144,1024]{3,2,1,0:T(8,128)(2,1)} %collective-permute-done.6), channel_id=1, source_target_pairs={{0,32},{1,49},{2,34},{3,51},{4,36},{5,53},{6,38},{7,55},{8,40},{9,... | collective-permute-start | bytes 5308424 | tf_op jit(solution)/shard_map/ppermute | solution.py:36
  76.0 4.3 %collective-permute-start.11 = (bf16[2,3,144,1024]{3,2,1,0:T(8,128)(2,1)}, bf16[2,3,144,1024]{3,2,1,0:T(8,128)(2,1)}, u32[]{:S(2)}, u32[]{:S(2)}) collective-permute-start(bf16[2,3,144,1024]{3,2,1,0:T(8,128)(2,1)} %collective-permute-done.6), channel_id=1, source_target_pairs={{0,2},{1,15},{2,4},{3,1},{4,6},{5,3},{6,8},{7,5},{8,10},{9,7},{10,... | collective-permute-start | bytes 5308424 | tf_op jit(solution)/shard_map/ppermute | solution.py:36
  80.5 5.2 %place_early_pieces.1 = (bf16[8,1152,1024]{2,1,0:T(8,128)(2,1)S(1)}, bf16[8,144,1024]{2,1,0:T(8,128)(2,1)S(1)}, bf16[8,144,1024]{2,1,0:T(8,128)(2,1)S(1)}) custom-call(s32[6]{0:T(128)S(1)} %stack.53.place, bf16[1152,1024]{1,0:T(8,128)(2,1)S(1)} %pad_maximum_fusion.pack, bf16[4,144,1024]{2,1,0:T(8,128)(2,1)} %bitcast.70, bf16[2,3,144,1024]{3,2,1,0:T(8,128)(2,1)} %copy-done.2, ...), custom_call_target="tpu_custom_call" | custom-call | flops 2415919104 | bytes 18874368 | tf_op jit(solution)/shard_map/place_early_pieces/pallas_call | solution.py:329
  85.7 1.9 collective-permute-start.8
  87.7 2.4 %collective-permute-start.9 = (bf16[8,144,1024]{2,1,0:T(8,128)(2,1)S(1)}, bf16[8,144,1024]{2,1,0:T(8,128)(2,1)S(1)}, u32[]{:S(2)}, u32[]{:S(2)}) collective-permute-start(bf16[8,144,1024]{2,1,0:T(8,128)(2,1)S(1)} %get-tuple-element.36), channel_id=1, source_target_pairs={{0,1},{1,0},{2,3},{3,2},{4,5},{5,4},{6,7},{7,6},{8,9},{9,8},{10,11... | collective-permute-start | bytes 7077896 | tf_op jit(solution)/shard_map/ppermute | solution.py:36
  90.1 7.0 %collective-permute-done.10.turn = bf16[2,3,144,1024]{3,2,1,0:T(8,128)(2,1)} collective-permute-done((bf16[2,3,144,1024]{3,2,1,0:T(8,128)(2,1)}, bf16[2,3,144,1024]{3,2,1,0:T(8,128)(2,1)}, u32[]{:S(2)}, u32[]{:S(2)}) %collective-permute-start.10) | collective-permute-done | bytes 1769504 | tf_op jit(solution)/shard_map/ppermute | solution.py:36
  97.0 3.1 %collective-permute-done.11.two = bf16[2,3,144,1024]{3,2,1,0:T(8,128)(2,1)} collective-permute-done((bf16[2,3,144,1024]{3,2,1,0:T(8,128)(2,1)}, bf16[2,3,144,1024]{3,2,1,0:T(8,128)(2,1)}, u32[]{:S(2)}, u32[]{:S(2)}) %collective-permute-start.11) | collective-permute-done | bytes 1769504 | tf_op jit(solution)/shard_map/ppermute | solution.py:36
  100.1 3.4 %collective-permute-start.12 = (bf16[2,3,144,1024]{3,2,1,0:T(8,128)(2,1)}, bf16[2,3,144,1024]{3,2,1,0:T(8,128)(2,1)S(1)}, u32[]{:S(2)}, u32[]{:S(2)}) collective-permute-start(bf16[2,3,144,1024]{3,2,1,0:T(8,128)(2,1)} %collective-permute-done.10.turn), channel_id=1, source_target_pairs={{0,1},{1,0},{2,3},{3,2},{4,5},{5,4},{6,7},{7,6},{8,9},{9,8},{10,11... | collective-permute-start | bytes 5308424 | tf_op jit(solution)/shard_map/ppermute | solution.py:36
  103.6 3.5 %collective-permute-done.12.turn_other = bf16[2,3,144,1024]{3,2,1,0:T(8,128)(2,1)S(1)} collective-permute-done((bf16[2,3,144,1024]{3,2,1,0:T(8,128)(2,1)}, bf16[2,3,144,1024]{3,2,1,0:T(8,128)(2,1)S(1)}, u32[]{:S(2)}, u32[]{:S(2)}) %collective-permute-start.12) | collective-permute-done | bytes 1769504 | tf_op jit(solution)/shard_map/ppermute | solution.py:36
  107.0 7.8 %forward_first_stage.1 = (bf16[128,1024]{1,0:T(8,128)(2,1)S(1)}, f32[8,128,1024]{2,1,0:T(8,128)S(1)}, f32[8,128,128]{2,1,0:T(8,128)S(1)}, bf16[8,1152,1024]{2,1,0:T(8,128)(2,1)S(1)}) custom-call(s32[6]{0:T(128)S(1)} %stack.53.place, bf16[16,64,128]{2,1,0:T(8,128)(2,1)S(1)} %all_to_all.24.arrived, ...), custom_call_target="tpu_custom_call", output_to_operand_aliasing={{3}: (7, {})} | custom-call | flops 2415919104 | bytes 18874368 | tf_op jit(solution)/shard_map/forward_first_stage/pallas_call | solution.py:349
  114.9 6.2 %collective-permute-start.13 = (bf16[128,1024]{1,0:T(8,128)(2,1)S(1)}, bf16[128,1024]{1,0:T(8,128)(2,1)S(1)}, u32[]{:S(2)}, u32[]{:S(2)}) collective-permute-start(bf16[128,1024]{1,0:T(8,128)(2,1)S(1)} %get-tuple-element.40), channel_id=1, source_target_pairs={{0,384},{1,385},{2,386},{3,387},{4,388},{5,389},{6,390},{7,391},{8... | collective-permute-start | bytes 786440 | tf_op jit(solution)/shard_map/ppermute | solution.py:36
  121.0 6.4 %collective-permute-start.15 = (bf16[2,16,4096]{2,1,0:T(8,128)(2,1)S(1)}, bf16[2,16,4096]{2,1,0:T(8,128)(2,1)S(1)}, u32[]{:S(2)}, u32[]{:S(2)}) collective-permute-start(bf16[2,16,4096]{2,1,0:T(8,128)(2,1)S(1)} %pad_maximum_fusion.5), channel_id=1, source_target_pairs={{0,16},{1,17},{2,18},{3,19},{4,20},{5,21},{6,22},{7,23},{8,24},{9,... | collective-permute-start | bytes 786440 | tf_op jit(solution)/shard_map/ppermute | solution.py:36
  127.4 4.5 %collective-permute-done.13.hidden = bf16[128,1024]{1,0:T(8,128)(2,1)S(1)} collective-permute-done((bf16[128,1024]{1,0:T(8,128)(2,1)S(1)}, bf16[128,1024]{1,0:T(8,128)(2,1)S(1)}, u32[]{:S(2)}, u32[]{:S(2)}) %collective-permute-start.13) | collective-permute-done | bytes 262176 | tf_op jit(solution)/shard_map/ppermute | solution.py:36
  133.9 21.4 %collective-permute-done.14.upstream = bf16[128,1024]{1,0:T(8,128)(2,1)S(1)} collective-permute-done((bf16[128,1024]{1,0:T(8,128)(2,1)S(1)}, bf16[128,1024]{1,0:T(8,128)(2,1)S(1)}, u32[]{:S(2)}, u32[]{:S(2)}) %collective-permute-start.14) | collective-permute-done | bytes 262176 | tf_op jit(solution)/shard_map/ppermute | solution.py:36
  155.3 10.0 %backward_first_stage.1 = bf16[8,32,128]{2,1,0:T(8,128)(2,1)} custom-call(s32[6]{0:T(128)S(1)} %stack.53.place, bf16[128,1024]{1,0:T(8,128)(2,1)S(1)} %collective-permute-done.14.upstream, f32[8,128,1024]{2,1,0:T(8,128)S(1)} %get-tuple-element.47.slope_in, f32[8,128,128]{2,1,0:T(8,128)S(1)} %get-tuple-element.48.left, ...), custom_call_target="tpu_custom_call" | custom-call | flops 2415919104 | bytes 18874368 | tf_op jit(solution)/shard_map/backward_first_stage/pallas_call | solution.py:379
  165.3 4.5 %all-to-all-start.1 = ((bf16[8,32,128]{2,1,0:T(8,128)(2,1)}), bf16[8,32,128]{2,1,0:T(8,128)(2,1)S(1)}, u32[]{:S(2)}, u32[]{:S(2)}) async-start(bf16[8,32,128]{2,1,0:T(8,128)(2,1)} %backward_first_stage.1), calls=%async_computation.1 | async-start | bytes 131072 | tf_op jit(solution)/shard_map/all_to_all | solution.py:397
  169.8 5.8 %all-to-all-done.1 = bf16[8,32,128]{2,1,0:T(8,128)(2,1)S(1)} async-done(((bf16[8,32,128]{2,1,0:T(8,128)(2,1)}), bf16[8,32,128]{2,1,0:T(8,128)(2,1)S(1)}, u32[]{:S(2)}, u32[]{:S(2)}) %all-to-all-start.1) | async-done | bytes 65568 | tf_op jit(solution)/shard_map/all_to_all | solution.py:397
  176.2 5.7 %all-to-all-start.2 = ((bf16[8,2,32,128]{3,2,1,0:T(8,128)(2,1)}), bf16[8,2,32,128]{3,2,1,0:T(8,128)(2,1)S(1)}, u32[]{:S(2)}, u32[]{:S(2)}) async-start(bf16[8,2,32,128]{3,2,1,0:T(8,128)(2,1)} %broadcast_in_dim.10), calls=%async_computation.2 | async-start | bytes 262144 | tf_op jit(solution)/shard_map/all_to_all | solution.py:402
  181.9 7.9 %all-to-all-done.2 = bf16[8,2,32,128]{3,2,1,0:T(8,128)(2,1)S(1)} async-done(((bf16[8,2,32,128]{3,2,1,0:T(8,128)(2,1)}), bf16[8,2,32,128]{3,2,1,0:T(8,128)(2,1)S(1)}, u32[]{:S(2)}, u32[]{:S(2)}) %all-to-all-start.2) | async-done | bytes 131104 | tf_op jit(solution)/shard_map/all_to_all | solution.py:402
  191.2 17.3 %all_to_all.25 = f32[64,1,32]{2,1,0:T(1,128)S(1)} all-to-all(f32[64,1,32]{2,1,0:T(1,128)S(1)} %bitcast.67), channel_id=1, replica_groups={{0,1,16,17,32,33,48,49,64,65,80,81,96,97,112,113,128,129,144,145,160,16..., dimensions={0} | all-to-all | bytes 16384 | tf_op jit(solution)/shard_map/all_to_all | solution.py:426
  (53 shorter events, 10.1 us)
Async XLA Ops:
  0.0 18.1 %copy-start = (bf16[2,512,64]{1,2,0:T(8,128)(2,1)S(1)}, bf16[2,512,64]{1,2,0:T(8,128)(2,1)}, u32[]{:S(2)}) copy-start(bf16[2,512,64]{1,2,0:T(8,128)(2,1)} %param.7) | copy-start | bytes 393220
  2.0 16.1 %copy-start.3 = (bf16[2,512,64]{1,2,0:T(8,128)(2,1)S(1)}, bf16[2,512,64]{1,2,0:T(8,128)(2,1)}, u32[]{:S(2)}) copy-start(bf16[2,512,64]{1,2,0:T(8,128)(2,1)} %param.6) | copy-start | bytes 393220
  2.0 16.2 %collective-permute-start = (bf16[144,1024]{1,0:T(8,128)(2,1)S(1)}, bf16[144,1024]{1,0:T(8,128)(2,1)S(1)}, u32[]{:S(2)}, u32[]{:S(2)}) collective-permute-start(bf16[144,1024]{1,0:T(8,128)(2,1)S(1)} %constant_dynamic-slice_fusion.1), channel_id=1, source_target_pairs={{0,64},{1,65},{2,66},{3,67},{4,68},{5,69},{6,70},{7,71},{8,72},{9,... | collective-permute-start | bytes 884744 | tf_op jit(solution)/shard_map/ppermute | solution.py:36
  6.2 21.6 %collective-permute-start.1 = (bf16[144,1024]{1,0:T(8,128)(2,1)S(1)}, bf16[144,1024]{1,0:T(8,128)(2,1)S(1)}, u32[]{:S(2)}, u32[]{:S(2)}) collective-permute-start(bf16[144,1024]{1,0:T(8,128)(2,1)S(1)} %constant_dynamic-slice_fusion.1), channel_id=1, source_target_pairs={{0,128},{1,129},{2,130},{3,131},{4,132},{5,133},{6,134},{7,135},{8... | collective-permute-start | bytes 884744 | tf_op jit(solution)/shard_map/ppermute | solution.py:36
  10.4 19.4 %collective-permute-start.2 = (bf16[144,1024]{1,0:T(8,128)(2,1)S(1)}, bf16[144,1024]{1,0:T(8,128)(2,1)}, u32[]{:S(2)}, u32[]{:S(2)}) collective-permute-start(bf16[144,1024]{1,0:T(8,128)(2,1)S(1)} %constant_dynamic-slice_fusion.1), channel_id=1, source_target_pairs={{0,192},{1,193},{2,194},{3,195},{4,196},{5,197},{6,198},{7,199},{8... | collective-permute-start | bytes 884744 | tf_op jit(solution)/shard_map/ppermute | solution.py:36
  13.5 20.7 %copy-start.4 = (bf16[1,16,4096]{2,1,0:T(8,128)(2,1)S(1)}, bf16[1,16,4096]{2,1,0:T(8,128)(2,1)}, u32[]{:S(2)}) copy-start(bf16[1,16,4096]{2,1,0:T(8,128)(2,1)} %param.11) | copy-start | bytes 393220
  13.5 24.2 %collective-permute-start.4 = (bf16[576,1024]{1,0:T(8,128)(2,1)S(1)}, bf16[576,1024]{1,0:T(8,128)(2,1)S(1)}, u32[]{:S(2)}, u32[]{:S(2)}) collective-permute-start(bf16[576,1024]{1,0:T(8,128)(2,1)S(1)} %constant_dynamic-slice_fusion), channel_id=1, source_target_pairs={{0,32},{1,49},{2,34},{3,51},{4,36},{5,53},{6,38},{7,55},{8,40},{9,... | collective-permute-start | bytes 3538952 | tf_op jit(solution)/shard_map/ppermute | solution.py:36
  30.9 6.6 %collective-permute-start.3 = (bf16[3,144,1024]{2,1,0:T(8,128)(2,1)S(1)}, bf16[3,144,1024]{2,1,0:T(8,128)(2,1)S(1)}, u32[]{:S(2)}, u32[]{:S(2)}) collective-permute-start(bf16[3,144,1024]{2,1,0:T(8,128)(2,1)S(1)} %get-tuple-element.52), channel_id=1, source_target_pairs={{0,1},{1,0},{2,3},{3,2},{4,5},{5,4},{6,7},{7,6},{8,9},{9,8},{10,11... | collective-permute-start | bytes 2654216 | tf_op jit(solution)/shard_map/ppermute | solution.py:36
  34.3 3.2 %collective-permute-start.5 = (bf16[1,16,4096]{2,1,0:T(8,128)(2,1)S(1)}, bf16[1,16,4096]{2,1,0:T(8,128)(2,1)S(1)}, u32[]{:S(2)}, u32[]{:S(2)}) collective-permute-start(bf16[1,16,4096]{2,1,0:T(8,128)(2,1)S(1)} %copy-done.4), channel_id=1, source_target_pairs={{0,1},{1,0},{2,3},{3,2},{4,5},{5,4},{6,7},{7,6},{8,9},{9,8},{10,11... | collective-permute-start | bytes 393224 | tf_op jit(solution)/shard_map/ppermute | solution.py:36
  37.7 8.5 %copy-start.2 = (bf16[2,3,144,1024]{3,2,1,0:T(8,128)(2,1)}, bf16[2,3,144,1024]{3,2,1,0:T(8,128)(2,1)S(1)}, u32[]{:S(2)}) copy-start(bf16[2,3,144,1024]{3,2,1,0:T(8,128)(2,1)S(1)} %pad_maximum_fusion.1.own) | copy-start | bytes 5308420
  37.7 38.3 %copy-start.6 = (bf16[576,1024]{1,0:T(8,128)(2,1)}, bf16[576,1024]{1,0:T(8,128)(2,1)S(1)}, u32[]{:S(2)}) copy-start(bf16[576,1024]{1,0:T(8,128)(2,1)S(1)} %collective-permute-done.4) | copy-start | bytes 3538948
  37.7 32.9 %collective-permute-start.6 = (bf16[2,3,144,1024]{3,2,1,0:T(8,128)(2,1)S(1)}, bf16[2,3,144,1024]{3,2,1,0:T(8,128)(2,1)}, u32[]{:S(2)}, u32[]{:S(2)}) collective-permute-start(bf16[2,3,144,1024]{3,2,1,0:T(8,128)(2,1)S(1)} %pad_maximum_fusion.1.own), channel_id=1, source_target_pairs={{0,2},{1,15},{2,4},{3,1},{4,6},{5,3},{6,8},{7,5},{8,10},{9,7},{10,... | collective-permute-start | bytes 5308424 | tf_op jit(solution)/shard_map/ppermute | solution.py:36
  46.2 24.5 %collective-permute-start.7 = (bf16[2,3,144,1024]{3,2,1,0:T(8,128)(2,1)S(1)}, bf16[2,3,144,1024]{3,2,1,0:T(8,128)(2,1)S(1)}, u32[]{:S(2)}, u32[]{:S(2)}) collective-permute-start(bf16[2,3,144,1024]{3,2,1,0:T(8,128)(2,1)S(1)} %pad_maximum_fusion.1.own), channel_id=1, source_target_pairs={{0,32},{1,49},{2,34},{3,51},{4,36},{5,53},{6,38},{7,55},{8,40},{9,... | collective-permute-start | bytes 5308424 | tf_op jit(solution)/shard_map/ppermute | solution.py:36
  70.7 1.3 copy-start.5
  72.0 25.1 %collective-permute-start.10 = (bf16[2,3,144,1024]{3,2,1,0:T(8,128)(2,1)}, bf16[2,3,144,1024]{3,2,1,0:T(8,128)(2,1)}, u32[]{:S(2)}, u32[]{:S(2)}) collective-permute-start(bf16[2,3,144,1024]{3,2,1,0:T(8,128)(2,1)} %collective-permute-done.6), channel_id=1, source_target_pairs={{0,32},{1,49},{2,34},{3,51},{4,36},{5,53},{6,38},{7,55},{8,40},{9,... | collective-permute-start | bytes 5308424 | tf_op jit(solution)/shard_map/ppermute | solution.py:36
  76.0 24.1 %collective-permute-start.11 = (bf16[2,3,144,1024]{3,2,1,0:T(8,128)(2,1)}, bf16[2,3,144,1024]{3,2,1,0:T(8,128)(2,1)}, u32[]{:S(2)}, u32[]{:S(2)}) collective-permute-start(bf16[2,3,144,1024]{3,2,1,0:T(8,128)(2,1)} %collective-permute-done.6), channel_id=1, source_target_pairs={{0,2},{1,15},{2,4},{3,1},{4,6},{5,3},{6,8},{7,5},{8,10},{9,7},{10,... | collective-permute-start | bytes 5308424 | tf_op jit(solution)/shard_map/ppermute | solution.py:36
  85.7 17.8 %collective-permute-start.8 = (bf16[8,144,1024]{2,1,0:T(8,128)(2,1)S(1)}, bf16[8,144,1024]{2,1,0:T(8,128)(2,1)S(1)}, u32[]{:S(2)}, u32[]{:S(2)}) collective-permute-start(bf16[8,144,1024]{2,1,0:T(8,128)(2,1)S(1)} %get-tuple-element.35), channel_id=1, source_target_pairs={{0,1},{1,0},{2,3},{3,2},{4,5},{5,4},{6,7},{7,6},{8,9},{9,8},{10,11... | collective-permute-start | bytes 7077896 | tf_op jit(solution)/shard_map/ppermute | solution.py:36
  87.7 15.9 %collective-permute-start.9 = (bf16[8,144,1024]{2,1,0:T(8,128)(2,1)S(1)}, bf16[8,144,1024]{2,1,0:T(8,128)(2,1)S(1)}, u32[]{:S(2)}, u32[]{:S(2)}) collective-permute-start(bf16[8,144,1024]{2,1,0:T(8,128)(2,1)S(1)} %get-tuple-element.36), channel_id=1, source_target_pairs={{0,1},{1,0},{2,3},{3,2},{4,5},{5,4},{6,7},{7,6},{8,9},{9,8},{10,11... | collective-permute-start | bytes 7077896 | tf_op jit(solution)/shard_map/ppermute | solution.py:36
  100.1 6.9 %collective-permute-start.12 = (bf16[2,3,144,1024]{3,2,1,0:T(8,128)(2,1)}, bf16[2,3,144,1024]{3,2,1,0:T(8,128)(2,1)S(1)}, u32[]{:S(2)}, u32[]{:S(2)}) collective-permute-start(bf16[2,3,144,1024]{3,2,1,0:T(8,128)(2,1)} %collective-permute-done.10.turn), channel_id=1, source_target_pairs={{0,1},{1,0},{2,3},{3,2},{4,5},{5,4},{6,7},{7,6},{8,9},{9,8},{10,11... | collective-permute-start | bytes 5308424 | tf_op jit(solution)/shard_map/ppermute | solution.py:36
  114.9 17.6 %copy-start.1 = (bf16[8,1152,1024]{2,1,0:T(8,128)(2,1)}, bf16[8,1152,1024]{2,1,0:T(8,128)(2,1)S(1)}, u32[]{:S(2)}) copy-start(bf16[8,1152,1024]{2,1,0:T(8,128)(2,1)S(1)} %get-tuple-element.41.layers.layers_in) | copy-start | bytes 56623108
  114.9 17.1 %collective-permute-start.13 = (bf16[128,1024]{1,0:T(8,128)(2,1)S(1)}, bf16[128,1024]{1,0:T(8,128)(2,1)S(1)}, u32[]{:S(2)}, u32[]{:S(2)}) collective-permute-start(bf16[128,1024]{1,0:T(8,128)(2,1)S(1)} %get-tuple-element.40), channel_id=1, source_target_pairs={{0,384},{1,385},{2,386},{3,387},{4,388},{5,389},{6,390},{7,391},{8... | collective-permute-start | bytes 786440 | tf_op jit(solution)/shard_map/ppermute | solution.py:36
  121.0 12.8 %collective-permute-start.15 = (bf16[2,16,4096]{2,1,0:T(8,128)(2,1)S(1)}, bf16[2,16,4096]{2,1,0:T(8,128)(2,1)S(1)}, u32[]{:S(2)}, u32[]{:S(2)}) collective-permute-start(bf16[2,16,4096]{2,1,0:T(8,128)(2,1)S(1)} %pad_maximum_fusion.5), channel_id=1, source_target_pairs={{0,16},{1,17},{2,18},{3,19},{4,20},{5,21},{6,22},{7,23},{8,24},{9,... | collective-permute-start | bytes 786440 | tf_op jit(solution)/shard_map/ppermute | solution.py:36
  132.5 22.8 %collective-permute-start.14 = (bf16[128,1024]{1,0:T(8,128)(2,1)S(1)}, bf16[128,1024]{1,0:T(8,128)(2,1)S(1)}, u32[]{:S(2)}, u32[]{:S(2)}) collective-permute-start(bf16[128,1024]{1,0:T(8,128)(2,1)S(1)} %get-tuple-element.42), channel_id=1, source_target_pairs={{256,128},{257,129},{258,130},{259,131},{260,132},{261,133},{262,1... | collective-permute-start | bytes 786440 | tf_op jit(solution)/shard_map/ppermute | solution.py:36
  165.3 10.2 %all-to-all-start.1 = ((bf16[8,32,128]{2,1,0:T(8,128)(2,1)}), bf16[8,32,128]{2,1,0:T(8,128)(2,1)S(1)}, u32[]{:S(2)}, u32[]{:S(2)}) async-start(bf16[8,32,128]{2,1,0:T(8,128)(2,1)} %backward_first_stage.1), calls=%async_computation.1 | async-start | bytes 131072 | tf_op jit(solution)/shard_map/all_to_all | solution.py:397
  176.2 13.6 %all-to-all-start.2 = ((bf16[8,2,32,128]{3,2,1,0:T(8,128)(2,1)}), bf16[8,2,32,128]{3,2,1,0:T(8,128)(2,1)S(1)}, u32[]{:S(2)}, u32[]{:S(2)}) async-start(bf16[8,2,32,128]{3,2,1,0:T(8,128)(2,1)} %broadcast_in_dim.10), calls=%async_computation.2 | async-start | bytes 262144 | tf_op jit(solution)/shard_map/all_to_all | solution.py:402
